TPU v7x, 32 devices: a whole 2x2x4 slice. The times are simulated.
32 devices in a mesh: elem: 16 (over z, y, x), face: 2 (over core).
Axes of the slice: x: 2, y: 2, z: 4, core: 2. Of those that a mesh axis runs over, the one named last changes fastest.
Arguments:
- forcing: float32 [8192, 512], P(('elem', 'face')), may hold values from -15 to 15, as said below
- kappa: float32 [8192], P(('elem', 'face')), may hold values from 0.3 to 3
- elem_order: int32 [32, 256], P(('elem', 'face')), may hold values from 0 to 255, each once within a row
Outputs:
- solution: float32 [8192, 512], P(('elem', 'face'))
- residual: float32 [8192, 512], P(('elem', 'face'))
Inputs may be any that keep to these rules, and one draw needn't show every extreme that they name: `forcing`: element loads of order one, with a scale that varies by element and along z. `elem_order`: each row is a permutation of the 256 grid positions of the device's block.
All inputs are finite; a program needn't handle non-finite values.
Results may differ from a plain program's by a relative error of at most 0.0004.
Values sent between devices are 32-bit elements; how exact they have to be, the bound alone decides.
No kernel may reach another device: no remote copies, remote signals or barrier semaphores. Data moves between devices by JAX's collectives and lax.ppermute only.
A program may use at most 192 MiB of HBM per device.

v0:
```python
import jax
import jax.numpy as jnp
import numpy as np
from jax import lax
from jax.sharding import PartitionSpec as P

EX = 8
EY = 32
EZ = 1
SWEEPS = 4
ITERS = 2


REACT = 0.02
OMEGA = 0.6


def padded_2(x, sides, width):
    for axis, dim in sides:
        size, length = (lax.axis_size(axis), x.shape[dim])
        up = [(i, (i + 1) % size) for i in range(size)]
        down = [(j, i) for i, j in up]
        last = lax.slice_in_dim(x, length - width, length, axis=dim)
        initial = lax.slice_in_dim(x, 0, width, axis=dim)
        before = lax.ppermute(last, axis, up)
        after = lax.ppermute(initial, axis, down)
        x = jnp.concatenate([before, x, after], axis=dim)
    return x


def from_behind(x, axis, by):
    size = lax.axis_size(axis)
    return lax.ppermute(x, axis, [(i, (i + by) % size) for i in range(size)])


def legendre_seven(points):
    before = np.ones(8)
    current = np.array(points)
    for degree in range(1, 7):
        following = ((2 * degree + 1) * points * current - degree * before) / (degree + 1)
        before = current
        current = following
    return current


def element_tables():
    points = np.array(
        [
            -1.0,
            -0.8717401485096066,
            -0.5917001814331423,
            -0.2092992179024789,
            0.2092992179024789,
            0.5917001814331423,
            0.8717401485096066,
            1.0,
        ]
    )
    weights = np.array(
        [
            1.0 / 28.0,
            0.2107042271435061,
            0.3411226924835044,
            0.4124587946587038,
            0.4124587946587038,
            0.3411226924835044,
            0.2107042271435061,
            1.0 / 28.0,
        ]
    )
    legendre = legendre_seven(points)
    derivative = np.zeros((8, 8))
    for left_node in range(8):
        for right_node in range(8):
            if left_node != right_node:
                derivative[left_node, right_node] = legendre[left_node] / (
                    legendre[right_node] * (points[left_node] - points[right_node])
                )
    derivative[0, 0] = -14.0
    derivative[7, 7] = 14.0
    stiffness = derivative.T @ (weights[:, None] * derivative)
    mass = np.eye(8) * weights[None, :]
    full_stiff = (
        np.kron(np.kron(mass, mass), stiffness)
        + np.kron(np.kron(mass, stiffness), mass)
        + np.kron(np.kron(stiffness, mass), mass)
    )
    mass_nodes = np.kron(np.kron(weights, weights), weights)
    interp = np.stack([(1.0 - points) / 2.0, (1.0 + points) / 2.0], 1)
    prolong = np.kron(np.kron(interp, interp), interp)
    coarse_stiff = prolong.T @ full_stiff @ prolong
    coarse_mass = prolong.T @ (mass_nodes[:, None] * prolong)
    ends = np.ones(8)
    ends[0] = 2.0
    ends[7] = 2.0
    inverse_mult = 1.0 / np.kron(np.kron(ends, ends), ends)
    return (
        stiffness,
        weights,
        full_stiff,
        mass_nodes,
        prolong,
        coarse_stiff,
        coarse_mass,
        inverse_mult,
    )


def pair_sum(grid, elem_axis, node_axis):
    upper = lax.index_in_dim(grid, 7, node_axis, keepdims=True)
    lower = lax.index_in_dim(grid, 0, node_axis, keepdims=True)
    shared = upper + jnp.roll(lower, -1, elem_axis)
    middle = lax.slice_in_dim(grid, 1, 7, axis=node_axis)
    return jnp.concatenate([jnp.roll(shared, 1, elem_axis), middle, shared], node_axis)


def direct_sum(field):
    grid = field.reshape(EZ, EY, EX, 8, 8, 8)
    grid = pair_sum(grid, 2, 5)
    grid = pair_sum(grid, 1, 4)
    upper = grid[:, :, :, 7]
    lower = grid[:, :, :, 0]
    rims = jnp.stack([lower[0], upper[-1]]).reshape(2, EY, EX * 64)
    padded = padded_2(rims, ((("elem", "face"), 0),), 1)
    below = padded[0].reshape(1, EY, EX, 8, 8)
    above = padded[3].reshape(1, EY, EX, 8, 8)
    shared = upper + jnp.concatenate([lower[1:], above], 0)
    first = jnp.concatenate([below, upper[:-1]], 0) + lower
    grid = jnp.concatenate([first[:, :, :, None], grid[:, :, :, 1:7], shared[:, :, :, None]], 3)
    return grid.reshape(-1, 512)


def vertex_corners(extended):
    planes = extended.shape[0] - 1
    parts = []
    for corner in range(8):
        along_z, along_y, along_x = (corner // 4, corner // 2 % 2, corner % 2)
        moved = jnp.roll(extended, (-along_y, -along_x), (1, 2))
        parts.append(moved[along_z : along_z + planes])
    return jnp.stack(parts, -1)


def with_next(vert):
    upper_plane = from_behind(vert[0], ("elem", "face"), -1)
    return jnp.concatenate([vert, upper_plane[None]], 0)


def raw_total(contrib):
    planes = contrib.shape[0]
    total = jnp.zeros((planes + 1,) + contrib.shape[1:3], jnp.float32)
    for corner in range(8):
        along_z, along_y, along_x = (corner // 4, corner // 2 % 2, corner % 2)
        moved = jnp.roll(contrib[..., corner], (along_y, along_x), (1, 2))
        total = total.at[along_z : along_z + planes].add(moved)
    return total


def local_assemble(contrib):
    planes = contrib.shape[0]
    total = raw_total(contrib)
    received = from_behind(total[planes], ("elem", "face"), 1)
    return total[:planes].at[0].add(received)


def per_device(forcing, kappa, elem_order):
    tabs = [jnp.asarray(table, jnp.float32) for table in element_tables()]
    stiffness, weights, full_stiff, mass_nodes = (tabs[0], tabs[1], tabs[2], tabs[3])
    prolong, coarse_stiff, coarse_mass, inverse_mult = (tabs[4], tabs[5], tabs[6], tabs[7])
    highest = lax.Precision.HIGHEST
    order = elem_order[0]
    count = order.shape[0]
    inverse = jnp.zeros((count,), jnp.int32).at[order].set(jnp.arange(count, dtype=jnp.int32))
    load = forcing[inverse]
    coeff = kappa[inverse]
    coeff_grid = coeff.reshape(EZ, EY, EX)
    corner_stiff = jnp.diag(coarse_stiff)
    corner_mass = jnp.diag(coarse_mass)
    diag_fine = direct_sum(
        coeff[:, None] * jnp.diag(full_stiff)[None, :] + REACT * mass_nodes[None, :]
    )
    coarse_diag = local_assemble(coeff_grid[..., None] * corner_stiff + REACT * corner_mass)

    def precondition(resid):
        restricted = jnp.dot(resid * inverse_mult[None, :], prolong, precision=highest).reshape(
            EZ, EY, EX, 8
        )
        target = local_assemble(restricted)
        vert = jnp.zeros_like(target)
        for sweep in range(SWEEPS):
            values = vertex_corners(with_next(vert)).reshape(-1, 8)
            contrib = coeff[:, None] * jnp.dot(
                values, coarse_stiff, precision=highest
            ) + REACT * jnp.dot(values, coarse_mass, precision=highest)
            vert = (
                vert
                + OMEGA * (target - local_assemble(contrib.reshape(EZ, EY, EX, 8))) / coarse_diag
            )
        extended = with_next(vert)
        values = vertex_corners(extended).reshape(-1, 8)
        return resid / diag_fine + jnp.dot(values, prolong.T, precision=highest)

    def inner(left, right):
        return jnp.sum(left * right * inverse_mult[None, :])

    def progress(resid, precond):
        return lax.psum(inner(resid, precond), ("elem", "face"))

    resid = direct_sum(load)
    solution = jnp.zeros_like(resid)
    precond = precondition(resid)
    direction = precond
    gamma = progress(resid, precond)
    for step in range(ITERS):
        cube = direction.reshape(-1, 8, 8, 8)
        term_x = jnp.einsum("xa,ecba->ecbx", stiffness, cube, precision=highest) * (
            weights[:, None, None] * weights[None, :, None]
        )
        term_y = jnp.einsum("yb,ecba->ecya", stiffness, cube, precision=highest) * (
            weights[:, None, None] * weights[None, None, :]
        )
        term_z = jnp.einsum("zc,ecba->ezba", stiffness, cube, precision=highest) * (
            weights[None, :, None] * weights[None, None, :]
        )
        local = (
            coeff[:, None] * (term_x + term_y + term_z).reshape(-1, 512)
            + REACT * mass_nodes[None, :] * direction
        )
        image = direct_sum(local)
        alpha = gamma / lax.psum(inner(direction, image), ("elem", "face"))
        solution = solution + alpha * direction
        resid = resid - alpha * image
        if step + 1 < ITERS:
            precond = precondition(resid)
            gamma_new = progress(resid, precond)
            direction = precond + gamma_new / gamma * direction
            gamma = gamma_new
    return (solution[order], resid[order])


def solution(mesh):
    in_specs = (P(("elem", "face"), None), P(("elem", "face")), P(("elem", "face"), None))
    out_specs = (P(("elem", "face"), None), P(("elem", "face"), None))
    return jax.shard_map(
        per_device, mesh=mesh, in_specs=in_specs, out_specs=out_specs, check_vma=False
    )
```

profile of v0, /device:TPU:0, one launch (start us, length us, event | category | flops | bytes accessed | tf_op | source)
XLA Modules:
  0.0 516.7 jit_solution(2784594638996156022)
XLA Ops:
  0.7 6.4 %collective-permute-start.5 = (f32[32,8]{0,1:T(8,128)S(1)}, f32[32,8]{0,1:T(8,128)S(1)}, u32[]{:S(2)}, u32[]{:S(2)}) collective-permute-start(f32[32,8]{0,1:T(8,128)S(1)} %broadcast.1378), channel_id=1, source_target_pairs={{0,31},{1,0},{2,1},{3,2},{4,3},{5,4},{6,5},{7,6},{8,7},{9,8},{10,9... | collective-permute-start | bytes 3080 | tf_op jit(solution)/shard_map/ppermute | solution.py:33
  10.2 6.2 %reshape.3978 = f32[1,32,8,8,8,8]{5,4,3,2,1,0:T(8,128)} reshape(f32[256,512]{1,0:T(8,128)S(1)} %gather_fusion) | data formatting | bytes 1048576 | tf_op jit(solution)/shard_map/reshape | solution.py:118
  16.4 9.1 %slice.4087 = f32[1,32,8,8,8,1]{5,4,3,2,1,0:T(8,128)} slice(f32[1,32,8,8,8,8]{5,4,3,2,1,0:T(8,128)} %reshape.3978), slice={[0:1], [0:32], [0:8], [0:8], [0:8], [7:8]} | slice | bytes 131072 | tf_op jit(solution)/shard_map/slice | solution.py:110
  25.6 3.7 slice.4088
  29.3 5.6 %slice.4092 = f32[1,32,8,8,8,6]{5,4,3,2,1,0:T(8,128)} slice(f32[1,32,8,8,8,8]{5,4,3,2,1,0:T(8,128)S(1)} %copy-done.3), slice={[0:1], [0:32], [0:8], [0:8], [0:8], [1:7]} | slice | bytes 786432 | tf_op jit(solution)/shard_map/slice | solution.py:113
  34.9 6.4 %copy.1039 = f32[1,32,8,8,8,1]{1,4,5,3,2,0:T(8,128)S(1)} copy(f32[1,32,8,8,8,1]{5,4,3,2,1,0:T(8,128)} %slice.4087) | data formatting | bytes 131072
  41.9 5.5 %copy.1040 = f32[1,32,7,8,8,1]{1,4,5,3,2,0:T(8,128)S(1)} copy(f32[1,32,7,8,8,1]{5,4,3,2,1,0:T(8,128)} %slice.4088) | data formatting | bytes 114688
  47.4 6.7 %copy.823 = f32[1,32,8,8,8,6]{1,5,4,3,2,0:T(8,128)S(1)} copy(f32[1,32,8,8,8,6]{5,4,3,2,1,0:T(8,128)} %slice.4092) | data formatting | bytes 786432 | tf_op jit(solution)/shard_map/slice | solution.py:113
  57.6 5.5 %collective-permute-start.1 = (f32[1,32,512]{1,2,0:T(8,128)S(1)}, f32[1,32,512]{1,2,0:T(8,128)S(1)}, u32[]{:S(2)}, u32[]{:S(2)}) collective-permute-start(f32[1,32,512]{1,2,0:T(8,128)S(1)} %bitcast.616), channel_id=1, source_target_pairs={{1,0},{2,1},{3,2},{4,3},{5,4},{6,5},{7,6},{8,7},{9,8},{10,9},{11,1... | collective-permute-start | bytes 196616 | tf_op jit(solution)/shard_map/ppermute | solution.py:26
  67.6 4.5 gather_fusion.2
  88.9 5.9 %collective-permute-done.4 = f32[32,8]{0,1:T(8,128)S(1)} collective-permute-done((f32[32,8]{0,1:T(8,128)S(1)}, f32[32,8]{0,1:T(8,128)S(1)}, u32[]{:S(2)}, u32[]{:S(2)}) %collective-permute-start.4) | collective-permute-done | bytes 1056 | tf_op jit(solution)/shard_map/ppermute | solution.py:33
  97.9 4.8 collective-permute-start.3
  106.3 6.1 %collective-permute-done.9 = f32[32,8]{0,1:T(8,128)S(1)} collective-permute-done((f32[32,8]{0,1:T(8,128)S(1)}, f32[32,8]{0,1:T(8,128)S(1)}, u32[]{:S(2)}, u32[]{:S(2)}) %collective-permute-start.9) | collective-permute-done | bytes 1056 | tf_op jit(solution)/shard_map/ppermute | solution.py:33
  120.0 5.6 %collective-permute-done.11 = f32[32,8]{0,1:T(8,128)S(1)} collective-permute-done((f32[32,8]{0,1:T(8,128)S(1)}, f32[32,8]{0,1:T(8,128)S(1)}, u32[]{:S(2)}, u32[]{:S(2)}) %collective-permute-start.11) | collective-permute-done | bytes 1056 | tf_op jit(solution)/shard_map/ppermute | solution.py:33
  130.8 5.7 %collective-permute-done.13 = f32[32,8]{0,1:T(8,128)S(1)} collective-permute-done((f32[32,8]{0,1:T(8,128)S(1)}, f32[32,8]{0,1:T(8,128)S(1)}, u32[]{:S(2)}, u32[]{:S(2)}) %collective-permute-start.13) | collective-permute-done | bytes 1056 | tf_op jit(solution)/shard_map/ppermute | solution.py:33
  139.8 7.3 %copy.829 = f32[1,32,8,8,8,8]{5,4,3,2,1,0:T(8,128)} copy(f32[1,32,8,8,8,8]{1,5,4,3,2,0:T(8,128)S(1)} %pad_maximum_fusion) | data formatting | bytes 1048576 | tf_op jit(solution)/shard_map/concatenate | solution.py:129
  147.1 6.9 %reshape.3979 = f32[256,512]{1,0:T(8,128)S(1)} reshape(f32[1,32,8,8,8,8]{5,4,3,2,1,0:T(8,128)} %copy.829) | data formatting | bytes 1048576 | tf_op jit(solution)/shard_map/reshape | solution.py:130
  154.0 8.2 %copy.831 = f32[1,32,8,8,8,8]{5,4,3,2,1,0:T(8,128)} copy(f32[1,32,8,8,8,8]{1,5,4,2,3,0:T(8,128)} %pad_maximum_fusion.1) | data formatting | bytes 1048576 | tf_op jit(solution)/shard_map/concatenate | solution.py:129
  162.3 7.6 %reshape.3980 = f32[256,512]{1,0:T(8,128)} reshape(f32[1,32,8,8,8,8]{5,4,3,2,1,0:T(8,128)} %copy.831) | data formatting | bytes 1048576 | tf_op jit(solution)/shard_map/reshape | solution.py:130
  183.5 7.5 %reshape.3988 = f32[1,32,8,8,8,8]{5,4,3,2,1,0:T(8,128)} reshape(f32[256,512]{1,0:T(8,128)} %multiply_add_fusion.18) | data formatting | bytes 1048576 | tf_op jit(solution)/shard_map/reshape | solution.py:118
  191.0 9.1 %slice.4267 = f32[1,32,8,8,8,1]{5,4,3,2,1,0:T(8,128)} slice(f32[1,32,8,8,8,8]{5,4,3,2,1,0:T(8,128)} %reshape.3988), slice={[0:1], [0:32], [0:8], [0:8], [0:8], [7:8]} | slice | bytes 131072 | tf_op jit(solution)/shard_map/slice | solution.py:110
  201.3 3.7 slice.4268
  204.9 5.6 %slice.4272 = f32[1,32,8,8,8,6]{5,4,3,2,1,0:T(8,128)} slice(f32[1,32,8,8,8,8]{5,4,3,2,1,0:T(8,128)S(1)} %copy-done.4), slice={[0:1], [0:32], [0:8], [0:8], [0:8], [1:7]} | slice | bytes 786432 | tf_op jit(solution)/shard_map/slice | solution.py:113
  210.5 7.0 %copy.1053 = f32[1,32,8,8,8,1]{1,4,5,3,2,0:T(8,128)} copy(f32[1,32,8,8,8,1]{5,4,3,2,1,0:T(8,128)} %slice.4267) | data formatting | bytes 131072
  219.3 6.1 %copy.1054 = f32[1,32,7,8,8,1]{1,4,5,3,2,0:T(8,128)} copy(f32[1,32,7,8,8,1]{5,4,3,2,1,0:T(8,128)} %slice.4268) | data formatting | bytes 114688
  227.1 7.4 %copy.938 = f32[1,32,8,8,8,6]{1,5,4,3,2,0:T(8,128)} copy(f32[1,32,8,8,8,6]{5,4,3,2,1,0:T(8,128)} %slice.4272) | data formatting | bytes 786432 | tf_op jit(solution)/shard_map/slice | solution.py:113
  238.7 4.8 collective-permute-start.16
  243.7 3.9 collective-permute-done.15
  249.9 8.3 %copy.944 = f32[1,32,8,8,8,8]{5,4,3,2,1,0:T(8,128)} copy(f32[1,32,8,8,8,8]{1,5,4,3,2,0:T(8,128)} %pad_maximum_fusion.2) | data formatting | bytes 1048576 | tf_op jit(solution)/shard_map/concatenate | solution.py:129
  258.2 7.6 %reshape.3989 = f32[256,512]{1,0:T(8,128)} reshape(f32[1,32,8,8,8,8]{5,4,3,2,1,0:T(8,128)} %copy.944) | data formatting | bytes 1048576 | tf_op jit(solution)/shard_map/reshape | solution.py:130
  267.7 38.4 %all-reduce.1 = (f32[]{:T(128)}, f32[]{:T(128)}) all-reduce(f32[]{:T(128)} %get-tuple-element.1155, f32[]{:T(128)} %get-tuple-element.1154), channel_id=1, replica_groups=mesh['elem'=16,'face'=2] {'elem','face'}, use_global_device_ids=true, to_apply=%region_2.3 | all-reduce | flops 2 | bytes 16 | tf_op jit(solution)/shard_map/psum | solution.py:206
  311.2 6.6 %collective-permute-done.17 = f32[32,8]{0,1:T(8,128)S(1)} collective-permute-done((f32[32,8]{0,1:T(8,128)S(1)}, f32[32,8]{0,1:T(8,128)S(1)}, u32[]{:S(2)}, u32[]{:S(2)}) %collective-permute-start.17) | collective-permute-done | bytes 1056 | tf_op jit(solution)/shard_map/ppermute | solution.py:33
  322.6 6.1 %collective-permute-done.19 = f32[32,8]{0,1:T(8,128)S(1)} collective-permute-done((f32[32,8]{0,1:T(8,128)S(1)}, f32[32,8]{0,1:T(8,128)S(1)}, u32[]{:S(2)}, u32[]{:S(2)}) %collective-permute-start.19) | collective-permute-done | bytes 1056 | tf_op jit(solution)/shard_map/ppermute | solution.py:33
  333.5 6.1 %collective-permute-done.21 = f32[32,8]{0,1:T(8,128)S(1)} collective-permute-done((f32[32,8]{0,1:T(8,128)S(1)}, f32[32,8]{0,1:T(8,128)S(1)}, u32[]{:S(2)}, u32[]{:S(2)}) %collective-permute-start.21) | collective-permute-done | bytes 1056 | tf_op jit(solution)/shard_map/ppermute | solution.py:33
  344.3 6.1 %collective-permute-done.23 = f32[32,8]{0,1:T(8,128)S(1)} collective-permute-done((f32[32,8]{0,1:T(8,128)S(1)}, f32[32,8]{0,1:T(8,128)S(1)}, u32[]{:S(2)}, u32[]{:S(2)}) %collective-permute-start.23) | collective-permute-done | bytes 1056 | tf_op jit(solution)/shard_map/ppermute | solution.py:33
  355.3 38.5 %psum.30 = f32[]{:T(128)} all-reduce(f32[]{:T(128)} %get-tuple-element.1158), channel_id=1, replica_groups=mesh['elem'=16,'face'=2] {'elem','face'}, use_global_device_ids=true, to_apply=%region_6.7 | all-reduce | flops 1 | bytes 8 | tf_op jit(solution)/shard_map/psum | solution.py:206
  398.2 6.2 %reshape.3995 = f32[1,32,8,8,8,8]{5,4,3,2,1,0:T(8,128)} reshape(f32[256,512]{1,0:T(8,128)S(1)} %multiply_add_fusion.16) | data formatting | bytes 1048576 | tf_op jit(solution)/shard_map/reshape | solution.py:118
  404.4 9.1 %slice.4398 = f32[1,32,8,8,8,1]{5,4,3,2,1,0:T(8,128)} slice(f32[1,32,8,8,8,8]{5,4,3,2,1,0:T(8,128)} %reshape.3995), slice={[0:1], [0:32], [0:8], [0:8], [0:8], [7:8]} | slice | bytes 131072 | tf_op jit(solution)/shard_map/slice | solution.py:110
  413.7 3.7 slice.4399
  417.3 5.6 %slice.4403 = f32[1,32,8,8,8,6]{5,4,3,2,1,0:T(8,128)} slice(f32[1,32,8,8,8,8]{5,4,3,2,1,0:T(8,128)S(1)} %copy-done.5), slice={[0:1], [0:32], [0:8], [0:8], [0:8], [1:7]} | slice | bytes 786432 | tf_op jit(solution)/shard_map/slice | solution.py:113
  422.9 6.4 %copy.1064 = f32[1,32,8,8,8,1]{1,4,5,3,2,0:T(8,128)S(1)} copy(f32[1,32,8,8,8,1]{5,4,3,2,1,0:T(8,128)} %slice.4398) | data formatting | bytes 131072
  429.9 5.7 %copy.1065 = f32[1,32,7,8,8,1]{1,4,5,3,2,0:T(8,128)S(1)} copy(f32[1,32,7,8,8,1]{5,4,3,2,1,0:T(8,128)} %slice.4399) | data formatting | bytes 114688
  436.3 6.7 %copy.1029 = f32[1,32,8,8,8,6]{1,5,4,3,2,0:T(8,128)S(1)} copy(f32[1,32,8,8,8,6]{5,4,3,2,1,0:T(8,128)} %slice.4403) | data formatting | bytes 786432 | tf_op jit(solution)/shard_map/slice | solution.py:113
  445.5 5.3 %collective-permute-start.26 = (f32[1,32,512]{1,2,0:T(8,128)S(1)}, f32[1,32,512]{1,2,0:T(8,128)S(1)}, u32[]{:S(2)}, u32[]{:S(2)}) collective-permute-start(f32[1,32,512]{1,2,0:T(8,128)S(1)} %bitcast.622), channel_id=1, source_target_pairs={{1,0},{2,1},{3,2},{4,3},{5,4},{6,5},{7,6},{8,7},{9,8},{10,9},{11,1... | collective-permute-start | bytes 196616 | tf_op jit(solution)/shard_map/ppermute | solution.py:26
  450.9 4.0 collective-permute-done.25
  455.3 7.3 %copy.1035 = f32[1,32,8,8,8,8]{5,4,3,2,1,0:T(8,128)} copy(f32[1,32,8,8,8,8]{1,5,4,3,2,0:T(8,128)S(1)} %pad_maximum_fusion.3) | data formatting | bytes 1048576 | tf_op jit(solution)/shard_map/concatenate | solution.py:129
  462.6 6.9 %reshape.3996 = f32[256,512]{1,0:T(8,128)S(1)} reshape(f32[1,32,8,8,8,8]{5,4,3,2,1,0:T(8,128)} %copy.1035) | data formatting | bytes 1048576 | tf_op jit(solution)/shard_map/reshape | solution.py:130
  470.2 40.9 %psum.31 = f32[]{:T(128)} all-reduce(f32[]{:T(128)} %multiply_reduce_fusion), channel_id=1, replica_groups=mesh['elem'=16,'face'=2] {'elem','face'}, use_global_device_ids=true, to_apply=%region_8.9 | all-reduce | flops 1 | bytes 8 | tf_op jit(solution)/shard_map/psum | solution.py:229
  (770 shorter events, 110.8 us)
Async XLA Ops:
  0.7 77.2 %collective-permute-start.5 = (f32[32,8]{0,1:T(8,128)S(1)}, f32[32,8]{0,1:T(8,128)S(1)}, u32[]{:S(2)}, u32[]{:S(2)}) collective-permute-start(f32[32,8]{0,1:T(8,128)S(1)} %broadcast.1378), channel_id=1, source_target_pairs={{0,31},{1,0},{2,1},{3,2},{4,3},{5,4},{6,5},{7,6},{8,7},{9,8},{10,9... | collective-permute-start | bytes 3080 | tf_op jit(solution)/shard_map/ppermute | solution.py:33
  56.9 10.7 %copy-start.15 = (f32[512,512]{1,0:T(8,128)S(1)}, f32[512,512]{1,0:T(8,128)}, u32[]{:S(2)}) copy-start(f32[512,512]{1,0:T(8,128)} %constant.1952.clone) | copy-start | bytes 3145732
  57.6 26.7 %collective-permute-start = (f32[1,32,512]{1,2,0:T(8,128)}, f32[1,32,512]{1,2,0:T(8,128)S(1)}, u32[]{:S(2)}, u32[]{:S(2)}) collective-permute-start(f32[1,32,512]{1,2,0:T(8,128)} %bitcast.4), channel_id=1, source_target_pairs={{0,1},{1,2},{2,3},{3,4},{4,5},{5,6},{6,7},{7,8},{8,9},{9,10},{10,1... | collective-permute-start | bytes 196616 | tf_op jit(solution)/shard_map/ppermute | solution.py:25
  57.6 26.7 %collective-permute-start.1 = (f32[1,32,512]{1,2,0:T(8,128)S(1)}, f32[1,32,512]{1,2,0:T(8,128)S(1)}, u32[]{:S(2)}, u32[]{:S(2)}) collective-permute-start(f32[1,32,512]{1,2,0:T(8,128)S(1)} %bitcast.616), channel_id=1, source_target_pairs={{1,0},{2,1},{3,2},{4,3},{5,4},{6,5},{7,6},{8,7},{9,8},{10,9},{11,1... | collective-permute-start | bytes 196616 | tf_op jit(solution)/shard_map/ppermute | solution.py:26
  67.6 20.7 %collective-permute-start.7 = (f32[32,8]{0,1:T(8,128)}, f32[32,8]{0,1:T(8,128)}, u32[]{:S(2)}, u32[]{:S(2)}) collective-permute-start(f32[32,8]{0,1:T(8,128)} %fusion.122), channel_id=1, source_target_pairs={{0,1},{1,2},{2,3},{3,4},{4,5},{5,6},{6,7},{7,8},{8,9},{9,10},{10,1... | collective-permute-start | bytes 3080 | tf_op jit(solution)/shard_map/ppermute | solution.py:33
  82.0 6.9 %collective-permute-start.6 = (f32[32,8]{0,1:T(8,128)}, f32[32,8]{0,1:T(8,128)}, u32[]{:S(2)}, u32[]{:S(2)}) collective-permute-start(f32[32,8]{0,1:T(8,128)} %fusion.136), channel_id=1, source_target_pairs={{0,1},{1,2},{2,3},{3,4},{4,5},{5,6},{6,7},{7,8},{8,9},{9,10},{10,1... | collective-permute-start | bytes 3080 | tf_op jit(solution)/shard_map/ppermute | solution.py:33
  86.0 18.5 %copy-start.36 = (f32[8]{0:T(128)S(1)}, f32[8]{0:T(128)}, u32[]{:S(2)}) copy-start(f32[8]{0:T(128)} %constant.2000) | copy-start | bytes 100
  86.0 18.5 %copy-start.37 = (f32[8]{0:T(128)S(1)}, f32[8]{0:T(128)}, u32[]{:S(2)}) copy-start(f32[8]{0:T(128)} %constant.1999) | copy-start | bytes 100
  88.2 6.6 %collective-permute-start.4 = (f32[32,8]{0,1:T(8,128)S(1)}, f32[32,8]{0,1:T(8,128)S(1)}, u32[]{:S(2)}, u32[]{:S(2)}) collective-permute-start(f32[32,8]{0,1:T(8,128)S(1)} %fusion.131), channel_id=1, source_target_pairs={{0,1},{1,2},{2,3},{3,4},{4,5},{5,6},{6,7},{7,8},{8,9},{9,10},{10,1... | collective-permute-start | bytes 3080 | tf_op jit(solution)/shard_map/ppermute | solution.py:33
  96.3 6.6 %collective-permute-start.8 = (f32[32,8]{0,1:T(8,128)S(1)}, f32[32,8]{0,1:T(8,128)S(1)}, u32[]{:S(2)}, u32[]{:S(2)}) collective-permute-start(f32[32,8]{0,1:T(8,128)S(1)} %get-tuple-element.1163), channel_id=1, source_target_pairs={{0,31},{1,0},{2,1},{3,2},{4,3},{5,4},{6,5},{7,6},{8,7},{9,8},{10,9... | collective-permute-start | bytes 3080 | tf_op jit(solution)/shard_map/ppermute | solution.py:33
  97.4 28.4 %collective-permute-start.2 = (f32[1,32,512]{1,2,0:T(8,128)S(1)}, f32[1,32,512]{1,2,0:T(8,128)S(1)}, u32[]{:S(2)}, u32[]{:S(2)}) collective-permute-start(f32[1,32,512]{1,2,0:T(8,128)S(1)} %bitcast.614), channel_id=1, source_target_pairs={{0,1},{1,2},{2,3},{3,4},{4,5},{5,6},{6,7},{7,8},{8,9},{9,10},{10,1... | collective-permute-start | bytes 196616 | tf_op jit(solution)/shard_map/ppermute | solution.py:25
  97.9 27.8 %collective-permute-start.3 = (f32[1,32,512]{1,2,0:T(8,128)S(1)}, f32[1,32,512]{1,2,0:T(8,128)S(1)}, u32[]{:S(2)}, u32[]{:S(2)}) collective-permute-start(f32[1,32,512]{1,2,0:T(8,128)S(1)} %bitcast.612), channel_id=1, source_target_pairs={{1,0},{2,1},{3,2},{4,3},{5,4},{6,5},{7,6},{8,7},{9,8},{10,9},{11,1... | collective-permute-start | bytes 196616 | tf_op jit(solution)/shard_map/ppermute | solution.py:26
  105.8 6.6 %collective-permute-start.9 = (f32[32,8]{0,1:T(8,128)S(1)}, f32[32,8]{0,1:T(8,128)S(1)}, u32[]{:S(2)}, u32[]{:S(2)}) collective-permute-start(f32[32,8]{0,1:T(8,128)S(1)} %fusion.145), channel_id=1, source_target_pairs={{0,1},{1,2},{2,3},{3,4},{4,5},{5,6},{6,7},{7,8},{8,9},{9,10},{10,1... | collective-permute-start | bytes 3080 | tf_op jit(solution)/shard_map/ppermute | solution.py:33
  112.5 3.7 collective-permute-start.10
  119.0 6.6 %collective-permute-start.11 = (f32[32,8]{0,1:T(8,128)S(1)}, f32[32,8]{0,1:T(8,128)S(1)}, u32[]{:S(2)}, u32[]{:S(2)}) collective-permute-start(f32[32,8]{0,1:T(8,128)S(1)} %fusion.154), channel_id=1, source_target_pairs={{0,1},{1,2},{2,3},{3,4},{4,5},{5,6},{6,7},{7,8},{8,9},{9,10},{10,1... | collective-permute-start | bytes 3080 | tf_op jit(solution)/shard_map/ppermute | solution.py:33
  125.8 1.3 collective-permute-start.12
  129.9 6.6 %collective-permute-start.13 = (f32[32,8]{0,1:T(8,128)S(1)}, f32[32,8]{0,1:T(8,128)S(1)}, u32[]{:S(2)}, u32[]{:S(2)}) collective-permute-start(f32[32,8]{0,1:T(8,128)S(1)} %fusion.163), channel_id=1, source_target_pairs={{0,1},{1,2},{2,3},{3,4},{4,5},{5,6},{6,7},{7,8},{8,9},{9,10},{10,1... | collective-permute-start | bytes 3080 | tf_op jit(solution)/shard_map/ppermute | solution.py:33
  136.6 33.5 %collective-permute-start.14 = (f32[32,8]{0,1:T(8,128)S(1)}, f32[32,8]{0,1:T(8,128)S(1)}, u32[]{:S(2)}, u32[]{:S(2)}) collective-permute-start(f32[32,8]{0,1:T(8,128)S(1)} %fusion.161), channel_id=1, source_target_pairs={{0,31},{1,0},{2,1},{3,2},{4,3},{5,4},{6,5},{7,6},{8,7},{9,8},{10,9... | collective-permute-start | bytes 3080 | tf_op jit(solution)/shard_map/ppermute | solution.py:33
  162.2 9.4 %copy-start.47 = (f32[512]{0:T(512)S(1)}, f32[512]{0:T(512)}, u32[]{:S(2)}) copy-start(f32[512]{0:T(512)} %constant.2014) | copy-start | bytes 6148
  162.2 9.4 %copy-start.49 = (f32[512]{0:T(512)S(1)}, f32[512]{0:T(512)}, u32[]{:S(2)}) copy-start(f32[512]{0:T(512)} %constant.2012) | copy-start | bytes 6148
  162.2 9.4 %copy-start.51 = (f32[512]{0:T(512)S(1)}, f32[512]{0:T(512)}, u32[]{:S(2)}) copy-start(f32[512]{0:T(512)} %constant.2010) | copy-start | bytes 6148
  162.2 9.4 %copy-start.53 = (f32[512]{0:T(512)S(1)}, f32[512]{0:T(512)}, u32[]{:S(2)}) copy-start(f32[512]{0:T(512)} %constant.2008) | copy-start | bytes 6148
  162.2 9.4 %copy-start.55 = (f32[512]{0:T(512)S(1)}, f32[512]{0:T(512)}, u32[]{:S(2)}) copy-start(f32[512]{0:T(512)} %constant.2006) | copy-start | bytes 6148
  162.2 9.4 %copy-start.57 = (f32[512]{0:T(512)S(1)}, f32[512]{0:T(512)}, u32[]{:S(2)}) copy-start(f32[512]{0:T(512)} %constant.2004) | copy-start | bytes 6148
  162.3 9.4 %copy-start.59 = (f32[512]{0:T(512)S(1)}, f32[512]{0:T(512)}, u32[]{:S(2)}) copy-start(f32[512]{0:T(512)} %constant.2002) | copy-start | bytes 6148
  238.2 9.4 %collective-permute-start.15 = (f32[1,32,512]{1,2,0:T(8,128)S(1)}, f32[1,32,512]{1,2,0:T(8,128)S(1)}, u32[]{:S(2)}, u32[]{:S(2)}) collective-permute-start(f32[1,32,512]{1,2,0:T(8,128)S(1)} %bitcast.624), channel_id=1, source_target_pairs={{0,1},{1,2},{2,3},{3,4},{4,5},{5,6},{6,7},{7,8},{8,9},{9,10},{10,1... | collective-permute-start | bytes 196616 | tf_op jit(solution)/shard_map/ppermute | solution.py:25
  238.7 8.9 %collective-permute-start.16 = (f32[1,32,512]{1,2,0:T(8,128)S(1)}, f32[1,32,512]{1,2,0:T(8,128)S(1)}, u32[]{:S(2)}, u32[]{:S(2)}) collective-permute-start(f32[1,32,512]{1,2,0:T(8,128)S(1)} %bitcast.620), channel_id=1, source_target_pairs={{1,0},{2,1},{3,2},{4,3},{5,4},{6,5},{7,6},{8,7},{9,8},{10,9},{11,1... | collective-permute-start | bytes 196616 | tf_op jit(solution)/shard_map/ppermute | solution.py:26
  311.1 6.6 %collective-permute-start.17 = (f32[32,8]{0,1:T(8,128)S(1)}, f32[32,8]{0,1:T(8,128)S(1)}, u32[]{:S(2)}, u32[]{:S(2)}) collective-permute-start(f32[32,8]{0,1:T(8,128)S(1)} %fusion.115), channel_id=1, source_target_pairs={{0,1},{1,2},{2,3},{3,4},{4,5},{5,6},{6,7},{7,8},{8,9},{9,10},{10,1... | collective-permute-start | bytes 3080 | tf_op jit(solution)/shard_map/ppermute | solution.py:33
  317.9 1.3 collective-permute-start.18
  320.8 32.6 %copy-start.13 = (f32[256,512]{1,0:T(8,128)S(1)}, f32[256,512]{1,0:T(8,128)}, u32[]{:S(2)}) copy-start(f32[256,512]{1,0:T(8,128)} %reshape.3980) | copy-start | bytes 1572868
  320.8 32.6 %copy-start.14 = (f32[256,512]{1,0:T(8,128)S(1)}, f32[256,512]{1,0:T(8,128)}, u32[]{:S(2)}) copy-start(f32[256,512]{1,0:T(8,128)} %reshape.3989) | copy-start | bytes 1572868
  320.8 32.6 %copy-start.46 = (f32[512]{0:T(512)S(1)}, f32[512]{0:T(512)}, u32[]{:S(2)}) copy-start(f32[512]{0:T(512)} %constant.2016) | copy-start | bytes 6148
  320.8 32.6 %copy-start.48 = (f32[512]{0:T(512)S(1)}, f32[512]{0:T(512)}, u32[]{:S(2)}) copy-start(f32[512]{0:T(512)} %constant.2014) | copy-start | bytes 6148
  320.8 32.6 %copy-start.50 = (f32[512]{0:T(512)S(1)}, f32[512]{0:T(512)}, u32[]{:S(2)}) copy-start(f32[512]{0:T(512)} %constant.2012) | copy-start | bytes 6148
  320.8 32.6 %copy-start.52 = (f32[512]{0:T(512)S(1)}, f32[512]{0:T(512)}, u32[]{:S(2)}) copy-start(f32[512]{0:T(512)} %constant.2010) | copy-start | bytes 6148
  320.8 32.6 %copy-start.54 = (f32[512]{0:T(512)S(1)}, f32[512]{0:T(512)}, u32[]{:S(2)}) copy-start(f32[512]{0:T(512)} %constant.2008) | copy-start | bytes 6148
  320.8 32.6 %copy-start.56 = (f32[512]{0:T(512)S(1)}, f32[512]{0:T(512)}, u32[]{:S(2)}) copy-start(f32[512]{0:T(512)} %constant.2006) | copy-start | bytes 6148
  320.9 32.6 %copy-start.58 = (f32[512]{0:T(512)S(1)}, f32[512]{0:T(512)}, u32[]{:S(2)}) copy-start(f32[512]{0:T(512)} %constant.2004) | copy-start | bytes 6148
  320.9 32.6 %copy-start.60 = (f32[512]{0:T(512)S(1)}, f32[512]{0:T(512)}, u32[]{:S(2)}) copy-start(f32[512]{0:T(512)} %constant.2002) | copy-start | bytes 6148
  322.1 6.6 %collective-permute-start.19 = (f32[32,8]{0,1:T(8,128)S(1)}, f32[32,8]{0,1:T(8,128)S(1)}, u32[]{:S(2)}, u32[]{:S(2)}) collective-permute-start(f32[32,8]{0,1:T(8,128)S(1)} %fusion.172), channel_id=1, source_target_pairs={{0,1},{1,2},{2,3},{3,4},{4,5},{5,6},{6,7},{7,8},{8,9},{9,10},{10,1... | collective-permute-start | bytes 3080 | tf_op jit(solution)/shard_map/ppermute | solution.py:33
  328.8 1.3 collective-permute-start.20
  333.0 6.6 %collective-permute-start.21 = (f32[32,8]{0,1:T(8,128)S(1)}, f32[32,8]{0,1:T(8,128)S(1)}, u32[]{:S(2)}, u32[]{:S(2)}) collective-permute-start(f32[32,8]{0,1:T(8,128)S(1)} %fusion.181), channel_id=1, source_target_pairs={{0,1},{1,2},{2,3},{3,4},{4,5},{5,6},{6,7},{7,8},{8,9},{9,10},{10,1... | collective-permute-start | bytes 3080 | tf_op jit(solution)/shard_map/ppermute | solution.py:33
  339.7 1.3 collective-permute-start.22
  343.8 6.6 %collective-permute-start.23 = (f32[32,8]{0,1:T(8,128)S(1)}, f32[32,8]{0,1:T(8,128)S(1)}, u32[]{:S(2)}, u32[]{:S(2)}) collective-permute-start(f32[32,8]{0,1:T(8,128)S(1)} %fusion.190), channel_id=1, source_target_pairs={{0,1},{1,2},{2,3},{3,4},{4,5},{5,6},{6,7},{7,8},{8,9},{9,10},{10,1... | collective-permute-start | bytes 3080 | tf_op jit(solution)/shard_map/ppermute | solution.py:33
  350.5 1.3 collective-permute-start.24
  445.4 9.5 %collective-permute-start.25 = (f32[1,32,512]{1,2,0:T(8,128)S(1)}, f32[1,32,512]{1,2,0:T(8,128)S(1)}, u32[]{:S(2)}, u32[]{:S(2)}) collective-permute-start(f32[1,32,512]{1,2,0:T(8,128)S(1)} %bitcast.625), channel_id=1, source_target_pairs={{0,1},{1,2},{2,3},{3,4},{4,5},{5,6},{6,7},{7,8},{8,9},{9,10},{10,1... | collective-permute-start | bytes 196616 | tf_op jit(solution)/shard_map/ppermute | solution.py:25
  445.5 9.5 %collective-permute-start.26 = (f32[1,32,512]{1,2,0:T(8,128)S(1)}, f32[1,32,512]{1,2,0:T(8,128)S(1)}, u32[]{:S(2)}, u32[]{:S(2)}) collective-permute-start(f32[1,32,512]{1,2,0:T(8,128)S(1)} %bitcast.622), channel_id=1, source_target_pairs={{1,0},{2,1},{3,2},{4,3},{5,4},{6,5},{7,6},{8,7},{9,8},{10,9},{11,1... | collective-permute-start | bytes 196616 | tf_op jit(solution)/shard_map/ppermute | solution.py:26
  469.5 43.1 %copy-start.17 = (f32[256,512]{1,0:T(8,128)S(1)}, f32[256,512]{1,0:T(8,128)}, u32[]{:S(2)}) copy-start(f32[256,512]{1,0:T(8,128)} %get-tuple-element.1160) | copy-start | bytes 1572868
  (47 other events, 237.2 us)
where the time goes:
time: 527 us; the launch traced here: 517 us
  local copies, waits for them, and re-layouts  252 us (48%)
  blocking collectives  118 us (22%)
  waiting for transfers between devices  61.8 us (12%)
  other arithmetic  37.6 us (7%)
  starting transfers between devices  29.3 us (6%)
  matrix products  10.5 us (2%)
  between operations  7.43 us (1%)
    psum x2, blocking collectives, progress(): return lax.psum(inner(resid, precond), ('elem', 'face'))  76.9 us
    ppermute x19, waiting for transfers between devices, from_behind(): return lax.ppermute(x, axis, [(i, (i + by) % size) for i in range(size)])  53.8 us
    unnamed x228, local copies, waits for them, and re-layouts  50.6 us
    psum x1, blocking collectives, per_device(): alpha = gamma / lax.psum(inner(direction, image), ('elem', 'face'))  40.9 us
    slice x7, local copies, waits for them, and re-layouts, pair_sum(): middle = lax.slice_in_dim(grid, 1, 7, axis=node_axis)  37.8 us
    concatenate x4, local copies, waits for them, and re-layouts, direct_sum(): jnp.concatenate([first[:, :, :, None], grid[:, :, :, 1:7], shared[:, :, :...  31.1 us
    reshape x4, local copies, waits for them, and re-layouts, direct_sum(): return grid.reshape(-1, 512)  29 us
    slice x3, local copies, waits for them, and re-layouts, pair_sum(): upper = lax.index_in_dim(grid, 7, node_axis, keepdims=True)  27.3 us
  transfers between devices with their start and end apart: 27, of which 15 were waited for; matrix products, arithmetic and copies ran while one was open for 23% of the time, Pallas kernels for 0%

commit v1 on v0

v1 whole, which is shorter than its diff:
```python
import functools
import math

import jax
import jax.numpy as jnp
import numpy as np
from jax import lax
from jax.experimental import pallas as pl
from jax.experimental.pallas import tpu as pltpu
from jax.sharding import PartitionSpec as P

EX = 8
EY = 32
PLANE = EX * EY
SWEEPS = 4
REACT = 0.02
OMEGA = 0.6
AXES = ("elem", "face")
F32 = jnp.float32


def legendre_seven(points):
    before = np.ones(8)
    current = np.array(points)
    for degree in range(1, 7):
        following = ((2 * degree + 1) * points * current - degree * before) / (degree + 1)
        before = current
        current = following
    return current


def line_tables():
    points = np.array(
        [
            -1.0,
            -0.8717401485096066,
            -0.5917001814331423,
            -0.2092992179024789,
            0.2092992179024789,
            0.5917001814331423,
            0.8717401485096066,
            1.0,
        ]
    )
    weights = np.array(
        [
            1.0 / 28.0,
            0.2107042271435061,
            0.3411226924835044,
            0.4124587946587038,
            0.4124587946587038,
            0.3411226924835044,
            0.2107042271435061,
            1.0 / 28.0,
        ]
    )
    legendre = legendre_seven(points)
    derivative = np.zeros((8, 8))
    for left_node in range(8):
        for right_node in range(8):
            if left_node != right_node:
                derivative[left_node, right_node] = legendre[left_node] / (
                    legendre[right_node] * (points[left_node] - points[right_node])
                )
    derivative[0, 0] = -14.0
    derivative[7, 7] = 14.0
    stiffness = derivative.T @ (weights[:, None] * derivative)
    return points, weights, stiffness


POINTS, WEIGHTS, STIFF = line_tables()
DIAG = np.diag(STIFF)
ENDS = np.array([2.0] + [1.0] * 6 + [2.0])
MASS = np.diag(WEIGHTS)
STIFF_XY = np.tile(np.kron(MASS, STIFF) + np.kron(STIFF, MASS), (1, 2))
INTERP = np.stack([(1.0 - POINTS) / 2.0, (1.0 + POINTS) / 2.0], 1)
LINE_MASS = INTERP.T @ (WEIGHTS[:, None] * INTERP)
LINE_STIFF = INTERP.T @ STIFF @ INTERP
MASS_SUM = (LINE_MASS[0, 0] + LINE_MASS[0, 1]) / 2.0
MASS_DIF = (LINE_MASS[0, 0] - LINE_MASS[0, 1]) / 2.0
STIFF_DIF = LINE_STIFF[0, 0]
MODE_STIFF = [
    0.0,
    STIFF_DIF * MASS_SUM**2,
    2.0 * STIFF_DIF * MASS_DIF * MASS_SUM,
    3.0 * STIFF_DIF * MASS_DIF**2,
]
MODE_MASS = [MASS_SUM ** (3 - j) * MASS_DIF**j for j in range(4)]
CORNER_STIFF = 3.0 * LINE_STIFF[0, 0] * LINE_MASS[0, 0] ** 2
CORNER_MASS = LINE_MASS[0, 0] ** 3


def lane(shape):
    return lax.broadcasted_iota(jnp.int32, shape, len(shape) - 1)


def next_x(v):
    return jnp.where(lane(v.shape) % EX == EX - 1, pltpu.roll(v, EX - 1, 1), pltpu.roll(v, PLANE - 1, 1))


def prev_x(v):
    return jnp.where(lane(v.shape) % EX == 0, pltpu.roll(v, PLANE - EX + 1, 1), pltpu.roll(v, 1, 1))


def next_y(v):
    return pltpu.roll(v, PLANE - EX, 1)


def prev_y(v):
    return pltpu.roll(v, EX, 1)


def next_z(v):
    half = v.shape[0] // 2
    return jnp.concatenate([v[half:], pltpu.roll(v[:half], half - 1, 0)], axis=0)


def prev_z(v):
    half = v.shape[0] // 2
    return jnp.concatenate([pltpu.roll(v[half:], 1, 0), v[:half]], axis=0)


def plane_row(layer, planes):
    layer = lax.rem(layer + planes, planes)
    return pl.ds(lax.div(layer, 2) + lax.rem(layer, 2) * (planes // 2), 1)


def column(values):
    row = lax.broadcasted_iota(jnp.int32, (8, PLANE), 0)
    out = jnp.full((8, PLANE), float(values[0]), F32)
    for k in range(1, 8):
        out = jnp.where(row == k, float(values[k]), out)
    return out


def rows_of(nz, ny):
    start = (nz * 8 + ny) * 8
    return slice(start, start + 8)


def get(ref, rows):
    return jnp.concatenate([ref[0, rows, :], ref[1, rows, :]], axis=1)


def put(ref, rows, value):
    ref[0, rows, :] = value[:, :128]
    ref[1, rows, :] = value[:, 128:]


def sum_xy(ref):
    planes = ref.shape[1] // 64
    first, last = pl.ds(0, planes * 8, stride=8), pl.ds(7, planes * 8, stride=8)
    shared = get(ref, last) + next_x(get(ref, first))
    put(ref, last, shared)
    put(ref, first, prev_x(shared))
    for nz in range(planes):
        shared = get(ref, rows_of(nz, 7)) + next_y(get(ref, rows_of(nz, 0)))
        put(ref, rows_of(nz, 7), shared)
        put(ref, rows_of(nz, 0), prev_y(shared))


def restrict(ref, points, inv_ends):
    sums_z, difs_z = [], []
    for ny in range(8):
        tiles = [get(ref, rows_of(nz, ny)) for nz in range(8)]
        sums_z.append(functools.reduce(lambda a, b: a + b, tiles))
        difs_z.append(sum(float(POINTS[7 - k]) * (tiles[7 - k] - tiles[k]) for k in range(4)))
    return restrict_xy(sums_z, difs_z, points, inv_ends)


def restrict_xy(sums_z, difs_z, points, inv_ends):
    planes = []
    for parts in (sums_z, difs_z):
        parts = [part * float(1.0 / ENDS[ny]) for ny, part in enumerate(parts)]
        total = functools.reduce(lambda a, b: a + b, parts)
        slope = sum(float(POINTS[7 - k]) * (parts[7 - k] - parts[k]) for k in range(4))
        in_y = []
        for part in (total * inv_ends, slope * inv_ends):
            flat = jnp.sum(part, axis=0, keepdims=True)
            steep = jnp.sum(part * points, axis=0, keepdims=True)
            in_y.append((flat - steep) + prev_x(flat + steep))
        planes.append((in_y[0] - in_y[1]) + prev_y(in_y[0] + in_y[1]))
    return (planes[0] - planes[1]) * 0.125, (planes[0] + planes[1]) * 0.125


def both(v, following):
    after = following(v)
    return after + v, after - v


def both_back(total, dif, preceding):
    return (total - dif) + preceding(total + dif)


def coarse_modes(coeff):
    return [float(REACT * MODE_MASS[0])] + [
        float(MODE_STIFF[j]) * coeff + float(REACT * MODE_MASS[j]) for j in range(1, 4)
    ]


def coarse_tables(coeff):
    near = coeff + prev_x(coeff)
    near = near + prev_y(near)
    near = near + prev_z(near)
    scale = float(OMEGA) / (float(CORNER_STIFF) * near + float(8.0 * REACT * CORNER_MASS))
    return coarse_modes(coeff), scale


def coarse_apply(vert, modes):
    in_x = both(vert, next_x)
    back_x = []
    for jx in range(2):
        in_y = both(in_x[jx], next_y)
        back_y = []
        for jy in range(2):
            in_z = both(in_y[jy], next_z)
            scaled = [modes[jx + jy + jz] * in_z[jz] for jz in range(2)]
            back_y.append(both_back(scaled[0], scaled[1], prev_z))
        back_x.append(both_back(back_y[0], back_y[1], prev_y))
    return both_back(back_x[0], back_x[1], prev_x)


def coarse_solve(target, modes, scale):
    vert = scale * target
    for _ in range(SWEEPS - 1):
        vert = vert + scale * (target - coarse_apply(vert, modes))
    return vert


def gathered(ref, k, size):
    chips = ref.shape[0] // (4 * size)
    parts = []
    for core in range(2):
        rows = [ref[pl.ds((core * size + k) * 2 + h, chips, stride=4 * size), :] for h in range(2)]
        parts.append(jnp.concatenate(rows, axis=1))
    return jnp.concatenate(parts, axis=0)


def halves(row):
    return [row[:, :128], row[:, 128:]]


def send(ref, planes):
    block = jnp.concatenate([half for plane in planes for half in halves(plane)], axis=0)
    rows = block.shape[0]
    times = 8 // math.gcd(rows, 8)
    block = jnp.concatenate([block] * times, axis=0)
    for k in range(0, ref.shape[0], rows * times):
        ref[k : k + rows * times, :] = block


def layer_modes(vert_ref, shift):
    me, devices = my_layer(), vert_ref.shape[0]
    lower, upper = (vert_ref[plane_row(me + shift + k, devices), :] for k in range(2))
    modes = []
    for along_z in (upper + lower, upper - lower):
        for along_y in both(along_z, next_y):
            modes += both(along_y, next_x)
    return 0.125 * jnp.concatenate(modes, axis=0)


class Smooth:
    def __init__(self, modes, coeff, points, weight_x):
        row = lax.broadcasted_iota(jnp.int32, (8, PLANE), 0)
        ends = jnp.where(row == 0, -1.0, jnp.where(row == 7, 1.0, 0.0))
        m = [[[modes[4 * z + 2 * y + x : 4 * z + 2 * y + x + 1] for x in range(2)] for y in range(2)] for z in range(2)]
        self.xy = [[m[z][y][0] + m[z][y][1] * points for y in range(2)] for z in range(2)]
        self.dx = [[m[z][y][1] for y in range(2)] for z in range(2)]
        self.ends_coeff = ends * coeff
        self.weight_coeff = weight_x * coeff
        self.mass = float(REACT) * weight_x

    def value(self, nz, ny):
        by_y = [self.xy[z][0] + float(POINTS[ny]) * self.xy[z][1] for z in range(2)]
        return by_y[0] + float(POINTS[nz]) * by_y[1]

    def operated(self, nz, ny, value):
        wy, wz, py, pz = (float(t) for t in (WEIGHTS[ny], WEIGHTS[nz], POINTS[ny], POINTS[nz]))
        slope = (self.dx[0][0] + py * self.dx[0][1]) + pz * (self.dx[1][0] + py * self.dx[1][1])
        out = self.ends_coeff * (slope * (wy * wz)) + (self.mass * (wy * wz)) * value
        flux = None
        if ny in (0, 7):
            flux = (self.xy[0][1] + pz * self.xy[1][1]) * (wz * py)
        if nz in (0, 7):
            along = (self.xy[1][0] + py * self.xy[1][1]) * (wy * pz)
            flux = along if flux is None else flux + along
        return out if flux is None else out + self.weight_coeff * flux


def kappa_sums(own, below, above):
    row = lax.broadcasted_iota(jnp.int32, (8, PLANE), 0)
    table = []
    for along_z in (own + below, own, own + above):
        in_z = []
        for along_y in (along_z + prev_y(along_z), along_z, along_z + next_y(along_z)):
            first = along_y + prev_x(along_y)
            last = along_y + next_x(along_y)
            in_z.append(jnp.where(row == 0, first, jnp.where(row == 7, last, along_y)))
        table.append(in_z)
    return table


def kind(node):
    return 0 if node == 0 else (2 if node == 7 else 1)


def operate(z_ref, xy_ref, out_ref, table_ref, coeff, weight_x):
    table = jnp.tile(table_ref[...], (4, 2))
    row, col = (lax.broadcasted_iota(jnp.int32, table.shape, axis) for axis in range(2))
    table = jnp.where(row // 64 == col // 64, table, 0.0)
    for half in range(2):
        rows = slice(half * 256, half * 256 + 256)
        xy_ref[rows, :] = jnp.dot(
            table, get(z_ref, rows), precision=lax.Precision.HIGHEST, preferred_element_type=F32
        )
    for ny in range(8):
        tiles = [get(z_ref, rows_of(nz, ny)) for nz in range(8)]
        even = [tiles[k] + tiles[7 - k] for k in range(4)]
        odd = [tiles[k] - tiles[7 - k] for k in range(4)]
        for nz in range(4):
            even_part = sum(float((STIFF[nz, k] + STIFF[nz, 7 - k]) / 2) * even[k] for k in range(4))
            odd_part = sum(float((STIFF[nz, k] - STIFF[nz, 7 - k]) / 2) * odd[k] for k in range(4))
            for node, term in ((nz, even_part + odd_part), (7 - nz, even_part - odd_part)):
                area = weight_x * float(WEIGHTS[ny])
                local = coeff * (
                    float(WEIGHTS[node]) * xy_ref[rows_of(node, ny), :] + area * term
                ) + (float(REACT * WEIGHTS[node]) * area) * tiles[node]
                put(out_ref, rows_of(node, ny), local)


def fine_diag(sums, nz, ny, weight_x, diag_x, ends_x):
    wy, wz, ky, kz = (float(t) for t in (WEIGHTS[ny], WEIGHTS[nz], DIAG[ny], DIAG[nz]))
    stiff = diag_x * (wy * wz) + weight_x * (ky * wz + wy * kz)
    mass = (weight_x * ends_x) * float(REACT * wy * wz * ENDS[ny] * ENDS[nz])
    return sums[kind(nz)][kind(ny)] * stiff + mass


def my_layer():
    return lax.axis_index("elem") * lax.axis_size("face") + lax.axis_index("face")


def face_rows(ref):
    even = lax.rem(my_layer(), 2) == 0
    last = ref.shape[1] - 64
    near = pl.multiple_of(jnp.where(even, last, 0), 64)
    far = pl.multiple_of(jnp.where(even, 0, last), 64)
    return pl.ds(near, 64), pl.ds(far, 64)


def faces_out(ref, near_ref, far_ref):
    near, far = face_rows(ref)
    near_ref[:, 0:64, :] = ref[:, near, :]
    far_ref[:, 0:64, :] = ref[:, far, :]


def faces_in(ref, near_ref, far_ref):
    near, far = face_rows(ref)
    ref[:, near, :] += near_ref[:, 0:64, :]
    ref[:, far, :] += far_ref[:, 0:64, :]


def columns_of_nodes():
    return column(POINTS), column(WEIGHTS), column(DIAG), column(ENDS)


def pieces(v):
    high = v.astype(jnp.bfloat16)
    rest = v - high.astype(F32)
    middle = rest.astype(jnp.bfloat16)
    low = (rest - middle.astype(F32)).astype(jnp.bfloat16)
    return low, middle, high


def selection(order):
    place = lax.broadcasted_iota(jnp.int32, (PLANE, PLANE), 0).astype(order.dtype)
    return jnp.where(place == order, 1.0, 0.0).astype(jnp.bfloat16)


def opening(
    forcing_ref, kappa_ref, order_ref, load_ref, far_ref, near_ref, own_ref, held, held_kappa, held_order, sems
):
    small = [
        pltpu.make_async_copy(order_ref, held_order, sems.at[0]),
        pltpu.make_async_copy(kappa_ref, held_kappa, sems.at[1]),
    ]
    parts = [
        pltpu.make_async_copy(forcing_ref.at[:, pl.ds(256 * k, 256)], held.at[k], sems.at[2 + k]) for k in range(2)
    ]
    for copy in small + parts:
        copy.start()
    for copy in small:
        copy.wait()
    order = held_order[...]
    choose = selection(order)
    coeff = jnp.zeros((8, PLANE), F32)
    for piece in pieces(jnp.broadcast_to(held_kappa[...], (8, PLANE))):
        coeff = coeff + lax.dot_general(piece, choose, (((1,), (1,)), ((), ())), preferred_element_type=F32)
    own = jnp.concatenate([coeff[0:3], order.astype(F32), coeff[4:8]], axis=0)
    own_ref[...] = own
    for k, copy in enumerate(parts):
        copy.wait()
        load = jnp.zeros((PLANE, 256), F32)
        for piece in pieces(held[k]):
            load = load + jnp.dot(choose, piece, preferred_element_type=F32)
        put(load_ref, slice(256 * k, 256 * k + 256), load.T)
    sum_xy(load_ref)
    faces_out(load_ref, near_ref, far_ref)
    put(near_ref, slice(64, 72), own)
    put(far_ref, slice(64, 72), own)


def opening_payload(load_ref, own_ref, payload_ref):
    lower, upper = restrict(load_ref, column(POINTS), column(1.0 / ENDS))
    send(payload_ref, [lower, upper, own_ref[0:1, :]])


def below_above(near, far):
    even = lax.rem(my_layer(), 2) == 0
    return jnp.where(even, far, near), jnp.where(even, near, far)


def row_after_face(ref):
    return get(ref, slice(64, 72))[0:1]


def first_faces(
    load_ref, far_in_ref, near_in_ref, own_ref, table_ref,
    resid_ref, scaled_ref, image_ref, layers_ref, lower_ref, far_ref, near_ref, xy_ref,
):
    points, weight_x, _, _ = columns_of_nodes()
    own = own_ref[0:1, :]
    below, above = below_above(row_after_face(near_in_ref), row_after_face(far_in_ref))
    layers_ref[...] = jnp.concatenate([own, below, above, own_ref[3:8, :]], axis=0)
    resid_ref[...] = load_ref[...]
    faces_in(resid_ref, near_in_ref, far_in_ref)
    over_diag(functools.partial(get, resid_ref), scaled_ref, layers_ref)
    operate(scaled_ref, xy_ref, image_ref, table_ref, own, weight_x)
    sum_xy(image_ref)
    faces_out(image_ref, near_ref, far_ref)
    lower, upper = restrict(image_ref, points, column(1.0 / ENDS))
    lower_ref[...] = jnp.broadcast_to(lower, lower_ref.shape)
    put(near_ref, slice(64, 72), jnp.broadcast_to(upper, (8, PLANE)))
    put(far_ref, slice(64, 72), jnp.broadcast_to(upper, (8, PLANE)))


def over_diag(resid, scaled_ref, layers_ref):
    _, weight_x, diag_x, ends_x = columns_of_nodes()
    sums = kappa_sums(*(layers_ref[k : k + 1, :] for k in range(3)))
    for nz in range(8):
        for ny in range(8):
            rows = rows_of(nz, ny)
            put(scaled_ref, rows, resid(rows) / fine_diag(sums, nz, ny, weight_x, diag_x, ends_x))


def three_modes(vert_ref):
    return jnp.concatenate([layer_modes(vert_ref, shift) for shift in (0, -1, 1)], axis=0)


def smooths_of(modes, layers_ref):
    points, weight_x, _, _ = columns_of_nodes()
    return [Smooth(modes[8 * k : 8 * k + 8], layers_ref[k : k + 1, :], points, weight_x) for k in range(3)]


def smooth_image(smooths, out_ref, edge_ref):
    own, below, above = smooths
    for nz in range(8):
        for ny in range(8):
            put(out_ref, rows_of(nz, ny), own.operated(nz, ny, own.value(nz, ny)))
    sum_xy(out_ref)
    for plane, (smooth, nz) in enumerate(((below, 7), (above, 0))):
        for ny in range(8):
            put(edge_ref, rows_of(plane, ny), smooth.operated(nz, ny, smooth.value(nz, ny)))
    sum_xy(edge_ref)
    out_ref[:, 0:64, :] += edge_ref[:, 0:64, :]
    out_ref[:, 448:512, :] += edge_ref[:, 64:128, :]


def first_coarse(
    coarse_ref, layers_ref, vert_ref, applied_ref, target_ref, scale_ref, coeff_ref, choose_ref, smooth_ref, edge_ref
):
    coeff = gathered(coarse_ref, 2, 3)
    coeff_ref[...] = coeff
    choose_ref[...] = selection(layers_ref[3:4, :]).astype(F32).T.astype(jnp.bfloat16)
    modes, scale = coarse_tables(coeff)
    target = gathered(coarse_ref, 0, 3) + prev_z(gathered(coarse_ref, 1, 3))
    vert = coarse_solve(target, modes, scale)
    vert_ref[...] = vert
    applied_ref[...] = coarse_apply(vert, modes)
    target_ref[...] = target
    scale_ref[...] = scale
    smooth_image(smooths_of(three_modes(vert_ref), layers_ref), smooth_ref, edge_ref)


def pack(sums):
    rows = [jnp.sum(t, axis=0, keepdims=True) for t in sums]
    rows = jnp.concatenate(rows + [jnp.zeros((1, PLANE), F32)] * (8 - len(rows)), axis=0)
    for by in (128, 64, 32):
        rows = rows + pltpu.roll(rows, by, 1)
    place = lax.broadcasted_iota(jnp.int32, rows.shape, 0)
    return jnp.sum(jnp.where(lane(rows.shape) // 32 == place, rows, 0.0), axis=0, keepdims=True)


def second_rough(
    first_ref, smooth_ref, near_in_ref, layers_ref, table_ref, resid_ref, scaled_ref,
    image_ref, whole_ref, scaled_change_ref, change_ref, sums_ref, planes_ref, xy_ref,
):
    points, weight_x, _, _ = columns_of_nodes()
    inv_ends = column(1.0 / ENDS)
    image_ref[...] = first_ref[...]
    near, _ = face_rows(image_ref)
    image_ref[:, near, :] += near_in_ref[:, 0:64, :]
    whole_ref[...] = image_ref[...] + smooth_ref[...]
    over_diag(functools.partial(get, whole_ref), scaled_change_ref, layers_ref)
    operate(scaled_change_ref, xy_ref, change_ref, table_ref, layers_ref[0:1, :], weight_x)
    sum_xy(change_ref)
    sums = [jnp.zeros((8, PLANE), F32)] * 5
    for nz in range(8):
        for ny in range(8):
            rows = rows_of(nz, ny)
            share = float(1.0 / (ENDS[nz] * ENDS[ny]))
            scaled, scaled_change = get(scaled_ref, rows) * share, get(scaled_change_ref, rows) * share
            whole, image = get(whole_ref, rows), get(image_ref, rows)
            terms = [
                scaled * get(resid_ref, rows), scaled * whole, scaled_change * whole, scaled * image, scaled_change * image
            ]
            sums = [total + term for total, term in zip(sums, terms)]
    sums_ref[...] = jnp.concatenate(sums, axis=0)
    planes_ref[...] = jnp.concatenate(list(restrict(change_ref, points, inv_ends)) * 4, axis=0)


def second_faces(
    first_ref, first_scaled_ref, first_change_ref, whole_ref, far_in_ref, near_in_ref, layers_ref, table_ref,
    scaled_ref, lower_ref, sums_ref, planes_ref,
    image_ref, scaled_change_ref, change_ref, far_ref, near_ref, payload_ref, edge_ref, xy_ref,
):
    points, weight_x, diag_x, ends_x = columns_of_nodes()
    inv_ends = column(1.0 / ENDS)
    for out_ref, ref in (
        (image_ref, first_ref), (scaled_change_ref, first_scaled_ref), (change_ref, first_change_ref)
    ):
        out_ref[...] = ref[...]
    even = lax.rem(my_layer(), 2) == 0
    own = layers_ref[0:1, :]
    beyond = jnp.where(even, layers_ref[1:2, :], layers_ref[2:3, :])
    kappas = kappa_sums(own, beyond, beyond)
    _, far = face_rows(image_ref)
    sums = [sums_ref[8 * k : 8 * k + 8, :] for k in range(5)]
    s_plane, q_plane, i_plane, w_plane = (
        get(ref, far) for ref in (scaled_ref, scaled_change_ref, image_ref, whole_ref)
    )
    added = []
    for ny in range(8):
        tile = slice(8 * ny, 8 * ny + 8)
        face = get(far_in_ref, tile)
        dq = face / fine_diag(kappas, 0, ny, weight_x, diag_x, ends_x)
        added.append(dq)
        share = float(1.0 / (ENDS[0] * ENDS[ny]))
        s, q, image, whole = s_plane[tile] * share, q_plane[tile] * share, i_plane[tile], w_plane[tile]
        dq = dq * share
        sums[1] = sums[1] + s * face
        sums[2] = sums[2] + (q * face + dq * (whole + face))
        sums[3] = sums[3] + s * face
        sums[4] = sums[4] + (q * face + dq * (image + face))
    plane = jnp.concatenate(added, axis=0)
    put(image_ref, far, i_plane + get(far_in_ref, slice(0, 64)))
    put(scaled_change_ref, far, q_plane + plane)
    xy_ref[...] = jnp.dot(
        table_ref[:, 0:64], plane, precision=lax.Precision.HIGHEST, preferred_element_type=F32
    )
    for ny in range(8):
        area = weight_x * float(WEIGHTS[ny])
        put(edge_ref, rows_of(0, ny), own * area * added[ny])
        flux = own * xy_ref[8 * ny : 8 * ny + 8, :] + (float(REACT) * area) * added[ny]
        put(edge_ref, rows_of(1, ny), float(WEIGHTS[0]) * flux)
    sum_xy(edge_ref)
    put(change_ref, far, get(change_ref, far) + get(edge_ref, slice(64, 128)))
    energy = jnp.zeros((8, PLANE), F32)
    for nz in range(8):
        factor = jnp.where(even, float(STIFF[nz, 0]), float(STIFF[nz, 7]))
        for ny in range(8):
            rows = rows_of(nz, ny)
            change = get(change_ref, rows) + factor * get(edge_ref, rows_of(0, ny))
            put(change_ref, rows, change)
            energy = energy + (get(scaled_change_ref, rows) * change) * float(1.0 / ENDS[ny])
    faces_out(change_ref, near_ref, far_ref)
    sign = jnp.where(even, -1.0, 1.0)
    along = [get(edge_ref, rows_of(0, ny)) for ny in range(8)]
    at_face = [get(edge_ref, rows_of(1, ny)) for ny in range(8)]
    lower, upper = restrict_xy(at_face, [sign * (a + b) for a, b in zip(along, at_face)], points, inv_ends)
    lower, upper = lower + planes_ref[0:1, :], upper + planes_ref[1:2, :]
    below, _ = below_above(row_after_face(near_in_ref), row_after_face(far_in_ref))
    sums = pack([total * inv_ends for total in sums + [energy]])
    send(payload_ref, [lower_ref[0:1, :] + below, lower, upper, sums])


def folded(value):
    return functools.reduce(lambda a, b: a + b, [value[k : k + 8] for k in range(0, value.shape[0], 8)])


def second_coarse(
    coeff_ref, step_ref, first_ref, applied_ref, target_ref, scale_ref, modes_ref, scalars_ref, vert_ref
):
    modes = coarse_modes(coeff_ref[...])
    target, first, applied = target_ref[...], first_ref[...], applied_ref[...]
    rough, rough_change = gathered(step_ref, 0, 4), gathered(step_ref, 1, 4) + prev_z(gathered(step_ref, 2, 4))
    parts = folded(gathered(step_ref, 3, 4))
    sums = [parts] + [pltpu.roll(parts, PLANE - 32 * k, 1) for k in range(1, 6)]
    used = lane(parts.shape) < 32

    def total(fine, coarse):
        return jnp.sum(jnp.where(used, fine, 0.0) + folded(coarse), keepdims=True)

    gamma = total(sums[0], target * first)
    energy = total(sums[3], first * (2.0 * rough + applied))
    alpha = gamma / energy
    change = rough + applied
    target = target - alpha * change
    vert = coarse_solve(target, modes, scale_ref[...])
    progress = total(sums[0] - alpha * (2.0 * sums[1] - alpha * sums[2]), target * vert)
    second = total(
        sums[3] - alpha * (2.0 * sums[4] - alpha * sums[5]),
        vert * (2.0 * (rough - alpha * rough_change) + coarse_apply(vert, modes)),
    )
    cross = total(sums[1] - alpha * sums[2], vert * change)
    beta = progress / gamma
    alpha_next = progress / (second + beta * (2.0 * cross + beta * energy))
    share = alpha + alpha_next * beta
    vert_ref[...] = share * first + alpha_next * vert
    modes_ref[...] = three_modes(vert_ref)
    scalars = [share + alpha_next, alpha_next * alpha]
    scalars_ref[...] = jnp.concatenate([jnp.broadcast_to(t, (1, 128)) for t in scalars * 4], axis=0)


def to_stored(choose, value):
    total = jnp.zeros((PLANE, value.shape[0]), F32)
    for piece in pieces(value)[1:]:
        total = total + lax.dot_general(choose, piece, (((1,), (1,)), ((), ())), preferred_element_type=F32)
    return total


def closing(
    resid_ref, scaled_ref, image_ref, scaled_change_ref, change_ref, far_ref, near_ref, modes_ref, layers_ref, scalars_ref,
    choose_ref, solution_ref, residual_ref, grid_ref, sum_ref, edge_ref, held, sems,
):
    smooths = smooths_of(modes_ref[...], layers_ref)
    first, second = scalars_ref[0:1, 0:1], scalars_ref[1:2, 0:1]
    choose = choose_ref[...]
    for nz in range(8):
        for ny in range(8):
            rows = rows_of(nz, ny)
            rough = first * get(scaled_ref, rows) - second * get(scaled_change_ref, rows)
            grid_ref[rows, :] = rough + smooths[0].value(nz, ny)
    held[0] = to_stored(choose, grid_ref[...])
    copies = [pltpu.make_async_copy(held.at[0], solution_ref, sems.at[0])]
    copies[0].start()
    smooth_image(smooths, sum_ref, edge_ref)
    first, second = first[None], second[None]
    sum_ref[...] = resid_ref[...] - first * image_ref[...] + second * change_ref[...] - sum_ref[...]
    near, far = face_rows(sum_ref)
    sum_ref[:, near, :] += second * near_ref[...]
    sum_ref[:, far, :] += second * far_ref[...]
    held[1] = to_stored(choose, get(sum_ref, slice(0, 512)))
    copies.append(pltpu.make_async_copy(held.at[1], residual_ref, sems.at[1]))
    copies[1].start()
    for copy in copies:
        copy.wait()


def call(kernel, outs, scratch=(), sems=0, hbm_out=False, cost=None, in_place=None, hbm_in=0):
    spec = pl.BlockSpec(memory_space=pltpu.HBM if hbm_out else pltpu.VMEM)
    more = {"in_specs": [pl.BlockSpec(memory_space=pltpu.HBM)] * hbm_in} if hbm_in else {}
    return pl.pallas_call(
        kernel,
        out_shape=[jax.ShapeDtypeStruct(*(s if isinstance(s[0], tuple) else (s, F32))) for s in outs],
        out_specs=[spec for _ in outs],
        scratch_shapes=[pltpu.VMEM(*(s if isinstance(s[0], tuple) else (s, F32))) for s in scratch]
        + ([pltpu.SemaphoreType.DMA((sems,))] if sems else []),
        compiler_params=pltpu.CompilerParams(vmem_limit_bytes=12 * 1024 * 1024),
        cost_estimate=cost,
        input_output_aliases=in_place or {},
        **more,
    )


def swapped(x, far):
    size = lax.axis_size(AXES)
    return lax.ppermute(x, AXES, [(i, (i + (1 if (i % 2 == 0) != far else -1)) % size) for i in range(size)])


def everyone(payload, size):
    devices = lax.axis_size(AXES)
    return lax.all_to_all(payload.reshape(devices, size, 2, 128), AXES, 0, 0, tiled=True).reshape(-1, 128)


def per_device(forcing, kappa, elem_order):
    devices = lax.axis_size(AXES)
    nodes, face, face_row = (2, 512, 128), (2, 64, 128), (2, 72, 128)
    plane, grid, flat = (8, PLANE), (devices, PLANE), (512, PLANE)
    edge, stored, choice = (2, 128, 128), (PLANE, 512), ((PLANE, PLANE), jnp.bfloat16)
    table = jnp.asarray(STIFF_XY, F32)
    long = pl.CostEstimate(flops=10**11, bytes_accessed=2**28, transcendentals=0)
    load, far, near, own = call(
        opening,
        [nodes, face_row, face_row, plane],
        [(2, PLANE, 256), (1, PLANE), ((1, PLANE), jnp.int32)],
        4,
        hbm_in=3,
    )(*(pltpu.with_memory_space_constraint(x, pltpu.HBM) for x in (forcing, kappa.reshape(1, PLANE), elem_order)))
    far, near = swapped(far, True), swapped(near, False)
    (payload,) = call(opening_payload, [(devices * 6, 128)])(load, own)
    gather = everyone(payload, 3)
    resid, scaled, image, layers, lower, far, near = call(
        first_faces, [nodes, nodes, nodes, plane, plane, face_row, face_row], [flat], cost=long, in_place={0: 0}
    )(load, far, near, own, table)
    far, near = swapped(far, True), swapped(near, False)
    vert, applied, target, scale, coeff, choose, smooth = call(first_coarse, [grid] * 5 + [choice, nodes], [edge])(
        gather, layers
    )
    image, whole, scaled_change, change, sums, planes = call(
        second_rough, [nodes] * 4 + [(40, PLANE), plane], [flat], in_place={0: 0, 1: 1}
    )(image, smooth, near, layers, table, resid, scaled)
    image, scaled_change, change, far, near, payload = call(
        second_faces, [nodes] * 3 + [face, face, (devices * 8, 128)], [edge, (64, PLANE)], in_place={0: 0, 1: 1, 2: 2}
    )(image, scaled_change, change, whole, far, near, layers, table, scaled, lower, sums, planes)
    step = everyone(payload, 4)
    far, near = swapped(far, True), swapped(near, False)
    modes, scalars = call(second_coarse, [(24, PLANE), (8, 128)], [grid])(coeff, step, vert, applied, target, scale)
    found, left = call(closing, [stored, stored], [flat, nodes, edge, (2,) + stored], 2, hbm_out=True)(
        resid, scaled, image, scaled_change, change, far, near, modes, layers, scalars, choose
    )
    return found, left


def solution(mesh):
    in_specs = (P(AXES, None), P(AXES), P(AXES, None))
    out_specs = (P(AXES, None), P(AXES, None))
    return jax.shard_map(
        per_device, mesh=mesh, in_specs=in_specs, out_specs=out_specs, check_vma=False
    )
```

time: 527 us -> 42.5 us (0.08); the launches traced: 517 us -> 41.8 us
  local copies, waits for them, and re-layouts: 252 us -> 0.01 us
  blocking collectives: 118 us -> 0 us
  waiting for transfers between devices: 61.8 us -> 3.61 us
  other arithmetic: 37.6 us -> 0 us
  Pallas kernels: 0 us -> 14.3 us
  matrix products: 10.5 us -> 0 us
  between operations: 7.43 us -> 0.73 us
  starting transfers between devices: 29.3 us -> 23.1 us
    psum x3 -> x0, blocking collectives: 118 us -> none  [the longest x2 76.9 us: progress(): return lax.psum(inner(resid, precond), ('elem', 'face'))]
    slice x191 -> x0, local copies, waits for them, and re-layouts: 95.9 us -> none  [the longest x7 37.8 us: pair_sum(): middle = lax.slice_in_dim(grid, 1, 7, axis=node_axis)]
    ppermute x27 -> x6, waiting for transfers between devices: 61.8 us -> 0.02 us  [swapped(): lax.ppermute(x, AXES, [(i, (i + (1 if (i % 2 == 0) != far else -1)) % siz...]
    reshape x16 -> x0, local copies, waits for them, and re-layouts: 51.9 us -> none  [the longest x4 29 us: direct_sum(): return grid.reshape(-1, 512)]
    unnamed x228 -> x2, local copies, waits for them, and re-layouts: 50.6 us -> 0.01 us
    concatenate x142 -> x0, local copies, waits for them, and re-layouts: 37.4 us -> none  [the longest x4 31.1 us: direct_sum(): jnp.concatenate([first[:, :, :, None], grid[:, :, :, 1:7], shared[:, :, :...]
    concatenate x86 -> x0, other arithmetic: 15.2 us -> none  [the longest x4 4.99 us: direct_sum(): jnp.concatenate([first[:, :, :, None], grid[:, :, :, 1:7], shared[:, :, :...]
    pallas_call x0 -> x8, Pallas kernels: none -> 14.3 us  [the longest x1 2.25 us: per_device(): call(first_coarse, [grid] * 5 + [choice, nodes], [edge])(gather, layers)]
  transfers between devices with their start and end apart: 27 -> 8, of which waited for: 15 -> 2; matrix products, arithmetic and copies ran while one was open for 23% -> 0% of each run, Pallas kernels for 0% -> 20%
where the time goes in v1:
time: 42.5 us; the launch traced here: 41.8 us
  starting transfers between devices  23.1 us (54%)
  Pallas kernels  14.3 us (34%)
  waiting for transfers between devices  3.61 us (8%)
  between operations  0.73 us (2%)
    ppermute x6, starting transfers between devices, swapped(): lax.ppermute(x, AXES, [(i, (i + (1 if (i % 2 == 0) != far else -1)) % siz...  17.3 us
    all_to_all x2, starting transfers between devices, everyone(): lax.all_to_all(payload.reshape(devices, size, 2, 128), AXES, 0, 0, tiled=...  5.76 us
    all_to_all x2, waiting for transfers between devices, everyone(): lax.all_to_all(payload.reshape(devices, size, 2, 128), AXES, 0, 0, tiled=...  3.59 us
    pallas_call x1, Pallas kernels, per_device(): call(first_coarse, [grid] * 5 + [choice, nodes], [edge])(gather, layers)  2.25 us
    pallas_call x1, Pallas kernels, per_device(): call(opening, [nodes, face_row, face_row, plane], [(2, PLANE, 256), (1, P...  2.23 us
    pallas_call x1, Pallas kernels, per_device(): call(second_coarse, [(24, PLANE), (8, 128)], [grid])  2 us
    pallas_call x1, Pallas kernels, per_device(): call(closing, [stored, stored], [flat, nodes, edge, (2,) + stored], 2, hb...  1.93 us
    pallas_call x1, Pallas kernels, per_device(): call(second_rough, [nodes] * 4 + [(40, PLANE), plane], [flat], in_place={...  1.78 us
  transfers between devices with their start and end apart: 8, of which 2 were waited for; matrix products, arithmetic and copies ran while one was open for 0% of the time, Pallas kernels for 20%

profile of v1, /device:TPU:0, one launch (start us, length us, event | category | flops | bytes accessed | tf_op | source)
XLA Modules:
  0.0 41.8 jit_solution(8721479849047442491)
XLA Ops:
  0.6 2.2 %shard_map.59 = (f32[2,512,128]{2,1,0:T(8,128)S(1)}, f32[2,72,128]{2,1,0:T(8,128)S(1)}, f32[2,72,128]{2,1,0:T(8,128)S(1)}, f32[8,256]{1,0:T(8,128)S(1)}) custom-call(f32[256,512]{1,0:T(8,128)} %forcing_ref.1, f32[1,256]{1,0:T(1,128)} %bitcast.7, s32[1,256]{1,0:T(1,128)} %order_ref.1), custom_call_target="tpu_custom_call" | custom-call | tf_op jit(solution)/shard_map/pallas_call | solution.py:702
  2.9 6.4 %collective-permute-start = (f32[2,72,128]{2,1,0:T(8,128)S(1)}, f32[2,72,128]{2,1,0:T(8,128)S(1)}, u32[]{:S(2)}, u32[]{:S(2)}) collective-permute-start(f32[2,72,128]{2,1,0:T(8,128)S(1)} %get-tuple-element.35), channel_id=1, source_target_pairs={{0,31},{1,2},{2,1},{3,4},{4,3},{5,6},{6,5},{7,8},{8,7},{9,10},{10,... | collective-permute-start | bytes 221192 | tf_op jit(solution)/shard_map/ppermute | solution.py:687
  9.3 0.0 collective-permute-start.1
  9.3 0.9 %shard_map.61 = f32[192,128]{1,0:T(8,128)} custom-call(f32[2,512,128]{2,1,0:T(8,128)S(1)} %get-tuple-element.34.load_ref, f32[8,256]{1,0:T(8,128)S(1)} %get-tuple-element.37.own_ref), custom_call_target="tpu_custom_call" | custom-call | tf_op jit(solution)/shard_map/pallas_call | solution.py:710
  10.2 0.0 copy-start
  10.2 2.7 %all-to-all-start = ((f32[32,3,2,128]{3,2,1,0:T(2,128)}), f32[32,3,2,128]{3,2,1,0:T(2,128)S(1)}, u32[]{:S(2)}, u32[]{:S(2)}) async-start(f32[32,3,2,128]{3,2,1,0:T(2,128)} %bitcast.1), calls=%async_computation | async-start | bytes 196608 | tf_op jit(solution)/shard_map/all_to_all | solution.py:692
  12.9 0.0 collective-permute-done.far_in_ref
  12.9 0.0 collective-permute-done.1.near_in_ref
  12.9 0.0 copy-done
  12.9 1.6 %shard_map.60 = (f32[2,512,128]{2,1,0:T(8,128)S(1)}, f32[2,512,128]{2,1,0:T(8,128)S(1)}, f32[2,512,128]{2,1,0:T(8,128)S(1)}, f32[8,256]{1,0:T(8,128)S(1)}, f32[8...) custom-call(f32[2,512,128]{2,1,0:T(8,128)S(1)} %get-tuple-element.34, ...), custom_call_target="tpu_custom_call", output_to_operand_aliasing={{0}: (0, {})} | custom-call | flops 99999997952 | bytes 268435456 | tf_op jit(solution)/shard_map/pallas_call | solution.py:712
  14.5 0.3 collective-permute-start.2
  14.7 5.3 %collective-permute-start.3 = (f32[2,72,128]{2,1,0:T(8,128)S(1)}, f32[2,72,128]{2,1,0:T(8,128)S(1)}, u32[]{:S(2)}, u32[]{:S(2)}) collective-permute-start(f32[2,72,128]{2,1,0:T(8,128)S(1)} %get-tuple-element.48), channel_id=1, source_target_pairs={{0,31},{1,2},{2,1},{3,4},{4,3},{5,6},{6,5},{7,8},{8,7},{9,10},{10,... | collective-permute-start | bytes 221192 | tf_op jit(solution)/shard_map/ppermute | solution.py:687
  20.1 0.6 %all-to-all-done = f32[32,3,2,128]{3,2,1,0:T(2,128)S(1)} async-done(((f32[32,3,2,128]{3,2,1,0:T(2,128)}), f32[32,3,2,128]{3,2,1,0:T(2,128)S(1)}, u32[]{:S(2)}, u32[]{:S(2)}) %all-to-all-start) | async-done | bytes 98336 | tf_op jit(solution)/shard_map/all_to_all | solution.py:692
  20.7 2.2 %shard_map.62 = (f32[32,256]{1,0:T(8,128)S(1)}, f32[32,256]{1,0:T(8,128)S(1)}, f32[32,256]{1,0:T(8,128)S(1)}, f32[32,256]{1,0:T(8,128)S(1)}, f32[32,256]{1,0:T(8...) custom-call(f32[192,128]{1,0:T(8,128)S(1)} %bitcast.6, f32[8,256]{1,0:T(8,128)S(1)} %get-tuple-element.41.layers_ref), custom_call_target="tpu_custom_call" | custom-call | tf_op jit(solution)/shard_map/pallas_call | solution.py:716
  23.0 0.0 collective-permute-done.2.near_in_ref
  23.0 1.8 %shard_map.63 = (f32[2,512,128]{2,1,0:T(8,128)S(1)}, f32[2,512,128]{2,1,0:T(8,128)S(1)}, f32[2,512,128]{2,1,0:T(8,128)S(1)}, f32[2,512,128]{2,1,0:T(8,128)S(1)},...) custom-call(f32[2,512,128]{2,1,0:T(8,128)S(1)} %get-tuple-element.40.first_ref, ...), custom_call_target="tpu_custom_call", output_to_operand_aliasing={{0}: (0, {}), {1}: (1, {})} | custom-call | tf_op jit(solution)/shard_map/pallas_call | solution.py:719
  24.7 0.0 collective-permute-done.3.far_in_ref
  24.8 1.7 %shard_map.64 = (f32[2,512,128]{2,1,0:T(8,128)S(1)}, f32[2,512,128]{2,1,0:T(8,128)S(1)}, f32[2,512,128]{2,1,0:T(8,128)S(1)}, f32[2,64,128]{2,1,0:T(8,128)S(1)}, ...) custom-call(f32[2,512,128]{2,1,0:T(8,128)S(1)} %get-tuple-element.44.fir, ...), custom_call_target="tpu_custom_call", output_to_operand_aliasing={{0}: (0, {}), {1}: (1, {}), {2}: (2, {})} | custom-call | tf_op jit(solution)/shard_map/pallas_call | solution.py:722
  26.5 3.1 %all-to-all-start.1 = ((f32[32,4,2,128]{3,2,1,0:T(2,128)}), f32[32,4,2,128]{3,2,1,0:T(2,128)S(1)}, u32[]{:S(2)}, u32[]{:S(2)}) async-start(f32[32,4,2,128]{3,2,1,0:T(2,128)} %bitcast.3), calls=%async_computation.1 | async-start | bytes 262144 | tf_op jit(solution)/shard_map/all_to_all | solution.py:692
  29.5 5.3 %collective-permute-start.4 = (f32[2,64,128]{2,1,0:T(8,128)S(1)}, f32[2,64,128]{2,1,0:T(8,128)S(1)}, u32[]{:S(2)}, u32[]{:S(2)}) collective-permute-start(f32[2,64,128]{2,1,0:T(8,128)S(1)} %get-tuple-element.55), channel_id=1, source_target_pairs={{0,31},{1,2},{2,1},{3,4},{4,3},{5,6},{6,5},{7,8},{8,7},{9,10},{10,... | collective-permute-start | bytes 196616 | tf_op jit(solution)/shard_map/ppermute | solution.py:687
  34.8 0.0 collective-permute-start.5
  34.8 3.0 %all-to-all-done.1 = f32[32,4,2,128]{3,2,1,0:T(2,128)S(1)} async-done(((f32[32,4,2,128]{3,2,1,0:T(2,128)}), f32[32,4,2,128]{3,2,1,0:T(2,128)S(1)}, u32[]{:S(2)}, u32[]{:S(2)}) %all-to-all-start.1) | async-done | bytes 131104 | tf_op jit(solution)/shard_map/all_to_all | solution.py:692
  37.8 2.0 %shard_map.65 = (f32[24,256]{1,0:T(8,128)S(1)}, f32[8,128]{1,0:T(8,128)S(1)}) custom-call(f32[32,256]{1,0:T(8,128)S(1)} %get-tuple-element.57.coeff_ref, f32[256,128]{1,0:T(8,128)S(1)} %bitcast.5, f32[32,256]{1,0:T(8,128)S(1)} %get-tuple-element.59.first_ref, f32[32,256]{1,0:T(8,128)S(1)} %get-tuple-element.60.applied_ref, ...), custom_call_target="tpu_custom_call" | custom-call | tf_op jit(solution)/shard_map/pallas_call | solution.py:727
  39.8 0.0 collective-permute-done.4.far_ref
  39.8 0.0 collective-permute-done.5.near_ref
  39.8 1.9 %shard_map.66 = (f32[256,512]{1,0:T(8,128)}, f32[256,512]{1,0:T(8,128)}) custom-call(f32[2,512,128]{2,1,0:T(8,128)S(1)} %get-tuple-element.38.resid_ref, f32[2,512,128]{2,1,0:T(8,128)S(1)} %get-tuple-element.39.scaled_ref, f32[2,512,128]{2,1,0:T(8,128)S(1)} %get-tuple-element.52.image_ref, f32[2,512,128]{2,1,0:T(8,128)S(1)} %get-tuple-element.53.scaled_change_ref, ...), custom_call_target="tpu_custom_call" | custom-call | tf_op jit(solution)/shard_map/pallas_call | solution.py:728
Async XLA Ops:
  2.9 10.0 %collective-permute-start = (f32[2,72,128]{2,1,0:T(8,128)S(1)}, f32[2,72,128]{2,1,0:T(8,128)S(1)}, u32[]{:S(2)}, u32[]{:S(2)}) collective-permute-start(f32[2,72,128]{2,1,0:T(8,128)S(1)} %get-tuple-element.35), channel_id=1, source_target_pairs={{0,31},{1,2},{2,1},{3,4},{4,3},{5,6},{6,5},{7,8},{8,7},{9,10},{10,... | collective-permute-start | bytes 221192 | tf_op jit(solution)/shard_map/ppermute | solution.py:687
  9.3 3.6 %collective-permute-start.1 = (f32[2,72,128]{2,1,0:T(8,128)S(1)}, f32[2,72,128]{2,1,0:T(8,128)S(1)}, u32[]{:S(2)}, u32[]{:S(2)}) collective-permute-start(f32[2,72,128]{2,1,0:T(8,128)S(1)} %get-tuple-element.36), channel_id=1, source_target_pairs={{0,1},{1,0},{2,3},{3,2},{4,5},{5,4},{6,7},{7,6},{8,9},{9,8},{10,11... | collective-permute-start | bytes 221192 | tf_op jit(solution)/shard_map/ppermute | solution.py:687
  10.2 2.7 %copy-start = (f32[64,128]{1,0:T(8,128)S(1)}, f32[64,128]{1,0:T(8,128)}, u32[]{:S(2)}) copy-start(f32[64,128]{1,0:T(8,128)} %constant.2.clone.table_ref) | copy-start | bytes 98308
  10.2 10.5 %all-to-all-start = ((f32[32,3,2,128]{3,2,1,0:T(2,128)}), f32[32,3,2,128]{3,2,1,0:T(2,128)S(1)}, u32[]{:S(2)}, u32[]{:S(2)}) async-start(f32[32,3,2,128]{3,2,1,0:T(2,128)} %bitcast.1), calls=%async_computation | async-start | bytes 196608 | tf_op jit(solution)/shard_map/all_to_all | solution.py:692
  14.5 8.5 %collective-permute-start.2 = (f32[2,72,128]{2,1,0:T(8,128)S(1)}, f32[2,72,128]{2,1,0:T(8,128)S(1)}, u32[]{:S(2)}, u32[]{:S(2)}) collective-permute-start(f32[2,72,128]{2,1,0:T(8,128)S(1)} %get-tuple-element.43), channel_id=1, source_target_pairs={{0,1},{1,0},{2,3},{3,2},{4,5},{5,4},{6,7},{7,6},{8,9},{9,8},{10,11... | collective-permute-start | bytes 221192 | tf_op jit(solution)/shard_map/ppermute | solution.py:687
  14.7 10.0 %collective-permute-start.3 = (f32[2,72,128]{2,1,0:T(8,128)S(1)}, f32[2,72,128]{2,1,0:T(8,128)S(1)}, u32[]{:S(2)}, u32[]{:S(2)}) collective-permute-start(f32[2,72,128]{2,1,0:T(8,128)S(1)} %get-tuple-element.48), channel_id=1, source_target_pairs={{0,31},{1,2},{2,1},{3,4},{4,3},{5,6},{6,5},{7,8},{8,7},{9,10},{10,... | collective-permute-start | bytes 221192 | tf_op jit(solution)/shard_map/ppermute | solution.py:687
  26.5 11.3 %all-to-all-start.1 = ((f32[32,4,2,128]{3,2,1,0:T(2,128)}), f32[32,4,2,128]{3,2,1,0:T(2,128)S(1)}, u32[]{:S(2)}, u32[]{:S(2)}) async-start(f32[32,4,2,128]{3,2,1,0:T(2,128)} %bitcast.3), calls=%async_computation.1 | async-start | bytes 262144 | tf_op jit(solution)/shard_map/all_to_all | solution.py:692
  29.5 10.3 %collective-permute-start.4 = (f32[2,64,128]{2,1,0:T(8,128)S(1)}, f32[2,64,128]{2,1,0:T(8,128)S(1)}, u32[]{:S(2)}, u32[]{:S(2)}) collective-permute-start(f32[2,64,128]{2,1,0:T(8,128)S(1)} %get-tuple-element.55), channel_id=1, source_target_pairs={{0,31},{1,2},{2,1},{3,4},{4,3},{5,6},{6,5},{7,8},{8,7},{9,10},{10,... | collective-permute-start | bytes 196616 | tf_op jit(solution)/shard_map/ppermute | solution.py:687
  34.8 5.0 %collective-permute-start.5 = (f32[2,64,128]{2,1,0:T(8,128)S(1)}, f32[2,64,128]{2,1,0:T(8,128)S(1)}, u32[]{:S(2)}, u32[]{:S(2)}) collective-permute-start(f32[2,64,128]{2,1,0:T(8,128)S(1)} %get-tuple-element.56), channel_id=1, source_target_pairs={{0,1},{1,0},{2,3},{3,2},{4,5},{5,4},{6,7},{7,6},{8,9},{9,8},{10,11... | collective-permute-start | bytes 196616 | tf_op jit(solution)/shard_map/ppermute | solution.py:687

commit v2 on v1

--- a/solution.py
+++ b/solution.py
@@ -3,6 +3,7 @@
 
 import jax
 import jax.numpy as jnp
+import ml_dtypes
 import numpy as np
 from jax import lax
 from jax.experimental import pallas as pl
@@ -73,6 +74,9 @@
 ENDS = np.array([2.0] + [1.0] * 6 + [2.0])
 MASS = np.diag(WEIGHTS)
 STIFF_XY = np.tile(np.kron(MASS, STIFF) + np.kron(STIFF, MASS), (1, 2))
+STIFF_PARTS = []
+for part in range(3):
+    STIFF_PARTS.append((STIFF_XY - sum(STIFF_PARTS)).astype(ml_dtypes.bfloat16).astype(np.float64))
 INTERP = np.stack([(1.0 - POINTS) / 2.0, (1.0 + POINTS) / 2.0], 1)
 LINE_MASS = INTERP.T @ (WEIGHTS[:, None] * INTERP)
 LINE_STIFF = INTERP.T @ STIFF @ INTERP
@@ -110,6 +114,14 @@
     return pltpu.roll(v, EX, 1)
 
 
+def next_xy(v):
+    return jnp.where(lane(v.shape) % EX == EX - 1, pltpu.roll(v, PLANE - 1, 1), pltpu.roll(v, PLANE - EX - 1, 1))
+
+
+def prev_xy(v):
+    return jnp.where(lane(v.shape) % EX == 0, pltpu.roll(v, 1, 1), pltpu.roll(v, EX + 1, 1))
+
+
 def next_z(v):
     half = v.shape[0] // 2
     return jnp.concatenate([v[half:], pltpu.roll(v[:half], half - 1, 0)], axis=0)
@@ -159,23 +171,33 @@
         put(ref, rows_of(nz, 0), prev_y(shared))
 
 
-def restrict(ref, points, inv_ends):
+def restrict(ref, points):
     sums_z, difs_z = [], []
     for ny in range(8):
         tiles = [get(ref, rows_of(nz, ny)) for nz in range(8)]
         sums_z.append(functools.reduce(lambda a, b: a + b, tiles))
         difs_z.append(sum(float(POINTS[7 - k]) * (tiles[7 - k] - tiles[k]) for k in range(4)))
-    return restrict_xy(sums_z, difs_z, points, inv_ends)
-
-
-def restrict_xy(sums_z, difs_z, points, inv_ends):
+    return restrict_xy(sums_z, difs_z, points)
+
+
+def restrict_summed(ref, points):
+    inv_ends = column(1.0 / ENDS)
+    sums_z, difs_z = [], []
+    for ny in range(8):
+        tiles = [get(ref, rows_of(nz, ny)) for nz in range(8)]
+        share = inv_ends * float(1.0 / ENDS[ny])
+        sums_z.append(functools.reduce(lambda a, b: a + b, tiles) * share)
+        difs_z.append(sum(float(POINTS[7 - k]) * (tiles[7 - k] - tiles[k]) for k in range(4)) * share)
+    return restrict_xy(sums_z, difs_z, points)
+
+
+def restrict_xy(sums_z, difs_z, points):
     planes = []
     for parts in (sums_z, difs_z):
-        parts = [part * float(1.0 / ENDS[ny]) for ny, part in enumerate(parts)]
         total = functools.reduce(lambda a, b: a + b, parts)
         slope = sum(float(POINTS[7 - k]) * (parts[7 - k] - parts[k]) for k in range(4))
         in_y = []
-        for part in (total * inv_ends, slope * inv_ends):
+        for part in (total, slope):
             flat = jnp.sum(part, axis=0, keepdims=True)
             steep = jnp.sum(part * points, axis=0, keepdims=True)
             in_y.append((flat - steep) + prev_x(flat + steep))
@@ -207,17 +229,18 @@
 
 
 def coarse_apply(vert, modes):
-    in_x = both(vert, next_x)
-    back_x = []
+    after_x, after_y, after_xy = next_x(vert), next_y(vert), next_xy(vert)
+    in_x = [(after_x + vert, after_xy + after_y), (after_x - vert, after_xy - after_y)]
+    back = []
     for jx in range(2):
-        in_y = both(in_x[jx], next_y)
-        back_y = []
-        for jy in range(2):
-            in_z = both(in_y[jy], next_z)
+        first, second = in_x[jx]
+        for jy, in_y in enumerate((second + first, second - first)):
+            in_z = both(in_y, next_z)
             scaled = [modes[jx + jy + jz] * in_z[jz] for jz in range(2)]
-            back_y.append(both_back(scaled[0], scaled[1], prev_z))
-        back_x.append(both_back(back_y[0], back_y[1], prev_y))
-    return both_back(back_x[0], back_x[1], prev_x)
+            back.append(both_back(scaled[0], scaled[1], prev_z))
+    ss, sd, ds, dd = back
+    low, high = (ss - sd, ss + sd), (ds - dd, ds + dd)
+    return ((low[0] - high[0]) + prev_x(low[0] + high[0])) + (prev_y(low[1] - high[1]) + prev_xy(low[1] + high[1]))
 
 
 def coarse_solve(target, modes, scale):
@@ -227,26 +250,25 @@
     return vert
 
 
+def gathered_rows(ref, row, size):
+    chips = ref.shape[0] // (2 * size)
+    return jnp.concatenate([ref[pl.ds(core * size + row, chips, stride=2 * size), :] for core in range(2)], axis=0)
+
+
 def gathered(ref, k, size):
-    chips = ref.shape[0] // (4 * size)
-    parts = []
-    for core in range(2):
-        rows = [ref[pl.ds((core * size + k) * 2 + h, chips, stride=4 * size), :] for h in range(2)]
-        parts.append(jnp.concatenate(rows, axis=1))
-    return jnp.concatenate(parts, axis=0)
+    return jnp.concatenate([gathered_rows(ref, 2 * k + h, size) for h in range(2)], axis=1)
 
 
 def halves(row):
     return [row[:, :128], row[:, 128:]]
 
 
-def send(ref, planes):
-    block = jnp.concatenate([half for plane in planes for half in halves(plane)], axis=0)
-    rows = block.shape[0]
-    times = 8 // math.gcd(rows, 8)
-    block = jnp.concatenate([block] * times, axis=0)
-    for k in range(0, ref.shape[0], rows * times):
-        ref[k : k + rows * times, :] = block
+def send(ref, rows):
+    count = len(rows)
+    times = 8 // math.gcd(count, 8)
+    block = jnp.concatenate(rows * times, axis=0)
+    for k in range(0, ref.shape[0], count * times):
+        ref[k : k + count * times, :] = block
 
 
 def layer_modes(vert_ref, shift):
@@ -304,15 +326,23 @@
     return 0 if node == 0 else (2 if node == 7 else 1)
 
 
+def product(tables, values):
+    low, middle, high = pieces(values)
+
+    def dot(k, right):
+        return jnp.dot(tables[k], right, preferred_element_type=F32)
+
+    return dot(0, high) + ((dot(0, middle) + dot(1, high)) + (dot(1, middle) + (dot(0, low) + dot(2, high))))
+
+
 def operate(z_ref, xy_ref, out_ref, table_ref, coeff, weight_x):
-    table = jnp.tile(table_ref[...], (4, 2))
-    row, col = (lax.broadcasted_iota(jnp.int32, table.shape, axis) for axis in range(2))
-    table = jnp.where(row // 64 == col // 64, table, 0.0)
+    row, col = (lax.broadcasted_iota(jnp.int32, (256, 256), axis) for axis in range(2))
+    tables = [
+        jnp.where(row // 64 == col // 64, jnp.tile(table_ref[k].astype(F32), (4, 2)), 0.0).astype(jnp.bfloat16) for k in range(3)
+    ]
     for half in range(2):
         rows = slice(half * 256, half * 256 + 256)
-        xy_ref[rows, :] = jnp.dot(
-            table, get(z_ref, rows), precision=lax.Precision.HIGHEST, preferred_element_type=F32
-        )
+        xy_ref[rows, :] = product(tables, get(z_ref, rows))
     for ny in range(8):
         tiles = [get(z_ref, rows_of(nz, ny)) for nz in range(8)]
         even = [tiles[k] + tiles[7 - k] for k in range(4)]
@@ -348,15 +378,17 @@
 
 
 def faces_out(ref, near_ref, far_ref):
-    near, far = face_rows(ref)
-    near_ref[:, 0:64, :] = ref[:, near, :]
-    far_ref[:, 0:64, :] = ref[:, far, :]
+    for rows, out_ref in zip(face_rows(ref), (near_ref, far_ref)):
+        out_ref[:, 0:56, :] = ref[:, pl.ds(rows.start, 56), :]
+
+
+def face_in(ref):
+    return jnp.concatenate([get(ref, slice(0, 56)), next_y(get(ref, slice(0, 8)))], axis=0)
 
 
 def faces_in(ref, near_ref, far_ref):
-    near, far = face_rows(ref)
-    ref[:, near, :] += near_ref[:, 0:64, :]
-    ref[:, far, :] += far_ref[:, 0:64, :]
+    for rows, in_ref in zip(face_rows(ref), (near_ref, far_ref)):
+        put(ref, rows, get(ref, rows) + face_in(in_ref))
 
 
 def columns_of_nodes():
@@ -377,7 +409,8 @@
 
 
 def opening(
-    forcing_ref, kappa_ref, order_ref, load_ref, far_ref, near_ref, own_ref, held, held_kappa, held_order, sems
+    forcing_ref, kappa_ref, order_ref, load_ref, far_ref, near_ref, own_ref, payload_ref,
+    held, held_kappa, held_order, held_payload, sems,
 ):
     small = [
         pltpu.make_async_copy(order_ref, held_order, sems.at[0]),
@@ -405,13 +438,31 @@
         put(load_ref, slice(256 * k, 256 * k + 256), load.T)
     sum_xy(load_ref)
     faces_out(load_ref, near_ref, far_ref)
-    put(near_ref, slice(64, 72), own)
-    put(far_ref, slice(64, 72), own)
-
-
-def opening_payload(load_ref, own_ref, payload_ref):
-    lower, upper = restrict(load_ref, column(POINTS), column(1.0 / ENDS))
-    send(payload_ref, [lower, upper, own_ref[0:1, :]])
+    put(near_ref, slice(56, 64), own)
+    put(far_ref, slice(56, 64), own)
+
+
+    @pl.when(starts_early())
+    def _():
+        write_payload(load_ref, own_ref, payload_ref, held_payload, sems.at[4])
+
+
+def starts_early():
+    return my_layer() < lax.axis_size("elem") * lax.axis_size("face") // 2
+
+
+def write_payload(load_ref, own_ref, payload_ref, held, sem):
+    lower, upper = restrict_summed(load_ref, column(POINTS))
+    send(held, halves(lower) + halves(upper) + halves(own_ref[0:1, :]))
+    copy = pltpu.make_async_copy(held, payload_ref, sem)
+    copy.start()
+    copy.wait()
+
+
+def late_payload(load_ref, own_ref, _, payload_ref, held, sems):
+    @pl.when(jnp.logical_not(starts_early()))
+    def _():
+        write_payload(load_ref, own_ref, payload_ref, held, sems.at[0])
 
 
 def below_above(near, far):
@@ -420,7 +471,7 @@
 
 
 def row_after_face(ref):
-    return get(ref, slice(64, 72))[0:1]
+    return get(ref, slice(56, 64))[0:1]
 
 
 def first_faces(
@@ -435,12 +486,12 @@
     faces_in(resid_ref, near_in_ref, far_in_ref)
     over_diag(functools.partial(get, resid_ref), scaled_ref, layers_ref)
     operate(scaled_ref, xy_ref, image_ref, table_ref, own, weight_x)
+    lower, upper = restrict(image_ref, points)
     sum_xy(image_ref)
     faces_out(image_ref, near_ref, far_ref)
-    lower, upper = restrict(image_ref, points, column(1.0 / ENDS))
     lower_ref[...] = jnp.broadcast_to(lower, lower_ref.shape)
-    put(near_ref, slice(64, 72), jnp.broadcast_to(upper, (8, PLANE)))
-    put(far_ref, slice(64, 72), jnp.broadcast_to(upper, (8, PLANE)))
+    put(near_ref, slice(56, 64), jnp.broadcast_to(upper, (8, PLANE)))
+    put(far_ref, slice(56, 64), jnp.broadcast_to(upper, (8, PLANE)))
 
 
 def over_diag(resid, scaled_ref, layers_ref):
@@ -475,122 +526,173 @@
     out_ref[:, 448:512, :] += edge_ref[:, 64:128, :]
 
 
-def first_coarse(
-    coarse_ref, layers_ref, vert_ref, applied_ref, target_ref, scale_ref, coeff_ref, choose_ref, smooth_ref, edge_ref
-):
-    coeff = gathered(coarse_ref, 2, 3)
+def first_coarse(coarse_ref, layers_ref, vert_ref, target_ref, scale_ref, coeff_ref, smooth_ref, edge_ref):
+    coeff = gathered(coarse_ref, 2, 6)
     coeff_ref[...] = coeff
-    choose_ref[...] = selection(layers_ref[3:4, :]).astype(F32).T.astype(jnp.bfloat16)
     modes, scale = coarse_tables(coeff)
-    target = gathered(coarse_ref, 0, 3) + prev_z(gathered(coarse_ref, 1, 3))
+    target = gathered(coarse_ref, 0, 6) + prev_z(gathered(coarse_ref, 1, 6))
     vert = coarse_solve(target, modes, scale)
     vert_ref[...] = vert
-    applied_ref[...] = coarse_apply(vert, modes)
     target_ref[...] = target
     scale_ref[...] = scale
     smooth_image(smooths_of(three_modes(vert_ref), layers_ref), smooth_ref, edge_ref)
 
 
 def pack(sums):
-    rows = [jnp.sum(t, axis=0, keepdims=True) for t in sums]
-    rows = jnp.concatenate(rows + [jnp.zeros((1, PLANE), F32)] * (8 - len(rows)), axis=0)
-    for by in (128, 64, 32):
-        rows = rows + pltpu.roll(rows, by, 1)
-    place = lax.broadcasted_iota(jnp.int32, rows.shape, 0)
-    return jnp.sum(jnp.where(lane(rows.shape) // 32 == place, rows, 0.0), axis=0, keepdims=True)
+    place = lane((8, 128)) // 16
+    packed = jnp.zeros((8, 128), F32)
+    for k, total in enumerate(sums):
+        total = total[:, :128] + total[:, 128:]
+        for by in (64, 32, 16):
+            total = total + pltpu.roll(total, by, 1)
+        packed = jnp.where(place == k, total, packed)
+    return jnp.sum(packed, axis=0, keepdims=True)
 
 
 def second_rough(
-    first_ref, smooth_ref, near_in_ref, layers_ref, table_ref, resid_ref, scaled_ref,
-    image_ref, whole_ref, scaled_change_ref, change_ref, sums_ref, planes_ref, xy_ref,
+    image_ref, smooth_ref, layers_ref, table_ref, resid_ref, scaled_ref,
+    scaled_change_ref, change_ref, sums_ref, planes_ref, column_ref, outer_ref, xy_ref, whole_ref,
 ):
     points, weight_x, _, _ = columns_of_nodes()
     inv_ends = column(1.0 / ENDS)
-    image_ref[...] = first_ref[...]
-    near, _ = face_rows(image_ref)
-    image_ref[:, near, :] += near_in_ref[:, 0:64, :]
     whole_ref[...] = image_ref[...] + smooth_ref[...]
     over_diag(functools.partial(get, whole_ref), scaled_change_ref, layers_ref)
     operate(scaled_change_ref, xy_ref, change_ref, table_ref, layers_ref[0:1, :], weight_x)
+    planes_ref[...] = jnp.concatenate(list(restrict(change_ref, points)) * 4, axis=0)
     sum_xy(change_ref)
-    sums = [jnp.zeros((8, PLANE), F32)] * 5
-    for nz in range(8):
-        for ny in range(8):
+    sums = [jnp.zeros((8, PLANE), F32)] * 6
+    for ny in range(8):
+        along = [jnp.zeros((8, PLANE), F32)] * 2
+        for nz in range(8):
             rows = rows_of(nz, ny)
             share = float(1.0 / (ENDS[nz] * ENDS[ny]))
-            scaled, scaled_change = get(scaled_ref, rows) * share, get(scaled_change_ref, rows) * share
+            scaled, change = get(scaled_ref, rows) * share, get(scaled_change_ref, rows)
+            along = [total + float(STIFF[nz, node]) * change for total, node in zip(along, (0, 7))]
+            change = change * share
             whole, image = get(whole_ref, rows), get(image_ref, rows)
             terms = [
-                scaled * get(resid_ref, rows), scaled * whole, scaled_change * whole, scaled * image, scaled_change * image
+                scaled * get(resid_ref, rows), scaled * whole, change * whole, scaled * image, change * image,
+                change * (get(change_ref, rows) * float(ENDS[nz])),
             ]
             sums = [total + term for total, term in zip(sums, terms)]
-    sums_ref[...] = jnp.concatenate(sums, axis=0)
-    planes_ref[...] = jnp.concatenate(list(restrict(change_ref, points, inv_ends)) * 4, axis=0)
+        for k in range(2):
+            column_ref[64 * k + 8 * ny : 64 * k + 8 * ny + 8, :] = along[k]
+    sums_ref[...] = jnp.concatenate([total * inv_ends for total in sums], axis=0)
+    for k, rows in enumerate((slice(0, 64), slice(448, 512))):
+        outer_ref[64 * k : 64 * k + 64, :] = get(whole_ref, rows)
 
 
 def second_faces(
-    first_ref, first_scaled_ref, first_change_ref, whole_ref, far_in_ref, near_in_ref, layers_ref, table_ref,
-    scaled_ref, lower_ref, sums_ref, planes_ref,
-    image_ref, scaled_change_ref, change_ref, far_ref, near_ref, payload_ref, edge_ref, xy_ref,
+    image_ref, scaled_change_ref, change_ref, outer_ref, far_in_ref, near_in_ref, layers_ref, table_ref,
+    scaled_ref, lower_ref, sums_ref, planes_ref, column_ref,
+    added_ref, far_ref, near_ref, payload_ref, edge_ref, xy_ref,
 ):
-    points, weight_x, diag_x, ends_x = columns_of_nodes()
+    points, weight_x, _, _ = columns_of_nodes()
     inv_ends = column(1.0 / ENDS)
-    for out_ref, ref in (
-        (image_ref, first_ref), (scaled_change_ref, first_scaled_ref), (change_ref, first_change_ref)
-    ):
-        out_ref[...] = ref[...]
     even = lax.rem(my_layer(), 2) == 0
     own = layers_ref[0:1, :]
-    beyond = jnp.where(even, layers_ref[1:2, :], layers_ref[2:3, :])
-    kappas = kappa_sums(own, beyond, beyond)
-    _, far = face_rows(image_ref)
-    sums = [sums_ref[8 * k : 8 * k + 8, :] for k in range(5)]
-    s_plane, q_plane, i_plane, w_plane = (
-        get(ref, far) for ref in (scaled_ref, scaled_change_ref, image_ref, whole_ref)
+    kappas = kappa_sums(*(layers_ref[k : k + 1, :] for k in range(3)))
+    faces = below_above(face_in(near_in_ref), face_in(far_in_ref))
+    tiles = [slice(8 * ny, 8 * ny + 8) for ny in range(8)]
+    added = added_by(faces, kappas, columns_of_nodes())
+    small_tables = [table_ref[k, :, 0:64] for k in range(3)]
+    xy_ref[...] = product(small_tables, jnp.concatenate(added, axis=1))
+    along, at_face = [], []
+    for k in range(2):
+        along.append(local_along(own, weight_x, added[k]))
+        flux = own * xy_ref[:, PLANE * k : PLANE * k + PLANE]
+        at_face.append(float(WEIGHTS[0]) * jnp.concatenate(
+            [flux[t] + (float(REACT * WEIGHTS[ny]) * weight_x) * added[k][t] for ny, t in enumerate(tiles)], axis=0
+        ))
+    local = [
+        (float(STIFF[nz, 0]) * along[0] + float(STIFF[nz, 7]) * along[1]) + at_face[k] for k, nz in enumerate((0, 7))
+    ]
+    flat = at_face[0] + at_face[1]
+    slope = (along[1] + at_face[1]) - (along[0] + at_face[0])
+    lower, upper = restrict_xy([flat[t] for t in tiles], [slope[t] for t in tiles], points)
+    lower, upper = lower + planes_ref[0:1, :], upper + planes_ref[1:2, :]
+    sums = [jnp.zeros((8, PLANE), F32)] * 5
+    energy = jnp.zeros((8, PLANE), F32)
+    planes = [slice(0, 64), slice(448, 512)]
+    for k in range(2):
+        s_plane, q_plane, i_plane, c_plane = (
+            get(ref, planes[k]) for ref in (scaled_ref, scaled_change_ref, image_ref, change_ref)
+        )
+        w_plane = outer_ref[64 * k : 64 * k + 64, :]
+        for ny in range(8):
+            tile = tiles[ny]
+            share = float(1.0 / ENDS[ny])
+            half = share * float(1.0 / ENDS[0])
+            face = faces[k][tile]
+            s, q, dq = s_plane[tile] * half, q_plane[tile] * half, added[k][tile] * half
+            sums[0] = sums[0] + s * face
+            sums[1] = sums[1] + (q * face + dq * (w_plane[tile] + face))
+            sums[2] = sums[2] + s * face
+            sums[3] = sums[3] + (q * face + dq * (i_plane[tile] + face))
+            sums[4] = sums[4] + (added[k][tile] * c_plane[tile]) * share
+            energy = energy + (
+                column_ref[64 * k + 8 * ny : 64 * k + 8 * ny + 8, :] * along[k][tile]
+                + q_plane[tile] * at_face[k][tile]
+                + added[k][tile] * local[k][tile]
+            )
+    sums = [sums_ref[8 * k + 8 : 8 * k + 16, :] + sums[k] * inv_ends for k in range(5)]
+    sums = pack([sums_ref[0:8, :]] + sums[:4] + [sums[4] + energy])
+    below, _ = below_above(row_after_face(near_in_ref), row_after_face(far_in_ref))
+    send(payload_ref, halves(lower_ref[0:1, :] + below) + halves(lower) + halves(upper) + [sums])
+    for k in range(2):
+        put(edge_ref, slice(64 * k, 64 * k + 64), local[k])
+        added_ref[64 * k : 64 * k + 64, :] = at_face[k]
+    sum_xy(edge_ref)
+    change = [(get(change_ref, planes[k]) + get(edge_ref, slice(64 * k, 64 * k + 64)))[0:56] for k in range(2)]
+    put(far_ref, slice(0, 56), jnp.where(even, change[0], change[1]))
+    put(near_ref, slice(0, 56), jnp.where(even, change[1], change[0]))
+
+
+def local_along(own, weight_x, added):
+    return own * jnp.concatenate(
+        [(weight_x * float(WEIGHTS[ny])) * added[8 * ny : 8 * ny + 8] for ny in range(8)], axis=0
     )
-    added = []
-    for ny in range(8):
-        tile = slice(8 * ny, 8 * ny + 8)
-        face = get(far_in_ref, tile)
-        dq = face / fine_diag(kappas, 0, ny, weight_x, diag_x, ends_x)
-        added.append(dq)
-        share = float(1.0 / (ENDS[0] * ENDS[ny]))
-        s, q, image, whole = s_plane[tile] * share, q_plane[tile] * share, i_plane[tile], w_plane[tile]
-        dq = dq * share
-        sums[1] = sums[1] + s * face
-        sums[2] = sums[2] + (q * face + dq * (whole + face))
-        sums[3] = sums[3] + s * face
-        sums[4] = sums[4] + (q * face + dq * (image + face))
-    plane = jnp.concatenate(added, axis=0)
-    put(image_ref, far, i_plane + get(far_in_ref, slice(0, 64)))
-    put(scaled_change_ref, far, q_plane + plane)
-    xy_ref[...] = jnp.dot(
-        table_ref[:, 0:64], plane, precision=lax.Precision.HIGHEST, preferred_element_type=F32
-    )
-    for ny in range(8):
-        area = weight_x * float(WEIGHTS[ny])
-        put(edge_ref, rows_of(0, ny), own * area * added[ny])
-        flux = own * xy_ref[8 * ny : 8 * ny + 8, :] + (float(REACT) * area) * added[ny]
-        put(edge_ref, rows_of(1, ny), float(WEIGHTS[0]) * flux)
+
+
+def added_by(faces, kappas, columns):
+    _, weight_x, diag_x, ends_x = columns
+    return [
+        jnp.concatenate(
+            [
+                face[8 * ny : 8 * ny + 8] / fine_diag(kappas, nz, ny, weight_x, diag_x, ends_x)
+                for ny in range(8)
+            ],
+            axis=0,
+        )
+        for nz, face in zip((0, 7), faces)
+    ]
+
+
+def complete(
+    first_ref, first_scaled_ref, first_change_ref, far_in_ref, near_in_ref, at_face_ref, layers_ref, coeff_ref, vert_ref,
+    image_ref, scaled_change_ref, change_ref, choose_ref, applied_ref, modes_ref, edge_ref,
+):
+    columns = columns_of_nodes()
+    applied_ref[...] = coarse_apply(vert_ref[...], coarse_modes(coeff_ref[...]))
+    modes_ref[...] = three_modes(vert_ref)
+    choose_ref[...] = selection(layers_ref[3:4, :]).astype(F32).T.astype(jnp.bfloat16)
+    image_ref[...] = first_ref[...]
+    scaled_change_ref[...] = first_scaled_ref[...]
+    faces_in(image_ref, near_in_ref, far_in_ref)
+    kappas = kappa_sums(*(layers_ref[k : k + 1, :] for k in range(3)))
+    added = added_by(below_above(face_in(near_in_ref), face_in(far_in_ref)), kappas, columns)
+    for k, rows in enumerate((slice(0, 64), slice(448, 512))):
+        put(scaled_change_ref, rows, get(scaled_change_ref, rows) + added[k])
+        put(edge_ref, slice(64 * k, 64 * k + 64), local_along(layers_ref[0:1, :], columns[1], added[k]))
+        put(edge_ref, slice(128 + 64 * k, 192 + 64 * k), at_face_ref[64 * k : 64 * k + 64, :])
     sum_xy(edge_ref)
-    put(change_ref, far, get(change_ref, far) + get(edge_ref, slice(64, 128)))
-    energy = jnp.zeros((8, PLANE), F32)
+    along = [get(edge_ref, slice(64 * k, 64 * k + 64)) for k in range(2)]
     for nz in range(8):
-        factor = jnp.where(even, float(STIFF[nz, 0]), float(STIFF[nz, 7]))
-        for ny in range(8):
-            rows = rows_of(nz, ny)
-            change = get(change_ref, rows) + factor * get(edge_ref, rows_of(0, ny))
-            put(change_ref, rows, change)
-            energy = energy + (get(scaled_change_ref, rows) * change) * float(1.0 / ENDS[ny])
-    faces_out(change_ref, near_ref, far_ref)
-    sign = jnp.where(even, -1.0, 1.0)
-    along = [get(edge_ref, rows_of(0, ny)) for ny in range(8)]
-    at_face = [get(edge_ref, rows_of(1, ny)) for ny in range(8)]
-    lower, upper = restrict_xy(at_face, [sign * (a + b) for a, b in zip(along, at_face)], points, inv_ends)
-    lower, upper = lower + planes_ref[0:1, :], upper + planes_ref[1:2, :]
-    below, _ = below_above(row_after_face(near_in_ref), row_after_face(far_in_ref))
-    sums = pack([total * inv_ends for total in sums + [energy]])
-    send(payload_ref, [lower_ref[0:1, :] + below, lower, upper, sums])
+        rows = slice(64 * nz, 64 * nz + 64)
+        new = get(first_change_ref, rows) + (float(STIFF[nz, 0]) * along[0] + float(STIFF[nz, 7]) * along[1])
+        if nz in (0, 7):
+            new = new + get(edge_ref, slice(128 + 64 * (nz // 7), 192 + 64 * (nz // 7)))
+        put(change_ref, rows, new)
 
 
 def folded(value):
@@ -598,41 +700,43 @@
 
 
 def second_coarse(
-    coeff_ref, step_ref, first_ref, applied_ref, target_ref, scale_ref, modes_ref, scalars_ref, vert_ref
+    coeff_ref, step_ref, first_ref, applied_ref, target_ref, scale_ref, first_modes_ref, modes_ref, scalars_ref, vert_ref
 ):
     modes = coarse_modes(coeff_ref[...])
     target, first, applied = target_ref[...], first_ref[...], applied_ref[...]
-    rough, rough_change = gathered(step_ref, 0, 4), gathered(step_ref, 1, 4) + prev_z(gathered(step_ref, 2, 4))
-    parts = folded(gathered(step_ref, 3, 4))
-    sums = [parts] + [pltpu.roll(parts, PLANE - 32 * k, 1) for k in range(1, 6)]
-    used = lane(parts.shape) < 32
+    rough, rough_change = gathered(step_ref, 0, 7), gathered(step_ref, 1, 7) + prev_z(gathered(step_ref, 2, 7))
+    parts = folded(gathered_rows(step_ref, 6, 7))
+    sums = [parts] + [pltpu.roll(parts, 128 - 16 * k, 1) for k in range(1, 6)]
+    used = lane(parts.shape) < 16
 
     def total(fine, coarse):
-        return jnp.sum(jnp.where(used, fine, 0.0) + folded(coarse), keepdims=True)
-
+        coarse = folded(coarse)
+        return jnp.sum(jnp.where(used, fine, 0.0) + (coarse[:, :128] + coarse[:, 128:]), keepdims=True)
+
+    image = rough + applied
+    change = coarse_solve(image, modes, scale_ref[...])
+    vert_ref[...] = change
+    change_modes = three_modes(vert_ref)
+    change_applied = coarse_apply(change, modes)
     gamma = total(sums[0], target * first)
     energy = total(sums[3], first * (2.0 * rough + applied))
     alpha = gamma / energy
-    change = rough + applied
-    target = target - alpha * change
-    vert = coarse_solve(target, modes, scale_ref[...])
-    progress = total(sums[0] - alpha * (2.0 * sums[1] - alpha * sums[2]), target * vert)
+    vert = first - alpha * change
+    progress = total(sums[0] - alpha * (2.0 * sums[1] - alpha * sums[2]), (target - alpha * image) * vert)
     second = total(
         sums[3] - alpha * (2.0 * sums[4] - alpha * sums[5]),
-        vert * (2.0 * (rough - alpha * rough_change) + coarse_apply(vert, modes)),
+        vert * (2.0 * (rough - alpha * rough_change) + (applied - alpha * change_applied)),
     )
-    cross = total(sums[1] - alpha * sums[2], vert * change)
+    cross = total(sums[1] - alpha * sums[2], vert * image)
     beta = progress / gamma
     alpha_next = progress / (second + beta * (2.0 * cross + beta * energy))
-    share = alpha + alpha_next * beta
-    vert_ref[...] = share * first + alpha_next * vert
-    modes_ref[...] = three_modes(vert_ref)
-    scalars = [share + alpha_next, alpha_next * alpha]
+    scalars = [alpha + alpha_next * beta + alpha_next, alpha_next * alpha]
+    modes_ref[...] = scalars[0] * first_modes_ref[...] - scalars[1] * change_modes
     scalars_ref[...] = jnp.concatenate([jnp.broadcast_to(t, (1, 128)) for t in scalars * 4], axis=0)
 
 
 def to_stored(choose, value):
-    total = jnp.zeros((PLANE, value.shape[0]), F32)
+    total = jnp.zeros((choose.shape[0], value.shape[0]), F32)
     for piece in pieces(value)[1:]:
         total = total + lax.dot_general(choose, piece, (((1,), (1,)), ((), ())), preferred_element_type=F32)
     return total
@@ -651,28 +755,31 @@
             rough = first * get(scaled_ref, rows) - second * get(scaled_change_ref, rows)
             grid_ref[rows, :] = rough + smooths[0].value(nz, ny)
     held[0] = to_stored(choose, grid_ref[...])
-    copies = [pltpu.make_async_copy(held.at[0], solution_ref, sems.at[0])]
-    copies[0].start()
     smooth_image(smooths, sum_ref, edge_ref)
     first, second = first[None], second[None]
     sum_ref[...] = resid_ref[...] - first * image_ref[...] + second * change_ref[...] - sum_ref[...]
-    near, far = face_rows(sum_ref)
-    sum_ref[:, near, :] += second * near_ref[...]
-    sum_ref[:, far, :] += second * far_ref[...]
-    held[1] = to_stored(choose, get(sum_ref, slice(0, 512)))
-    copies.append(pltpu.make_async_copy(held.at[1], residual_ref, sems.at[1]))
-    copies[1].start()
+    for rows, ref in zip(face_rows(sum_ref), (near_ref, far_ref)):
+        put(sum_ref, rows, get(sum_ref, rows) + second[0] * face_in(ref))
+    copies = [pltpu.make_async_copy(held.at[0], solution_ref, sems.at[0])]
+    copies[0].start()
+    for part in range(2):
+        stored = slice(128 * part, 128 * part + 128)
+        held[1, stored, :] = to_stored(choose[stored], get(sum_ref, slice(0, 512)))
+        copies.append(pltpu.make_async_copy(held.at[1, stored], residual_ref.at[stored], sems.at[1 + part]))
+        copies[-1].start()
     for copy in copies:
         copy.wait()
 
 
-def call(kernel, outs, scratch=(), sems=0, hbm_out=False, cost=None, in_place=None, hbm_in=0):
-    spec = pl.BlockSpec(memory_space=pltpu.HBM if hbm_out else pltpu.VMEM)
-    more = {"in_specs": [pl.BlockSpec(memory_space=pltpu.HBM)] * hbm_in} if hbm_in else {}
+def call(kernel, outs, scratch=(), sems=0, cost=None, in_place=None, hbm_in=(), hbm_out=(), inputs=0):
+    def specs(count, far):
+        return [pl.BlockSpec(memory_space=pltpu.HBM if k in far else pltpu.VMEM) for k in range(count)]
+
+    more = {"in_specs": specs(inputs, hbm_in)} if hbm_in else {}
     return pl.pallas_call(
         kernel,
         out_shape=[jax.ShapeDtypeStruct(*(s if isinstance(s[0], tuple) else (s, F32))) for s in outs],
-        out_specs=[spec for _ in outs],
+        out_specs=specs(len(outs), hbm_out),
         scratch_shapes=[pltpu.VMEM(*(s if isinstance(s[0], tuple) else (s, F32))) for s in scratch]
         + ([pltpu.SemaphoreType.DMA((sems,))] if sems else []),
         compiler_params=pltpu.CompilerParams(vmem_limit_bytes=12 * 1024 * 1024),
@@ -687,46 +794,54 @@
     return lax.ppermute(x, AXES, [(i, (i + (1 if (i % 2 == 0) != far else -1)) % size) for i in range(size)])
 
 
-def everyone(payload, size):
+def everyone(payload, shape):
     devices = lax.axis_size(AXES)
-    return lax.all_to_all(payload.reshape(devices, size, 2, 128), AXES, 0, 0, tiled=True).reshape(-1, 128)
+    return lax.all_to_all(payload.reshape((devices,) + shape), AXES, 0, 0, tiled=True).reshape(-1, 128)
 
 
 def per_device(forcing, kappa, elem_order):
     devices = lax.axis_size(AXES)
-    nodes, face, face_row = (2, 512, 128), (2, 64, 128), (2, 72, 128)
+    nodes, face, face_row = (2, 512, 128), (2, 56, 128), (2, 64, 128)
     plane, grid, flat = (8, PLANE), (devices, PLANE), (512, PLANE)
     edge, stored, choice = (2, 128, 128), (PLANE, 512), ((PLANE, PLANE), jnp.bfloat16)
-    table = jnp.asarray(STIFF_XY, F32)
+    table = jnp.asarray(np.stack(STIFF_PARTS), jnp.bfloat16)
     long = pl.CostEstimate(flops=10**11, bytes_accessed=2**28, transcendentals=0)
-    load, far, near, own = call(
+    payload_rows = (devices * 6, 128)
+    load, far, near, own, payload = call(
         opening,
-        [nodes, face_row, face_row, plane],
-        [(2, PLANE, 256), (1, PLANE), ((1, PLANE), jnp.int32)],
-        4,
-        hbm_in=3,
+        [nodes, face_row, face_row, plane, payload_rows],
+        [(2, PLANE, 256), (1, PLANE), ((1, PLANE), jnp.int32), payload_rows],
+        5,
+        hbm_in=(0, 1, 2),
+        hbm_out=(4,),
+        inputs=3,
     )(*(pltpu.with_memory_space_constraint(x, pltpu.HBM) for x in (forcing, kappa.reshape(1, PLANE), elem_order)))
     far, near = swapped(far, True), swapped(near, False)
-    (payload,) = call(opening_payload, [(devices * 6, 128)])(load, own)
-    gather = everyone(payload, 3)
+    (payload,) = call(
+        late_payload, [payload_rows], [payload_rows], 1, in_place={2: 0}, hbm_in=(2,), hbm_out=(0,), inputs=3
+    )(load, own, payload)
+    gather = everyone(payload, (3, 2, 128))
     resid, scaled, image, layers, lower, far, near = call(
         first_faces, [nodes, nodes, nodes, plane, plane, face_row, face_row], [flat], cost=long, in_place={0: 0}
     )(load, far, near, own, table)
     far, near = swapped(far, True), swapped(near, False)
-    vert, applied, target, scale, coeff, choose, smooth = call(first_coarse, [grid] * 5 + [choice, nodes], [edge])(
-        gather, layers
+    vert, target, scale, coeff, smooth = call(first_coarse, [grid] * 4 + [nodes], [edge])(gather, layers)
+    scaled_change, change, sums, planes, column_planes, outer = call(
+        second_rough, [nodes] * 2 + [(48, PLANE), plane, (128, PLANE), (128, PLANE)], [flat, nodes], in_place={1: 0}
+    )(image, smooth, layers, table, resid, scaled)
+    added, next_far, next_near, payload = call(
+        second_faces, [(128, PLANE), face, face, (devices * 7, 128)], [edge, (64, 2 * PLANE)]
+    )(image, scaled_change, change, outer, far, near, layers, table, scaled, lower, sums, planes, column_planes)
+    step = everyone(payload, (7, 1, 128))
+    next_far, next_near = swapped(next_far, True), swapped(next_near, False)
+    image, scaled_change, change, choose, applied, first_modes = call(
+        complete, [nodes] * 3 + [choice, grid, (24, PLANE)], [(2, 256, 128)], in_place={0: 0, 1: 1, 2: 2}
+    )(image, scaled_change, change, far, near, added, layers, coeff, vert)
+    modes, scalars = call(second_coarse, [(24, PLANE), (8, 128)], [grid])(
+        coeff, step, vert, applied, target, scale, first_modes
     )
-    image, whole, scaled_change, change, sums, planes = call(
-        second_rough, [nodes] * 4 + [(40, PLANE), plane], [flat], in_place={0: 0, 1: 1}
-    )(image, smooth, near, layers, table, resid, scaled)
-    image, scaled_change, change, far, near, payload = call(
-        second_faces, [nodes] * 3 + [face, face, (devices * 8, 128)], [edge, (64, PLANE)], in_place={0: 0, 1: 1, 2: 2}
-    )(image, scaled_change, change, whole, far, near, layers, table, scaled, lower, sums, planes)
-    step = everyone(payload, 4)
-    far, near = swapped(far, True), swapped(near, False)
-    modes, scalars = call(second_coarse, [(24, PLANE), (8, 128)], [grid])(coeff, step, vert, applied, target, scale)
-    found, left = call(closing, [stored, stored], [flat, nodes, edge, (2,) + stored], 2, hbm_out=True)(
-        resid, scaled, image, scaled_change, change, far, near, modes, layers, scalars, choose
+    found, left = call(closing, [stored, stored], [flat, nodes, edge, (2,) + stored], 3, hbm_out=(0, 1))(
+        resid, scaled, image, scaled_change, change, next_far, next_near, modes, layers, scalars, choose
     )
     return found, left
 

time: 42.5 us -> 39.6 us (0.932)
  starting transfers between devices: 23.1 us -> 21.8 us
  Pallas kernels: 14.3 us -> 13.5 us
  waiting for transfers between devices: 3.61 us -> 2.97 us
    ppermute x6, starting transfers between devices: 17.3 us -> 16.1 us  [swapped(): lax.ppermute(x, AXES, [(i, (i + (1 if (i % 2 == 0) != far else -1)) % siz...]
    pallas_call x1, Pallas kernels: 2 us -> 1.2 us  [per_device(): call(second_coarse, [(24, PLANE), (8, 128)], [grid])]
    all_to_all x2, waiting for transfers between devices: 3.59 us -> 2.96 us  [everyone(): lax.all_to_all(payload.reshape((devices,) + shape), AXES, 0, 0, tiled=True)]
    pallas_call x6 -> x7, Pallas kernels: 10.8 us -> 11 us  [the longest x1 3.11 us: per_device(): call(opening, [nodes, face_row, face_row, plane, payload_rows], [(2, PLAN...]
  transfers between devices with their start and end apart: 8 -> 8, of which waited for: 2 -> 2; matrix products, arithmetic and copies ran while one was open for 0% -> 0% of each run, Pallas kernels for 20% -> 18%
where the time goes in v2:
time: 39.6 us; the launch traced here: 39 us
  starting transfers between devices  21.8 us (55%)
  Pallas kernels  13.5 us (34%)
  waiting for transfers between devices  2.97 us (8%)
  between operations  0.75 us (2%)
    ppermute x6, starting transfers between devices, swapped(): lax.ppermute(x, AXES, [(i, (i + (1 if (i % 2 == 0) != far else -1)) % siz...  16.1 us
    all_to_all x2, starting transfers between devices, everyone(): lax.all_to_all(payload.reshape((devices,) + shape), AXES, 0, 0, tiled=True)  5.61 us
    pallas_call x1, Pallas kernels, per_device(): call(opening, [nodes, face_row, face_row, plane, payload_rows], [(2, PLAN...  3.11 us
    all_to_all x2, waiting for transfers between devices, everyone(): lax.all_to_all(payload.reshape((devices,) + shape), AXES, 0, 0, tiled=True)  2.96 us
    pallas_call x1, Pallas kernels, per_device(): call(closing, [stored, stored], [flat, nodes, edge, (2,) + stored], 3, hb...  2.01 us
    pallas_call x1, Pallas kernels, per_device(): call(first_coarse, [grid] * 4 + [nodes], [edge])(gather, layers)  1.8 us
    pallas_call x1, Pallas kernels, per_device(): call(second_rough, [nodes] * 2 + [(48, PLANE), plane, (128, PLANE), (128,...  1.63 us
    pallas_call x1, Pallas kernels, per_device(): call(second_faces, [(128, PLANE), face, face, (devices * 7, 128)], [edge,...  1.4 us
  transfers between devices with their start and end apart: 8, of which 2 were waited for; matrix products, arithmetic and copies ran while one was open for 0% of the time, Pallas kernels for 18%

profile of v2, /device:TPU:0, one launch (start us, length us, event | category | flops | bytes accessed | tf_op | source)
XLA Modules:
  0.0 39.0 jit_solution(2601984526027394176)
XLA Ops:
  0.6 3.1 %shard_map.59 = (f32[2,512,128]{2,1,0:T(8,128)S(1)}, f32[2,64,128]{2,1,0:T(8,128)S(1)}, f32[2,64,128]{2,1,0:T(8,128)S(1)}, f32[8,256]{1,0:T(8,128)S(1)}, f32[192,128]{1,0:T(8,128)}) custom-call(f32[256,512]{1,0:T(8,128)} %forcing_ref.1, f32[1,256]{1,0:T(1,128)} %bitcast.7, s32[1,256]{1,0:T(1,128)} %order_ref.1), custom_call_target="tpu_custom_call" | custom-call | tf_op jit(solution)/shard_map/pallas_call | solution.py:810
  3.8 5.6 %collective-permute-start = (f32[2,64,128]{2,1,0:T(8,128)S(1)}, f32[2,64,128]{2,1,0:T(8,128)S(1)}, u32[]{:S(2)}, u32[]{:S(2)}) collective-permute-start(f32[2,64,128]{2,1,0:T(8,128)S(1)} %get-tuple-element.38), channel_id=1, source_target_pairs={{0,31},{1,2},{2,1},{3,4},{4,3},{5,6},{6,5},{7,8},{8,7},{9,10},{10,... | collective-permute-start | bytes 196616 | tf_op jit(solution)/shard_map/ppermute | solution.py:794
  9.3 0.0 collective-permute-start.1
  9.3 0.0 copy-start
  9.3 2.6 %all-to-all-start = ((f32[32,3,2,128]{3,2,1,0:T(2,128)}), f32[32,3,2,128]{3,2,1,0:T(2,128)S(1)}, u32[]{:S(2)}, u32[]{:S(2)}) async-start(f32[32,3,2,128]{3,2,1,0:T(2,128)} %bitcast.1), calls=%async_computation | async-start | bytes 196608 | tf_op jit(solution)/shard_map/all_to_all | solution.py:799
  11.9 0.0 collective-permute-done.far_in_ref
  12.0 0.0 collective-permute-done.1.near_in_ref
  12.0 0.0 copy-done
  12.0 1.3 %shard_map.60 = (f32[2,512,128]{2,1,0:T(8,128)S(1)}, f32[2,512,128]{2,1,0:T(8,128)S(1)}, f32[2,512,128]{2,1,0:T(8,128)S(1)}, f32[8,256]{1,0:T(8,128)S(1)}, f32[8...) custom-call(f32[2,512,128]{2,1,0:T(8,128)S(1)} %get-tuple-element.37, ...), custom_call_target="tpu_custom_call", output_to_operand_aliasing={{0}: (0, {})} | custom-call | flops 99999997952 | bytes 268435456 | tf_op jit(solution)/shard_map/pallas_call | solution.py:824
  13.3 5.3 %collective-permute-start.2 = (f32[2,64,128]{2,1,0:T(8,128)S(1)}, f32[2,64,128]{2,1,0:T(8,128)S(1)}, u32[]{:S(2)}, u32[]{:S(2)}) collective-permute-start(f32[2,64,128]{2,1,0:T(8,128)S(1)} %get-tuple-element.49), channel_id=1, source_target_pairs={{0,31},{1,2},{2,1},{3,4},{4,3},{5,6},{6,5},{7,8},{8,7},{9,10},{10,... | collective-permute-start | bytes 196616 | tf_op jit(solution)/shard_map/ppermute | solution.py:794
  18.6 0.0 collective-permute-start.3
  18.6 1.2 %all-to-all-done = f32[32,3,2,128]{3,2,1,0:T(2,128)S(1)} async-done(((f32[32,3,2,128]{3,2,1,0:T(2,128)}), f32[32,3,2,128]{3,2,1,0:T(2,128)S(1)}, u32[]{:S(2)}, u32[]{:S(2)}) %all-to-all-start) | async-done | bytes 98336 | tf_op jit(solution)/shard_map/all_to_all | solution.py:799
  19.8 1.8 %shard_map.62 = (f32[32,256]{1,0:T(8,128)S(1)}, f32[32,256]{1,0:T(8,128)S(1)}, f32[32,256]{1,0:T(8,128)S(1)}, f32[32,256]{1,0:T(8,128)S(1)}, f32[2,512,128]{2,1,0:T(8,128)S(1)}) custom-call(f32[192,128]{1,0:T(8,128)S(1)} %bitcast.6, f32[8,256]{1,0:T(8,128)S(1)} %get-tuple-element.45.layers_ref), custom_call_target="tpu_custom_call" | custom-call | tf_op jit(solution)/shard_map/pallas_call | solution.py:828
  21.6 1.6 %shard_map.63 = (f32[2,512,128]{2,1,0:T(8,128)S(1)}, f32[2,512,128]{2,1,0:T(8,128)S(1)}, f32[48,256]{1,0:T(8,128)S(1)}, f32[8,256]{1,0:T(8,128)S(1)}, f32[128,256]{1,0:T(8,128)S(1)}, /*index=5*/f32[128,256]{1,0:T(8,128)S(1)}) custom-call(f32[2,512,128]{2,1,0:T(8,128)S(1)} %get-tuple-element.43.image_ref.first_ref, ...), custom_call_target="tpu_custom_call", output_to_operand_aliasing={{0}: (1, {})} | custom-call | tf_op jit(solution)/shard_map/pallas_call | solution.py:829
  23.2 0.0 collective-permute-done.2.far_in_ref
  23.2 0.0 collective-permute-done.3.near_in_ref
  23.2 1.4 %shard_map.64 = (f32[128,256]{1,0:T(8,128)S(1)}, f32[2,56,128]{2,1,0:T(8,128)S(1)}, f32[2,56,128]{2,1,0:T(8,128)S(1)}, f32[224,128]{1,0:T(8,128)}) custom-call(f32[2,512,128]{2,1,0:T(8,128)S(1)} %get-tuple-element.43.image_ref.first_ref, f32[2,512,128]{2,1,0:T(8,128)S(1)} %get-tuple-element.47.scaled_change_ref.first_scaled_ref, ...), custom_call_target="tpu_custom_call" | custom-call | tf_op jit(solution)/shard_map/pallas_call | solution.py:832
  24.6 3.0 %all-to-all-start.1 = ((f32[32,7,1,128]{3,2,1,0:T(1,128)}), f32[32,7,1,128]{3,2,1,0:T(1,128)S(1)}, u32[]{:S(2)}, u32[]{:S(2)}) async-start(f32[32,7,1,128]{3,2,1,0:T(1,128)} %bitcast.3), calls=%async_computation.1 | async-start | bytes 229376 | tf_op jit(solution)/shard_map/all_to_all | solution.py:799
  27.6 5.3 %collective-permute-start.4 = (f32[2,56,128]{2,1,0:T(8,128)S(1)}, f32[2,56,128]{2,1,0:T(8,128)S(1)}, u32[]{:S(2)}, u32[]{:S(2)}) collective-permute-start(f32[2,56,128]{2,1,0:T(8,128)S(1)} %get-tuple-element.62), channel_id=1, source_target_pairs={{0,31},{1,2},{2,1},{3,4},{4,3},{5,6},{6,5},{7,8},{8,7},{9,10},{10,... | collective-permute-start | bytes 172040 | tf_op jit(solution)/shard_map/ppermute | solution.py:794
  32.9 0.0 collective-permute-start.5
  32.9 1.0 %shard_map.65 = (f32[2,512,128]{2,1,0:T(8,128)S(1)}, f32[2,512,128]{2,1,0:T(8,128)S(1)}, f32[2,512,128]{2,1,0:T(8,128)S(1)}, bf16[256,256]{1,0:T(8,128)(2,1)S(1)...) custom-call(f32[2,512,128]{2,1,0:T(8,128)S(1)} %get-tuple-element.43.i, ...), custom_call_target="tpu_custom_call", output_to_operand_aliasing={{0}: (0, {}), {1}: (1, {}), {2}: (2, {})} | custom-call | tf_op jit(solution)/shard_map/pallas_call | solution.py:837
  34.0 1.8 %all-to-all-done.1 = f32[32,7,1,128]{3,2,1,0:T(1,128)S(1)} async-done(((f32[32,7,1,128]{3,2,1,0:T(1,128)}), f32[32,7,1,128]{3,2,1,0:T(1,128)S(1)}, u32[]{:S(2)}, u32[]{:S(2)}) %all-to-all-start.1) | async-done | bytes 114720 | tf_op jit(solution)/shard_map/all_to_all | solution.py:799
  35.8 1.2 %shard_map.66 = (f32[24,256]{1,0:T(8,128)S(1)}, f32[8,128]{1,0:T(8,128)S(1)}) custom-call(f32[32,256]{1,0:T(8,128)S(1)} %get-tuple-element.57.coeff_ref, f32[224,128]{1,0:T(8,128)S(1)} %bitcast.5, f32[32,256]{1,0:T(8,128)S(1)} %get-tuple-element.58.vert_ref.first_ref, f32[32,256]{1,0:T(8,128)S(1)} %get-tuple-element.65.applied_ref, ...), custom_call_target="tpu_custom_call" | custom-call | tf_op jit(solution)/shard_map/pallas_call | solution.py:840
  37.0 0.0 collective-permute-done.4.far_ref
  37.0 0.0 collective-permute-done.5.near_ref
  37.0 2.0 %shard_map.67 = (f32[256,512]{1,0:T(8,128)}, f32[256,512]{1,0:T(8,128)}) custom-call(f32[2,512,128]{2,1,0:T(8,128)S(1)} %get-tuple-element.41.resid_ref, f32[2,512,128]{2,1,0:T(8,128)S(1)} %get-tuple-element.42.scaled_ref, f32[2,512,128]{2,1,0:T(8,128)S(1)} %get-tuple-element.59.image_ref, f32[2,512,128]{2,1,0:T(8,128)S(1)} %get-tuple-element.60.scaled_change_ref, ...), custom_call_target="tpu_custom_call" | custom-call | tf_op jit(solution)/shard_map/pallas_call | solution.py:843
  (1 shorter events, 0.0 us)
Async XLA Ops:
  3.8 8.2 %collective-permute-start = (f32[2,64,128]{2,1,0:T(8,128)S(1)}, f32[2,64,128]{2,1,0:T(8,128)S(1)}, u32[]{:S(2)}, u32[]{:S(2)}) collective-permute-start(f32[2,64,128]{2,1,0:T(8,128)S(1)} %get-tuple-element.38), channel_id=1, source_target_pairs={{0,31},{1,2},{2,1},{3,4},{4,3},{5,6},{6,5},{7,8},{8,7},{9,10},{10,... | collective-permute-start | bytes 196616 | tf_op jit(solution)/shard_map/ppermute | solution.py:794
  9.3 2.6 %collective-permute-start.1 = (f32[2,64,128]{2,1,0:T(8,128)S(1)}, f32[2,64,128]{2,1,0:T(8,128)S(1)}, u32[]{:S(2)}, u32[]{:S(2)}) collective-permute-start(f32[2,64,128]{2,1,0:T(8,128)S(1)} %get-tuple-element.39), channel_id=1, source_target_pairs={{0,1},{1,0},{2,3},{3,2},{4,5},{5,4},{6,7},{7,6},{8,9},{9,8},{10,11... | collective-permute-start | bytes 196616 | tf_op jit(solution)/shard_map/ppermute | solution.py:794
  9.3 2.6 %copy-start = (bf16[3,64,128]{2,1,0:T(8,128)(2,1)S(1)}, bf16[3,64,128]{2,1,0:T(8,128)(2,1)}, u32[]{:S(2)}) copy-start(bf16[3,64,128]{2,1,0:T(8,128)(2,1)} %constant.2.clone.table_ref) | copy-start | bytes 147460
  9.3 10.4 %all-to-all-start = ((f32[32,3,2,128]{3,2,1,0:T(2,128)}), f32[32,3,2,128]{3,2,1,0:T(2,128)S(1)}, u32[]{:S(2)}, u32[]{:S(2)}) async-start(f32[32,3,2,128]{3,2,1,0:T(2,128)} %bitcast.1), calls=%async_computation | async-start | bytes 196608 | tf_op jit(solution)/shard_map/all_to_all | solution.py:799
  13.3 9.9 %collective-permute-start.2 = (f32[2,64,128]{2,1,0:T(8,128)S(1)}, f32[2,64,128]{2,1,0:T(8,128)S(1)}, u32[]{:S(2)}, u32[]{:S(2)}) collective-permute-start(f32[2,64,128]{2,1,0:T(8,128)S(1)} %get-tuple-element.49), channel_id=1, source_target_pairs={{0,31},{1,2},{2,1},{3,4},{4,3},{5,6},{6,5},{7,8},{8,7},{9,10},{10,... | collective-permute-start | bytes 196616 | tf_op jit(solution)/shard_map/ppermute | solution.py:794
  18.6 4.6 %collective-permute-start.3 = (f32[2,64,128]{2,1,0:T(8,128)S(1)}, f32[2,64,128]{2,1,0:T(8,128)S(1)}, u32[]{:S(2)}, u32[]{:S(2)}) collective-permute-start(f32[2,64,128]{2,1,0:T(8,128)S(1)} %get-tuple-element.50), channel_id=1, source_target_pairs={{0,1},{1,0},{2,3},{3,2},{4,5},{5,4},{6,7},{7,6},{8,9},{9,8},{10,11... | collective-permute-start | bytes 196616 | tf_op jit(solution)/shard_map/ppermute | solution.py:794
  24.6 11.1 %all-to-all-start.1 = ((f32[32,7,1,128]{3,2,1,0:T(1,128)}), f32[32,7,1,128]{3,2,1,0:T(1,128)S(1)}, u32[]{:S(2)}, u32[]{:S(2)}) async-start(f32[32,7,1,128]{3,2,1,0:T(1,128)} %bitcast.3), calls=%async_computation.1 | async-start | bytes 229376 | tf_op jit(solution)/shard_map/all_to_all | solution.py:799
  27.6 9.3 %collective-permute-start.4 = (f32[2,56,128]{2,1,0:T(8,128)S(1)}, f32[2,56,128]{2,1,0:T(8,128)S(1)}, u32[]{:S(2)}, u32[]{:S(2)}) collective-permute-start(f32[2,56,128]{2,1,0:T(8,128)S(1)} %get-tuple-element.62), channel_id=1, source_target_pairs={{0,31},{1,2},{2,1},{3,4},{4,3},{5,6},{6,5},{7,8},{8,7},{9,10},{10,... | collective-permute-start | bytes 172040 | tf_op jit(solution)/shard_map/ppermute | solution.py:794
  32.9 4.0 %collective-permute-start.5 = (f32[2,56,128]{2,1,0:T(8,128)S(1)}, f32[2,56,128]{2,1,0:T(8,128)S(1)}, u32[]{:S(2)}, u32[]{:S(2)}) collective-permute-start(f32[2,56,128]{2,1,0:T(8,128)S(1)} %get-tuple-element.63), channel_id=1, source_target_pairs={{0,1},{1,0},{2,3},{3,2},{4,5},{5,4},{6,7},{7,6},{8,9},{9,8},{10,11... | collective-permute-start | bytes 172040 | tf_op jit(solution)/shard_map/ppermute | solution.py:794

commit v3 on v2

--- a/solution.py
+++ b/solution.py
@@ -73,7 +73,7 @@
 DIAG = np.diag(STIFF)
 ENDS = np.array([2.0] + [1.0] * 6 + [2.0])
 MASS = np.diag(WEIGHTS)
-STIFF_XY = np.tile(np.kron(MASS, STIFF) + np.kron(STIFF, MASS), (1, 2))
+STIFF_XY = np.kron(MASS, STIFF) + np.kron(STIFF, MASS)
 STIFF_PARTS = []
 for part in range(3):
     STIFF_PARTS.append((STIFF_XY - sum(STIFF_PARTS)).astype(ml_dtypes.bfloat16).astype(np.float64))
@@ -326,23 +326,16 @@
     return 0 if node == 0 else (2 if node == 7 else 1)
 
 
-def product(tables, values):
+def product(table, values):
     low, middle, high = pieces(values)
-
-    def dot(k, right):
-        return jnp.dot(tables[k], right, preferred_element_type=F32)
-
-    return dot(0, high) + ((dot(0, middle) + dot(1, high)) + (dot(1, middle) + (dot(0, low) + dot(2, high))))
+    stacked = jnp.concatenate([high, middle, high, middle, low, high], axis=0)
+    return jnp.dot(table, stacked, preferred_element_type=F32)
 
 
 def operate(z_ref, xy_ref, out_ref, table_ref, coeff, weight_x):
-    row, col = (lax.broadcasted_iota(jnp.int32, (256, 256), axis) for axis in range(2))
-    tables = [
-        jnp.where(row // 64 == col // 64, jnp.tile(table_ref[k].astype(F32), (4, 2)), 0.0).astype(jnp.bfloat16) for k in range(3)
-    ]
-    for half in range(2):
-        rows = slice(half * 256, half * 256 + 256)
-        xy_ref[rows, :] = product(tables, get(z_ref, rows))
+    for nz in range(8):
+        rows = slice(64 * nz, 64 * nz + 64)
+        xy_ref[rows, :] = product(table_ref[...], get(z_ref, rows))
     for ny in range(8):
         tiles = [get(z_ref, rows_of(nz, ny)) for nz in range(8)]
         even = [tiles[k] + tiles[7 - k] for k in range(4)]
@@ -595,8 +588,7 @@
     faces = below_above(face_in(near_in_ref), face_in(far_in_ref))
     tiles = [slice(8 * ny, 8 * ny + 8) for ny in range(8)]
     added = added_by(faces, kappas, columns_of_nodes())
-    small_tables = [table_ref[k, :, 0:64] for k in range(3)]
-    xy_ref[...] = product(small_tables, jnp.concatenate(added, axis=1))
+    xy_ref[...] = product(table_ref[...], jnp.concatenate(added, axis=1))
     along, at_face = [], []
     for k in range(2):
         along.append(local_along(own, weight_x, added[k]))
@@ -742,30 +734,34 @@
     return total
 
 
-def closing(
-    resid_ref, scaled_ref, image_ref, scaled_change_ref, change_ref, far_ref, near_ref, modes_ref, layers_ref, scalars_ref,
-    choose_ref, solution_ref, residual_ref, grid_ref, sum_ref, edge_ref, held, sems,
+def combine(
+    first_scaled_ref, first_resid_ref, scaled_change_ref, image_ref, change_ref, modes_ref, layers_ref, scalars_ref,
+    found_ref, rest_ref, smooth_ref, edge_ref,
 ):
     smooths = smooths_of(modes_ref[...], layers_ref)
     first, second = scalars_ref[0:1, 0:1], scalars_ref[1:2, 0:1]
-    choose = choose_ref[...]
+    smooth_image(smooths, smooth_ref, edge_ref)
     for nz in range(8):
         for ny in range(8):
             rows = rows_of(nz, ny)
-            rough = first * get(scaled_ref, rows) - second * get(scaled_change_ref, rows)
-            grid_ref[rows, :] = rough + smooths[0].value(nz, ny)
-    held[0] = to_stored(choose, grid_ref[...])
-    smooth_image(smooths, sum_ref, edge_ref)
+            rough = first * get(first_scaled_ref, rows) - second * get(scaled_change_ref, rows)
+            put(found_ref, rows, rough + smooths[0].value(nz, ny))
     first, second = first[None], second[None]
-    sum_ref[...] = resid_ref[...] - first * image_ref[...] + second * change_ref[...] - sum_ref[...]
+    rest_ref[...] = first_resid_ref[...] - first * image_ref[...] + second * change_ref[...] - smooth_ref[...]
+
+
+def closing(
+    found_ref, rest_ref, far_ref, near_ref, scalars_ref, choose_ref, solution_ref, residual_ref, sum_ref, held, sems
+):
+    choose, every = choose_ref[...], slice(0, 512)
+    second = scalars_ref[1:2, 0:1]
+    sum_ref[...] = rest_ref[...]
     for rows, ref in zip(face_rows(sum_ref), (near_ref, far_ref)):
-        put(sum_ref, rows, get(sum_ref, rows) + second[0] * face_in(ref))
-    copies = [pltpu.make_async_copy(held.at[0], solution_ref, sems.at[0])]
-    copies[0].start()
-    for part in range(2):
-        stored = slice(128 * part, 128 * part + 128)
-        held[1, stored, :] = to_stored(choose[stored], get(sum_ref, slice(0, 512)))
-        copies.append(pltpu.make_async_copy(held.at[1, stored], residual_ref.at[stored], sems.at[1 + part]))
+        put(sum_ref, rows, get(sum_ref, rows) + second * face_in(ref))
+    copies = []
+    for k, (ref, out_ref) in enumerate(((found_ref, solution_ref), (sum_ref, residual_ref))):
+        held[k] = to_stored(choose, get(ref, every))
+        copies.append(pltpu.make_async_copy(held.at[k], out_ref, sems.at[k]))
         copies[-1].start()
     for copy in copies:
         copy.wait()
@@ -804,7 +800,7 @@
     nodes, face, face_row = (2, 512, 128), (2, 56, 128), (2, 64, 128)
     plane, grid, flat = (8, PLANE), (devices, PLANE), (512, PLANE)
     edge, stored, choice = (2, 128, 128), (PLANE, 512), ((PLANE, PLANE), jnp.bfloat16)
-    table = jnp.asarray(np.stack(STIFF_PARTS), jnp.bfloat16)
+    table = jnp.asarray(np.concatenate([STIFF_PARTS[k] for k in (0, 0, 1, 1, 0, 2)], 1), jnp.bfloat16)
     long = pl.CostEstimate(flops=10**11, bytes_accessed=2**28, transcendentals=0)
     payload_rows = (devices * 6, 128)
     load, far, near, own, payload = call(
@@ -840,8 +836,11 @@
     modes, scalars = call(second_coarse, [(24, PLANE), (8, 128)], [grid])(
         coeff, step, vert, applied, target, scale, first_modes
     )
-    found, left = call(closing, [stored, stored], [flat, nodes, edge, (2,) + stored], 3, hbm_out=(0, 1))(
-        resid, scaled, image, scaled_change, change, next_far, next_near, modes, layers, scalars, choose
+    found, rest = call(combine, [nodes, nodes], [nodes, edge], in_place={0: 0, 1: 1})(
+        scaled, resid, scaled_change, image, change, modes, layers, scalars
+    )
+    found, left = call(closing, [stored, stored], [nodes, (2,) + stored], 2, hbm_out=(0, 1))(
+        found, rest, next_far, next_near, scalars, choose
     )
     return found, left
 

time: 39.6 us -> 39.5 us (level)
  waiting for transfers between devices: 2.97 us -> 3.4 us
    all_to_all x2, waiting for transfers between devices: 2.96 us -> 3.39 us  [everyone(): lax.all_to_all(payload.reshape((devices,) + shape), AXES, 0, 0, tiled=True)]
    pallas_call x1 -> x2, Pallas kernels: 2.01 us -> 2.19 us  [the longest x1 1.38 us: per_device(): call(closing, [stored, stored], [nodes, (2,) + stored], 2, hbm_out=(0, 1))]
  transfers between devices with their start and end apart: 8 -> 8, of which waited for: 2 -> 2; matrix products, arithmetic and copies ran while one was open for 0% -> 0% of each run, Pallas kernels for 18% -> 19%
where the time goes in v3:
time: 39.5 us; the launch traced here: 38.8 us
  starting transfers between devices  21.5 us (54%)
  Pallas kernels  13.2 us (33%)
  waiting for transfers between devices  3.4 us (9%)
  between operations  0.73 us (2%)
    ppermute x6, starting transfers between devices, swapped(): lax.ppermute(x, AXES, [(i, (i + (1 if (i % 2 == 0) != far else -1)) % siz...  16.1 us
    all_to_all x2, starting transfers between devices, everyone(): lax.all_to_all(payload.reshape((devices,) + shape), AXES, 0, 0, tiled=True)  5.36 us
    all_to_all x2, waiting for transfers between devices, everyone(): lax.all_to_all(payload.reshape((devices,) + shape), AXES, 0, 0, tiled=True)  3.39 us
    pallas_call x1, Pallas kernels, per_device(): call(opening, [nodes, face_row, face_row, plane, payload_rows], [(2, PLAN...  3.11 us
    pallas_call x1, Pallas kernels, per_device(): call(first_coarse, [grid] * 4 + [nodes], [edge])(gather, layers)  1.8 us
    pallas_call x1, Pallas kernels, per_device(): call(second_rough, [nodes] * 2 + [(48, PLANE), plane, (128, PLANE), (128,...  1.46 us
    pallas_call x1, Pallas kernels, per_device(): call(closing, [stored, stored], [nodes, (2,) + stored], 2, hbm_out=(0, 1))  1.38 us
    pallas_call x1, Pallas kernels, per_device(): call(second_faces, [(128, PLANE), face, face, (devices * 7, 128)], [edge,...  1.35 us
  transfers between devices with their start and end apart: 8, of which 2 were waited for; matrix products, arithmetic and copies ran while one was open for 0% of the time, Pallas kernels for 19%

profile of v3, /device:TPU:0, one launch (start us, length us, event | category | flops | bytes accessed | tf_op | source)
XLA Modules:
  0.0 38.8 jit_solution(14633693227450472729)
XLA Ops:
  0.6 3.1 %shard_map.59 = (f32[2,512,128]{2,1,0:T(8,128)S(1)}, f32[2,64,128]{2,1,0:T(8,128)S(1)}, f32[2,64,128]{2,1,0:T(8,128)S(1)}, f32[8,256]{1,0:T(8,128)S(1)}, f32[192,128]{1,0:T(8,128)}) custom-call(f32[256,512]{1,0:T(8,128)} %forcing_ref.1, f32[1,256]{1,0:T(1,128)} %bitcast.7, s32[1,256]{1,0:T(1,128)} %order_ref.1), custom_call_target="tpu_custom_call" | custom-call | tf_op jit(solution)/shard_map/pallas_call | solution.py:806
  3.8 5.6 %collective-permute-start = (f32[2,64,128]{2,1,0:T(8,128)S(1)}, f32[2,64,128]{2,1,0:T(8,128)S(1)}, u32[]{:S(2)}, u32[]{:S(2)}) collective-permute-start(f32[2,64,128]{2,1,0:T(8,128)S(1)} %get-tuple-element.40), channel_id=1, source_target_pairs={{0,31},{1,2},{2,1},{3,4},{4,3},{5,6},{6,5},{7,8},{8,7},{9,10},{10,... | collective-permute-start | bytes 196616 | tf_op jit(solution)/shard_map/ppermute | solution.py:790
  9.3 0.0 collective-permute-start.1
  9.3 0.0 copy-start
  9.3 2.6 %all-to-all-start = ((f32[32,3,2,128]{3,2,1,0:T(2,128)}), f32[32,3,2,128]{3,2,1,0:T(2,128)S(1)}, u32[]{:S(2)}, u32[]{:S(2)}) async-start(f32[32,3,2,128]{3,2,1,0:T(2,128)} %bitcast.1), calls=%async_computation | async-start | bytes 196608 | tf_op jit(solution)/shard_map/all_to_all | solution.py:795
  11.9 0.0 collective-permute-done.far_in_ref
  12.0 0.0 collective-permute-done.1.near_in_ref
  12.0 0.0 copy-done
  12.0 1.1 %shard_map.60 = (f32[2,512,128]{2,1,0:T(8,128)S(1)}, f32[2,512,128]{2,1,0:T(8,128)S(1)}, f32[2,512,128]{2,1,0:T(8,128)S(1)}, f32[8,256]{1,0:T(8,128)S(1)}, f32[8...) custom-call(f32[2,512,128]{2,1,0:T(8,128)S(1)} %get-tuple-element.39, ...), custom_call_target="tpu_custom_call", output_to_operand_aliasing={{0}: (0, {})} | custom-call | flops 99999997952 | bytes 268435456 | tf_op jit(solution)/shard_map/pallas_call | solution.py:820
  13.0 5.3 %collective-permute-start.2 = (f32[2,64,128]{2,1,0:T(8,128)S(1)}, f32[2,64,128]{2,1,0:T(8,128)S(1)}, u32[]{:S(2)}, u32[]{:S(2)}) collective-permute-start(f32[2,64,128]{2,1,0:T(8,128)S(1)} %get-tuple-element.51), channel_id=1, source_target_pairs={{0,31},{1,2},{2,1},{3,4},{4,3},{5,6},{6,5},{7,8},{8,7},{9,10},{10,... | collective-permute-start | bytes 196616 | tf_op jit(solution)/shard_map/ppermute | solution.py:790
  18.3 0.0 collective-permute-start.3
  18.3 1.6 %all-to-all-done = f32[32,3,2,128]{3,2,1,0:T(2,128)S(1)} async-done(((f32[32,3,2,128]{3,2,1,0:T(2,128)}), f32[32,3,2,128]{3,2,1,0:T(2,128)S(1)}, u32[]{:S(2)}, u32[]{:S(2)}) %all-to-all-start) | async-done | bytes 98336 | tf_op jit(solution)/shard_map/all_to_all | solution.py:795
  19.9 1.8 %shard_map.62 = (f32[32,256]{1,0:T(8,128)S(1)}, f32[32,256]{1,0:T(8,128)S(1)}, f32[32,256]{1,0:T(8,128)S(1)}, f32[32,256]{1,0:T(8,128)S(1)}, f32[2,512,128]{2,1,0:T(8,128)S(1)}) custom-call(f32[192,128]{1,0:T(8,128)S(1)} %bitcast.6, f32[8,256]{1,0:T(8,128)S(1)} %get-tuple-element.47.layers_ref), custom_call_target="tpu_custom_call" | custom-call | tf_op jit(solution)/shard_map/pallas_call | solution.py:824
  21.7 1.5 %shard_map.63 = (f32[2,512,128]{2,1,0:T(8,128)S(1)}, f32[2,512,128]{2,1,0:T(8,128)S(1)}, f32[48,256]{1,0:T(8,128)S(1)}, f32[8,256]{1,0:T(8,128)S(1)}, f32[128,256]{1,0:T(8,128)S(1)}, /*index=5*/f32[128,256]{1,0:T(8,128)S(1)}) custom-call(f32[2,512,128]{2,1,0:T(8,128)S(1)} %get-tuple-element.45.image_ref.first_ref, ...), custom_call_target="tpu_custom_call", output_to_operand_aliasing={{0}: (1, {})} | custom-call | tf_op jit(solution)/shard_map/pallas_call | solution.py:825
  23.2 0.0 collective-permute-done.2.far_in_ref
  23.2 0.0 collective-permute-done.3.near_in_ref
  23.2 1.3 %shard_map.64 = (f32[128,256]{1,0:T(8,128)S(1)}, f32[2,56,128]{2,1,0:T(8,128)S(1)}, f32[2,56,128]{2,1,0:T(8,128)S(1)}, f32[224,128]{1,0:T(8,128)}) custom-call(f32[2,512,128]{2,1,0:T(8,128)S(1)} %get-tuple-element.45.image_ref.first_ref, f32[2,512,128]{2,1,0:T(8,128)S(1)} %get-tuple-element.49.scaled_change_ref.first_scaled_ref, ...), custom_call_target="tpu_custom_call" | custom-call | tf_op jit(solution)/shard_map/pallas_call | solution.py:828
  24.5 2.8 %all-to-all-start.1 = ((f32[32,7,1,128]{3,2,1,0:T(1,128)}), f32[32,7,1,128]{3,2,1,0:T(1,128)S(1)}, u32[]{:S(2)}, u32[]{:S(2)}) async-start(f32[32,7,1,128]{3,2,1,0:T(1,128)} %bitcast.3), calls=%async_computation.1 | async-start | bytes 229376 | tf_op jit(solution)/shard_map/all_to_all | solution.py:795
  27.3 5.3 %collective-permute-start.4 = (f32[2,56,128]{2,1,0:T(8,128)S(1)}, f32[2,56,128]{2,1,0:T(8,128)S(1)}, u32[]{:S(2)}, u32[]{:S(2)}) collective-permute-start(f32[2,56,128]{2,1,0:T(8,128)S(1)} %get-tuple-element.73), channel_id=1, source_target_pairs={{0,31},{1,2},{2,1},{3,4},{4,3},{5,6},{6,5},{7,8},{8,7},{9,10},{10,... | collective-permute-start | bytes 172040 | tf_op jit(solution)/shard_map/ppermute | solution.py:790
  32.6 0.0 collective-permute-start.5
  32.6 1.0 %shard_map.65 = (f32[2,512,128]{2,1,0:T(8,128)S(1)}, f32[2,512,128]{2,1,0:T(8,128)S(1)}, f32[2,512,128]{2,1,0:T(8,128)S(1)}, bf16[256,256]{1,0:T(8,128)(2,1)S(1)...) custom-call(f32[2,512,128]{2,1,0:T(8,128)S(1)} %get-tuple-element.45.i, ...), custom_call_target="tpu_custom_call", output_to_operand_aliasing={{0}: (0, {}), {1}: (1, {}), {2}: (2, {})} | custom-call | tf_op jit(solution)/shard_map/pallas_call | solution.py:833
  33.6 1.8 %all-to-all-done.1 = f32[32,7,1,128]{3,2,1,0:T(1,128)S(1)} async-done(((f32[32,7,1,128]{3,2,1,0:T(1,128)}), f32[32,7,1,128]{3,2,1,0:T(1,128)S(1)}, u32[]{:S(2)}, u32[]{:S(2)}) %all-to-all-start.1) | async-done | bytes 114720 | tf_op jit(solution)/shard_map/all_to_all | solution.py:795
  35.4 1.2 %shard_map.66 = (f32[24,256]{1,0:T(8,128)S(1)}, f32[8,128]{1,0:T(8,128)S(1)}) custom-call(f32[32,256]{1,0:T(8,128)S(1)} %get-tuple-element.59.coeff_ref, f32[224,128]{1,0:T(8,128)S(1)} %bitcast.5, f32[32,256]{1,0:T(8,128)S(1)} %get-tuple-element.60.vert_ref.first_ref, f32[32,256]{1,0:T(8,128)S(1)} %get-tuple-element.65.applied_ref, ...), custom_call_target="tpu_custom_call" | custom-call | tf_op jit(solution)/shard_map/pallas_call | solution.py:836
  36.6 0.8 %shard_map.67 = (f32[2,512,128]{2,1,0:T(8,128)S(1)}, f32[2,512,128]{2,1,0:T(8,128)S(1)}) custom-call(f32[2,512,128]{2,1,0:T(8,128)S(1)} %get-tuple-element.43.scaled_ref.first_scaled_ref, f32[2,512,128]{2,1,0:T(8,128)S(1)} %get-tuple-element.44.resid_ref.first_resid_ref, ...), custom_call_target="tpu_custom_call", output_to_operand_aliasing={{0}: (0, {}), {1}: (1, {})} | custom-call | tf_op jit(solution)/shard_map/pallas_call | solution.py:839
  37.4 0.0 collective-permute-done.4.far_ref
  37.4 0.0 collective-permute-done.5.near_ref
  37.5 1.4 %shard_map.68 = (f32[256,512]{1,0:T(8,128)}, f32[256,512]{1,0:T(8,128)}) custom-call(f32[2,512,128]{2,1,0:T(8,128)S(1)} %get-tuple-element.71.found_ref, f32[2,512,128]{2,1,0:T(8,128)S(1)} %get-tuple-element.72.rest_ref, f32[2,56,128]{2,1,0:T(8,128)S(1)} %collective-permute-done.4.far_ref, f32[2,56,128]{2,1,0:T(8,128)S(1)} %collective-permute-done.5.near_ref, ...), custom_call_target="tpu_custom_call" | custom-call | tf_op jit(solution)/shard_map/pallas_call | solution.py:842
  (1 shorter events, 0.0 us)
Async XLA Ops:
  3.8 8.2 %collective-permute-start = (f32[2,64,128]{2,1,0:T(8,128)S(1)}, f32[2,64,128]{2,1,0:T(8,128)S(1)}, u32[]{:S(2)}, u32[]{:S(2)}) collective-permute-start(f32[2,64,128]{2,1,0:T(8,128)S(1)} %get-tuple-element.40), channel_id=1, source_target_pairs={{0,31},{1,2},{2,1},{3,4},{4,3},{5,6},{6,5},{7,8},{8,7},{9,10},{10,... | collective-permute-start | bytes 196616 | tf_op jit(solution)/shard_map/ppermute | solution.py:790
  9.3 2.6 %collective-permute-start.1 = (f32[2,64,128]{2,1,0:T(8,128)S(1)}, f32[2,64,128]{2,1,0:T(8,128)S(1)}, u32[]{:S(2)}, u32[]{:S(2)}) collective-permute-start(f32[2,64,128]{2,1,0:T(8,128)S(1)} %get-tuple-element.41), channel_id=1, source_target_pairs={{0,1},{1,0},{2,3},{3,2},{4,5},{5,4},{6,7},{7,6},{8,9},{9,8},{10,11... | collective-permute-start | bytes 196616 | tf_op jit(solution)/shard_map/ppermute | solution.py:790
  9.3 2.6 %copy-start = (bf16[64,384]{1,0:T(8,128)(2,1)S(1)}, bf16[64,384]{1,0:T(8,128)(2,1)}, u32[]{:S(2)}) copy-start(bf16[64,384]{1,0:T(8,128)(2,1)} %constant.2.clone.table_ref) | copy-start | bytes 147460
  9.3 10.6 %all-to-all-start = ((f32[32,3,2,128]{3,2,1,0:T(2,128)}), f32[32,3,2,128]{3,2,1,0:T(2,128)S(1)}, u32[]{:S(2)}, u32[]{:S(2)}) async-start(f32[32,3,2,128]{3,2,1,0:T(2,128)} %bitcast.1), calls=%async_computation | async-start | bytes 196608 | tf_op jit(solution)/shard_map/all_to_all | solution.py:795
  13.0 10.1 %collective-permute-start.2 = (f32[2,64,128]{2,1,0:T(8,128)S(1)}, f32[2,64,128]{2,1,0:T(8,128)S(1)}, u32[]{:S(2)}, u32[]{:S(2)}) collective-permute-start(f32[2,64,128]{2,1,0:T(8,128)S(1)} %get-tuple-element.51), channel_id=1, source_target_pairs={{0,31},{1,2},{2,1},{3,4},{4,3},{5,6},{6,5},{7,8},{8,7},{9,10},{10,... | collective-permute-start | bytes 196616 | tf_op jit(solution)/shard_map/ppermute | solution.py:790
  18.3 4.9 %collective-permute-start.3 = (f32[2,64,128]{2,1,0:T(8,128)S(1)}, f32[2,64,128]{2,1,0:T(8,128)S(1)}, u32[]{:S(2)}, u32[]{:S(2)}) collective-permute-start(f32[2,64,128]{2,1,0:T(8,128)S(1)} %get-tuple-element.52), channel_id=1, source_target_pairs={{0,1},{1,0},{2,3},{3,2},{4,5},{5,4},{6,7},{7,6},{8,9},{9,8},{10,11... | collective-permute-start | bytes 196616 | tf_op jit(solution)/shard_map/ppermute | solution.py:790
  24.5 10.9 %all-to-all-start.1 = ((f32[32,7,1,128]{3,2,1,0:T(1,128)}), f32[32,7,1,128]{3,2,1,0:T(1,128)S(1)}, u32[]{:S(2)}, u32[]{:S(2)}) async-start(f32[32,7,1,128]{3,2,1,0:T(1,128)} %bitcast.3), calls=%async_computation.1 | async-start | bytes 229376 | tf_op jit(solution)/shard_map/all_to_all | solution.py:795
  27.3 10.1 %collective-permute-start.4 = (f32[2,56,128]{2,1,0:T(8,128)S(1)}, f32[2,56,128]{2,1,0:T(8,128)S(1)}, u32[]{:S(2)}, u32[]{:S(2)}) collective-permute-start(f32[2,56,128]{2,1,0:T(8,128)S(1)} %get-tuple-element.73), channel_id=1, source_target_pairs={{0,31},{1,2},{2,1},{3,4},{4,3},{5,6},{6,5},{7,8},{8,7},{9,10},{10,... | collective-permute-start | bytes 172040 | tf_op jit(solution)/shard_map/ppermute | solution.py:790
  32.6 4.8 %collective-permute-start.5 = (f32[2,56,128]{2,1,0:T(8,128)S(1)}, f32[2,56,128]{2,1,0:T(8,128)S(1)}, u32[]{:S(2)}, u32[]{:S(2)}) collective-permute-start(f32[2,56,128]{2,1,0:T(8,128)S(1)} %get-tuple-element.74), channel_id=1, source_target_pairs={{0,1},{1,0},{2,3},{3,2},{4,5},{5,4},{6,7},{7,6},{8,9},{9,8},{10,11... | collective-permute-start | bytes 172040 | tf_op jit(solution)/shard_map/ppermute | solution.py:790

commit v4 on v3

--- a/solution.py
+++ b/solution.py
@@ -661,14 +661,19 @@
 
 
 def complete(
-    first_ref, first_scaled_ref, first_change_ref, far_in_ref, near_in_ref, at_face_ref, layers_ref, coeff_ref, vert_ref,
-    image_ref, scaled_change_ref, change_ref, choose_ref, applied_ref, modes_ref, edge_ref,
+    first_ref, first_scaled_ref, first_change_ref, rough_ref, far_in_ref, near_in_ref, at_face_ref, layers_ref, coeff_ref,
+    vert_ref, image_ref, scaled_change_ref, change_ref, z_ref, choose_ref, applied_ref, edge_ref, smooth_ref, sides_ref,
 ):
     columns = columns_of_nodes()
     applied_ref[...] = coarse_apply(vert_ref[...], coarse_modes(coeff_ref[...]))
-    modes_ref[...] = three_modes(vert_ref)
+    smooths = smooths_of(three_modes(vert_ref), layers_ref)
+    for nz in range(8):
+        for ny in range(8):
+            rows = rows_of(nz, ny)
+            put(z_ref, rows, get(rough_ref, rows) + smooths[0].value(nz, ny))
+    smooth_image(smooths, smooth_ref, sides_ref)
     choose_ref[...] = selection(layers_ref[3:4, :]).astype(F32).T.astype(jnp.bfloat16)
-    image_ref[...] = first_ref[...]
+    image_ref[...] = first_ref[...] + smooth_ref[...]
     scaled_change_ref[...] = first_scaled_ref[...]
     faces_in(image_ref, near_in_ref, far_in_ref)
     kappas = kappa_sums(*(layers_ref[k : k + 1, :] for k in range(3)))
@@ -691,8 +696,17 @@
     return functools.reduce(lambda a, b: a + b, [value[k : k + 8] for k in range(0, value.shape[0], 8)])
 
 
-def second_coarse(
-    coeff_ref, step_ref, first_ref, applied_ref, target_ref, scale_ref, first_modes_ref, modes_ref, scalars_ref, vert_ref
+def to_stored(choose, value):
+    total = jnp.zeros((choose.shape[0], value.shape[0]), F32)
+    for piece in pieces(value)[1:]:
+        total = total + lax.dot_general(choose, piece, (((1,), (1,)), ((), ())), preferred_element_type=F32)
+    return total
+
+
+def closing(
+    coeff_ref, step_ref, first_ref, applied_ref, target_ref, scale_ref, layers_ref,
+    resid_ref, z_ref, image_ref, scaled_change_ref, change_ref, far_ref, near_ref, choose_ref,
+    solution_ref, residual_ref, vert_ref, grid_ref, sum_ref, edge_ref, held, sems,
 ):
     modes = coarse_modes(coeff_ref[...])
     target, first, applied = target_ref[...], first_ref[...], applied_ref[...]
@@ -708,7 +722,7 @@
     image = rough + applied
     change = coarse_solve(image, modes, scale_ref[...])
     vert_ref[...] = change
-    change_modes = three_modes(vert_ref)
+    smooths = smooths_of(three_modes(vert_ref), layers_ref)
     change_applied = coarse_apply(change, modes)
     gamma = total(sums[0], target * first)
     energy = total(sums[3], first * (2.0 * rough + applied))
@@ -720,49 +734,25 @@
         vert * (2.0 * (rough - alpha * rough_change) + (applied - alpha * change_applied)),
     )
     cross = total(sums[1] - alpha * sums[2], vert * image)
+    smooth_image(smooths, sum_ref, edge_ref)
+    sum_ref[...] += change_ref[...]
+    faces_in(sum_ref, near_ref, far_ref)
     beta = progress / gamma
     alpha_next = progress / (second + beta * (2.0 * cross + beta * energy))
-    scalars = [alpha + alpha_next * beta + alpha_next, alpha_next * alpha]
-    modes_ref[...] = scalars[0] * first_modes_ref[...] - scalars[1] * change_modes
-    scalars_ref[...] = jnp.concatenate([jnp.broadcast_to(t, (1, 128)) for t in scalars * 4], axis=0)
-
-
-def to_stored(choose, value):
-    total = jnp.zeros((choose.shape[0], value.shape[0]), F32)
-    for piece in pieces(value)[1:]:
-        total = total + lax.dot_general(choose, piece, (((1,), (1,)), ((), ())), preferred_element_type=F32)
-    return total
-
-
-def combine(
-    first_scaled_ref, first_resid_ref, scaled_change_ref, image_ref, change_ref, modes_ref, layers_ref, scalars_ref,
-    found_ref, rest_ref, smooth_ref, edge_ref,
-):
-    smooths = smooths_of(modes_ref[...], layers_ref)
-    first, second = scalars_ref[0:1, 0:1], scalars_ref[1:2, 0:1]
-    smooth_image(smooths, smooth_ref, edge_ref)
+    share, change_share = alpha + alpha_next * beta + alpha_next, alpha_next * alpha
+    choose, every = choose_ref[...], slice(0, 512)
     for nz in range(8):
         for ny in range(8):
             rows = rows_of(nz, ny)
-            rough = first * get(first_scaled_ref, rows) - second * get(scaled_change_ref, rows)
-            put(found_ref, rows, rough + smooths[0].value(nz, ny))
-    first, second = first[None], second[None]
-    rest_ref[...] = first_resid_ref[...] - first * image_ref[...] + second * change_ref[...] - smooth_ref[...]
-
-
-def closing(
-    found_ref, rest_ref, far_ref, near_ref, scalars_ref, choose_ref, solution_ref, residual_ref, sum_ref, held, sems
-):
-    choose, every = choose_ref[...], slice(0, 512)
-    second = scalars_ref[1:2, 0:1]
-    sum_ref[...] = rest_ref[...]
-    for rows, ref in zip(face_rows(sum_ref), (near_ref, far_ref)):
-        put(sum_ref, rows, get(sum_ref, rows) + second * face_in(ref))
-    copies = []
-    for k, (ref, out_ref) in enumerate(((found_ref, solution_ref), (sum_ref, residual_ref))):
-        held[k] = to_stored(choose, get(ref, every))
-        copies.append(pltpu.make_async_copy(held.at[k], out_ref, sems.at[k]))
-        copies[-1].start()
+            other = get(scaled_change_ref, rows) + smooths[0].value(nz, ny)
+            grid_ref[rows, :] = share * get(z_ref, rows) - change_share * other
+    held[0] = to_stored(choose, grid_ref[...])
+    sum_ref[...] = resid_ref[...] - share[None] * image_ref[...] + change_share[None] * sum_ref[...]
+    copies = [pltpu.make_async_copy(held.at[0], solution_ref, sems.at[0])]
+    copies[0].start()
+    held[1] = to_stored(choose, get(sum_ref, every))
+    copies.append(pltpu.make_async_copy(held.at[1], residual_ref, sems.at[1]))
+    copies[1].start()
     for copy in copies:
         copy.wait()
 
@@ -830,17 +820,15 @@
     )(image, scaled_change, change, outer, far, near, layers, table, scaled, lower, sums, planes, column_planes)
     step = everyone(payload, (7, 1, 128))
     next_far, next_near = swapped(next_far, True), swapped(next_near, False)
-    image, scaled_change, change, choose, applied, first_modes = call(
-        complete, [nodes] * 3 + [choice, grid, (24, PLANE)], [(2, 256, 128)], in_place={0: 0, 1: 1, 2: 2}
-    )(image, scaled_change, change, far, near, added, layers, coeff, vert)
-    modes, scalars = call(second_coarse, [(24, PLANE), (8, 128)], [grid])(
-        coeff, step, vert, applied, target, scale, first_modes
-    )
-    found, rest = call(combine, [nodes, nodes], [nodes, edge], in_place={0: 0, 1: 1})(
-        scaled, resid, scaled_change, image, change, modes, layers, scalars
-    )
-    found, left = call(closing, [stored, stored], [nodes, (2,) + stored], 2, hbm_out=(0, 1))(
-        found, rest, next_far, next_near, scalars, choose
+    image, scaled_change, change, z, choose, applied = call(
+        complete,
+        [nodes] * 4 + [choice, grid],
+        [(2, 256, 128), nodes, edge],
+        in_place={0: 0, 1: 1, 2: 2, 3: 3},
+    )(image, scaled_change, change, scaled, far, near, added, layers, coeff, vert)
+    found, left = call(closing, [stored, stored], [grid, flat, nodes, edge, (2,) + stored], 2, hbm_out=(0, 1))(
+        coeff, step, vert, applied, target, scale, layers,
+        resid, z, image, scaled_change, change, next_far, next_near, choose,
     )
     return found, left
 

time: 39.5 us -> 39.6 us (level)
  waiting for transfers between devices: 3.4 us -> 3.93 us
    ppermute x6, waiting for transfers between devices: 0.02 us -> 2.33 us  [swapped(): lax.ppermute(x, AXES, [(i, (i + (1 if (i % 2 == 0) != far else -1)) % siz...]
    all_to_all x2, waiting for transfers between devices: 3.39 us -> 1.6 us  [everyone(): lax.all_to_all(payload.reshape((devices,) + shape), AXES, 0, 0, tiled=True)]
    pallas_call x4 -> x2, Pallas kernels: 4.41 us -> 4.37 us  [the longest x1 2.97 us: per_device(): call(closing, [stored, stored], [grid, flat, nodes, edge, (2,) + stored],...]
  transfers between devices with their start and end apart: 8 -> 8, of which waited for: 2 -> 2; matrix products, arithmetic and copies ran while one was open for 0% -> 0% of each run, Pallas kernels for 19% -> 15%
where the time goes in v4:
time: 39.6 us; the launch traced here: 39.3 us
  starting transfers between devices  21.5 us (54%)
  Pallas kernels  13.2 us (33%)
  waiting for transfers between devices  3.93 us (10%)
  between operations  0.72 us (2%)
    ppermute x6, starting transfers between devices, swapped(): lax.ppermute(x, AXES, [(i, (i + (1 if (i % 2 == 0) != far else -1)) % siz...  16.1 us
    all_to_all x2, starting transfers between devices, everyone(): lax.all_to_all(payload.reshape((devices,) + shape), AXES, 0, 0, tiled=True)  5.36 us
    pallas_call x1, Pallas kernels, per_device(): call(opening, [nodes, face_row, face_row, plane, payload_rows], [(2, PLAN...  3.11 us
    pallas_call x1, Pallas kernels, per_device(): call(closing, [stored, stored], [grid, flat, nodes, edge, (2,) + stored],...  2.97 us
    ppermute x6, waiting for transfers between devices, swapped(): lax.ppermute(x, AXES, [(i, (i + (1 if (i % 2 == 0) != far else -1)) % siz...  2.33 us
    pallas_call x1, Pallas kernels, per_device(): call(first_coarse, [grid] * 4 + [nodes], [edge])(gather, layers)  1.8 us
    all_to_all x2, waiting for transfers between devices, everyone(): lax.all_to_all(payload.reshape((devices,) + shape), AXES, 0, 0, tiled=True)  1.6 us
    pallas_call x1, Pallas kernels, per_device(): call(second_rough, [nodes] * 2 + [(48, PLANE), plane, (128, PLANE), (128,...  1.46 us
  transfers between devices with their start and end apart: 8, of which 2 were waited for; matrix products, arithmetic and copies ran while one was open for 0% of the time, Pallas kernels for 15%

profile of v4, /device:TPU:0, one launch (start us, length us, event | category | flops | bytes accessed | tf_op | source)
XLA Modules:
  0.0 39.3 jit_solution(11182304594667354443)
XLA Ops:
  0.6 3.1 %shard_map.59 = (f32[2,512,128]{2,1,0:T(8,128)S(1)}, f32[2,64,128]{2,1,0:T(8,128)S(1)}, f32[2,64,128]{2,1,0:T(8,128)S(1)}, f32[8,256]{1,0:T(8,128)S(1)}, f32[192,128]{1,0:T(8,128)}) custom-call(f32[256,512]{1,0:T(8,128)} %forcing_ref.1, f32[1,256]{1,0:T(1,128)} %bitcast.7, s32[1,256]{1,0:T(1,128)} %order_ref.1), custom_call_target="tpu_custom_call" | custom-call | tf_op jit(solution)/shard_map/pallas_call | solution.py:796
  3.8 5.6 %collective-permute-start = (f32[2,64,128]{2,1,0:T(8,128)S(1)}, f32[2,64,128]{2,1,0:T(8,128)S(1)}, u32[]{:S(2)}, u32[]{:S(2)}) collective-permute-start(f32[2,64,128]{2,1,0:T(8,128)S(1)} %get-tuple-element.38), channel_id=1, source_target_pairs={{0,31},{1,2},{2,1},{3,4},{4,3},{5,6},{6,5},{7,8},{8,7},{9,10},{10,... | collective-permute-start | bytes 196616 | tf_op jit(solution)/shard_map/ppermute | solution.py:780
  9.3 0.0 collective-permute-start.1
  9.3 0.0 copy-start
  9.3 2.6 %all-to-all-start = ((f32[32,3,2,128]{3,2,1,0:T(2,128)}), f32[32,3,2,128]{3,2,1,0:T(2,128)S(1)}, u32[]{:S(2)}, u32[]{:S(2)}) async-start(f32[32,3,2,128]{3,2,1,0:T(2,128)} %bitcast.1), calls=%async_computation | async-start | bytes 196608 | tf_op jit(solution)/shard_map/all_to_all | solution.py:785
  11.9 0.0 collective-permute-done.far_in_ref
  12.0 0.0 collective-permute-done.1.near_in_ref
  12.0 0.0 copy-done
  12.0 1.1 %shard_map.61 = (f32[2,512,128]{2,1,0:T(8,128)S(1)}, f32[2,512,128]{2,1,0:T(8,128)S(1)}, f32[2,512,128]{2,1,0:T(8,128)S(1)}, f32[8,256]{1,0:T(8,128)S(1)}, f32[8...) custom-call(f32[2,512,128]{2,1,0:T(8,128)S(1)} %get-tuple-element.35, ...), custom_call_target="tpu_custom_call", output_to_operand_aliasing={{0}: (0, {})} | custom-call | flops 99999997952 | bytes 268435456 | tf_op jit(solution)/shard_map/pallas_call | solution.py:810
  13.0 5.3 %collective-permute-start.2 = (f32[2,64,128]{2,1,0:T(8,128)S(1)}, f32[2,64,128]{2,1,0:T(8,128)S(1)}, u32[]{:S(2)}, u32[]{:S(2)}) collective-permute-start(f32[2,64,128]{2,1,0:T(8,128)S(1)} %get-tuple-element.49), channel_id=1, source_target_pairs={{0,31},{1,2},{2,1},{3,4},{4,3},{5,6},{6,5},{7,8},{8,7},{9,10},{10,... | collective-permute-start | bytes 196616 | tf_op jit(solution)/shard_map/ppermute | solution.py:780
  18.3 0.0 collective-permute-start.3
  18.3 1.6 %all-to-all-done = f32[32,3,2,128]{3,2,1,0:T(2,128)S(1)} async-done(((f32[32,3,2,128]{3,2,1,0:T(2,128)}), f32[32,3,2,128]{3,2,1,0:T(2,128)S(1)}, u32[]{:S(2)}, u32[]{:S(2)}) %all-to-all-start) | async-done | bytes 98336 | tf_op jit(solution)/shard_map/all_to_all | solution.py:785
  19.9 1.8 %shard_map.62 = (f32[32,256]{1,0:T(8,128)S(1)}, f32[32,256]{1,0:T(8,128)S(1)}, f32[32,256]{1,0:T(8,128)S(1)}, f32[32,256]{1,0:T(8,128)S(1)}, f32[2,512,128]{2,1,0:T(8,128)S(1)}) custom-call(f32[192,128]{1,0:T(8,128)S(1)} %bitcast.6, f32[8,256]{1,0:T(8,128)S(1)} %get-tuple-element.40.layers_ref), custom_call_target="tpu_custom_call" | custom-call | tf_op jit(solution)/shard_map/pallas_call | solution.py:814
  21.7 1.5 %shard_map.63 = (f32[2,512,128]{2,1,0:T(8,128)S(1)}, f32[2,512,128]{2,1,0:T(8,128)S(1)}, f32[48,256]{1,0:T(8,128)S(1)}, f32[8,256]{1,0:T(8,128)S(1)}, f32[128,256]{1,0:T(8,128)S(1)}, /*index=5*/f32[128,256]{1,0:T(8,128)S(1)}) custom-call(f32[2,512,128]{2,1,0:T(8,128)S(1)} %get-tuple-element.42.image_ref.first_ref, ...), custom_call_target="tpu_custom_call", output_to_operand_aliasing={{0}: (1, {})} | custom-call | tf_op jit(solution)/shard_map/pallas_call | solution.py:815
  23.2 0.0 collective-permute-done.2.far_in_ref
  23.2 0.0 collective-permute-done.3.near_in_ref
  23.2 1.3 %shard_map.64 = (f32[128,256]{1,0:T(8,128)S(1)}, f32[2,56,128]{2,1,0:T(8,128)S(1)}, f32[2,56,128]{2,1,0:T(8,128)S(1)}, f32[224,128]{1,0:T(8,128)}) custom-call(f32[2,512,128]{2,1,0:T(8,128)S(1)} %get-tuple-element.42.image_ref.first_ref, f32[2,512,128]{2,1,0:T(8,128)S(1)} %get-tuple-element.46.scaled_change_ref.first_scaled_ref, ...), custom_call_target="tpu_custom_call" | custom-call | tf_op jit(solution)/shard_map/pallas_call | solution.py:818
  24.5 2.8 %all-to-all-start.1 = ((f32[32,7,1,128]{3,2,1,0:T(1,128)}), f32[32,7,1,128]{3,2,1,0:T(1,128)S(1)}, u32[]{:S(2)}, u32[]{:S(2)}) async-start(f32[32,7,1,128]{3,2,1,0:T(1,128)} %bitcast.3), calls=%async_computation.1 | async-start | bytes 229376 | tf_op jit(solution)/shard_map/all_to_all | solution.py:785
  27.3 5.3 %collective-permute-start.4 = (f32[2,56,128]{2,1,0:T(8,128)S(1)}, f32[2,56,128]{2,1,0:T(8,128)S(1)}, u32[]{:S(2)}, u32[]{:S(2)}) collective-permute-start(f32[2,56,128]{2,1,0:T(8,128)S(1)} %get-tuple-element.65), channel_id=1, source_target_pairs={{0,31},{1,2},{2,1},{3,4},{4,3},{5,6},{6,5},{7,8},{8,7},{9,10},{10,... | collective-permute-start | bytes 172040 | tf_op jit(solution)/shard_map/ppermute | solution.py:780
  32.6 0.0 collective-permute-start.5
  32.6 1.4 %shard_map.65 = (f32[2,512,128]{2,1,0:T(8,128)S(1)}, f32[2,512,128]{2,1,0:T(8,128)S(1)}, f32[2,512,128]{2,1,0:T(8,128)S(1)}, f32[2,512,128]{2,1,0:T(8,128)S(1)},...) custom-call(f32[2,512,128]{2,1,0:T(8,128)S(1)} %get-tuple-element.42, ...), custom_call_target="tpu_custom_call", output_to_operand_aliasing={{0}: (0, {}), {1}: (1, {}), {2}: (2, {}), {3}: (3, {})} | custom-call | tf_op jit(solution)/shard_map/pallas_call | solution.py:823
  34.0 2.3 %collective-permute-done.4.far_ref = f32[2,56,128]{2,1,0:T(8,128)S(1)} collective-permute-done((f32[2,56,128]{2,1,0:T(8,128)S(1)}, f32[2,56,128]{2,1,0:T(8,128)S(1)}, u32[]{:S(2)}, u32[]{:S(2)}) %collective-permute-start.4) | collective-permute-done | bytes 57376 | tf_op jit(solution)/shard_map/ppermute | solution.py:780
  36.3 0.0 collective-permute-done.5.near_ref
  36.3 0.0 all-to-all-done.1
  36.3 3.0 %shard_map.66 = (f32[256,512]{1,0:T(8,128)}, f32[256,512]{1,0:T(8,128)}) custom-call(f32[32,256]{1,0:T(8,128)S(1)} %get-tuple-element.41.coeff_ref, f32[224,128]{1,0:T(8,128)S(1)} %bitcast.5, f32[32,256]{1,0:T(8,128)S(1)} %get-tuple-element.56.vert_ref.first_ref, f32[32,256]{1,0:T(8,128)S(1)} %get-tuple-element.58.applied_ref, ...), custom_call_target="tpu_custom_call" | custom-call | tf_op jit(solution)/shard_map/pallas_call | solution.py:829
  (1 shorter events, 0.0 us)
Async XLA Ops:
  3.8 8.2 %collective-permute-start = (f32[2,64,128]{2,1,0:T(8,128)S(1)}, f32[2,64,128]{2,1,0:T(8,128)S(1)}, u32[]{:S(2)}, u32[]{:S(2)}) collective-permute-start(f32[2,64,128]{2,1,0:T(8,128)S(1)} %get-tuple-element.38), channel_id=1, source_target_pairs={{0,31},{1,2},{2,1},{3,4},{4,3},{5,6},{6,5},{7,8},{8,7},{9,10},{10,... | collective-permute-start | bytes 196616 | tf_op jit(solution)/shard_map/ppermute | solution.py:780
  9.3 2.6 %collective-permute-start.1 = (f32[2,64,128]{2,1,0:T(8,128)S(1)}, f32[2,64,128]{2,1,0:T(8,128)S(1)}, u32[]{:S(2)}, u32[]{:S(2)}) collective-permute-start(f32[2,64,128]{2,1,0:T(8,128)S(1)} %get-tuple-element.39), channel_id=1, source_target_pairs={{0,1},{1,0},{2,3},{3,2},{4,5},{5,4},{6,7},{7,6},{8,9},{9,8},{10,11... | collective-permute-start | bytes 196616 | tf_op jit(solution)/shard_map/ppermute | solution.py:780
  9.3 2.6 %copy-start = (bf16[64,384]{1,0:T(8,128)(2,1)S(1)}, bf16[64,384]{1,0:T(8,128)(2,1)}, u32[]{:S(2)}) copy-start(bf16[64,384]{1,0:T(8,128)(2,1)} %constant.2.clone.table_ref) | copy-start | bytes 147460
  9.3 10.6 %all-to-all-start = ((f32[32,3,2,128]{3,2,1,0:T(2,128)}), f32[32,3,2,128]{3,2,1,0:T(2,128)S(1)}, u32[]{:S(2)}, u32[]{:S(2)}) async-start(f32[32,3,2,128]{3,2,1,0:T(2,128)} %bitcast.1), calls=%async_computation | async-start | bytes 196608 | tf_op jit(solution)/shard_map/all_to_all | solution.py:785
  13.0 10.1 %collective-permute-start.2 = (f32[2,64,128]{2,1,0:T(8,128)S(1)}, f32[2,64,128]{2,1,0:T(8,128)S(1)}, u32[]{:S(2)}, u32[]{:S(2)}) collective-permute-start(f32[2,64,128]{2,1,0:T(8,128)S(1)} %get-tuple-element.49), channel_id=1, source_target_pairs={{0,31},{1,2},{2,1},{3,4},{4,3},{5,6},{6,5},{7,8},{8,7},{9,10},{10,... | collective-permute-start | bytes 196616 | tf_op jit(solution)/shard_map/ppermute | solution.py:780
  18.3 4.9 %collective-permute-start.3 = (f32[2,64,128]{2,1,0:T(8,128)S(1)}, f32[2,64,128]{2,1,0:T(8,128)S(1)}, u32[]{:S(2)}, u32[]{:S(2)}) collective-permute-start(f32[2,64,128]{2,1,0:T(8,128)S(1)} %get-tuple-element.50), channel_id=1, source_target_pairs={{0,1},{1,0},{2,3},{3,2},{4,5},{5,4},{6,7},{7,6},{8,9},{9,8},{10,11... | collective-permute-start | bytes 196616 | tf_op jit(solution)/shard_map/ppermute | solution.py:780
  24.5 11.8 %all-to-all-start.1 = ((f32[32,7,1,128]{3,2,1,0:T(1,128)}), f32[32,7,1,128]{3,2,1,0:T(1,128)S(1)}, u32[]{:S(2)}, u32[]{:S(2)}) async-start(f32[32,7,1,128]{3,2,1,0:T(1,128)} %bitcast.3), calls=%async_computation.1 | async-start | bytes 229376 | tf_op jit(solution)/shard_map/all_to_all | solution.py:785
  27.3 9.0 %collective-permute-start.4 = (f32[2,56,128]{2,1,0:T(8,128)S(1)}, f32[2,56,128]{2,1,0:T(8,128)S(1)}, u32[]{:S(2)}, u32[]{:S(2)}) collective-permute-start(f32[2,56,128]{2,1,0:T(8,128)S(1)} %get-tuple-element.65), channel_id=1, source_target_pairs={{0,31},{1,2},{2,1},{3,4},{4,3},{5,6},{6,5},{7,8},{8,7},{9,10},{10,... | collective-permute-start | bytes 172040 | tf_op jit(solution)/shard_map/ppermute | solution.py:780
  32.6 3.7 %collective-permute-start.5 = (f32[2,56,128]{2,1,0:T(8,128)S(1)}, f32[2,56,128]{2,1,0:T(8,128)S(1)}, u32[]{:S(2)}, u32[]{:S(2)}) collective-permute-start(f32[2,56,128]{2,1,0:T(8,128)S(1)} %get-tuple-element.66), channel_id=1, source_target_pairs={{0,1},{1,0},{2,3},{3,2},{4,5},{5,4},{6,7},{7,6},{8,9},{9,8},{10,11... | collective-permute-start | bytes 172040 | tf_op jit(solution)/shard_map/ppermute | solution.py:780

commit v5 on v4

--- a/solution.py
+++ b/solution.py
@@ -414,20 +414,21 @@
     ]
     for copy in small + parts:
         copy.start()
-    for copy in small:
+    for copy in small + parts:
         copy.wait()
     order = held_order[...]
     choose = selection(order)
-    coeff = jnp.zeros((8, PLANE), F32)
-    for piece in pieces(jnp.broadcast_to(held_kappa[...], (8, PLANE))):
-        coeff = coeff + lax.dot_general(piece, choose, (((1,), (1,)), ((), ())), preferred_element_type=F32)
+    choose = jnp.concatenate([choose] * 3, axis=1)
+    coeff = lax.dot_general(
+        jnp.concatenate(pieces(jnp.broadcast_to(held_kappa[...], (8, PLANE))), axis=1),
+        choose,
+        (((1,), (1,)), ((), ())),
+        preferred_element_type=F32,
+    )
     own = jnp.concatenate([coeff[0:3], order.astype(F32), coeff[4:8]], axis=0)
     own_ref[...] = own
-    for k, copy in enumerate(parts):
-        copy.wait()
-        load = jnp.zeros((PLANE, 256), F32)
-        for piece in pieces(held[k]):
-            load = load + jnp.dot(choose, piece, preferred_element_type=F32)
+    for k in range(2):
+        load = jnp.dot(choose, jnp.concatenate(pieces(held[k]), axis=0), preferred_element_type=F32)
         put(load_ref, slice(256 * k, 256 * k + 256), load.T)
     sum_xy(load_ref)
     faces_out(load_ref, near_ref, far_ref)
@@ -697,16 +698,18 @@
 
 
 def to_stored(choose, value):
-    total = jnp.zeros((choose.shape[0], value.shape[0]), F32)
-    for piece in pieces(value)[1:]:
-        total = total + lax.dot_general(choose, piece, (((1,), (1,)), ((), ())), preferred_element_type=F32)
-    return total
-
-
-def closing(
-    coeff_ref, step_ref, first_ref, applied_ref, target_ref, scale_ref, layers_ref,
-    resid_ref, z_ref, image_ref, scaled_change_ref, change_ref, far_ref, near_ref, choose_ref,
-    solution_ref, residual_ref, vert_ref, grid_ref, sum_ref, edge_ref, held, sems,
+    return lax.dot_general(
+        jnp.concatenate([choose] * 2, axis=1),
+        jnp.concatenate(pieces(value)[1:], axis=1),
+        (((1,), (1,)), ((), ())),
+        preferred_element_type=F32,
+    )
+
+
+def second_step(
+    resid_ref, coeff_ref, step_ref, first_ref, applied_ref, target_ref, scale_ref, layers_ref,
+    z_ref, image_ref, scaled_change_ref, change_ref, choose_ref,
+    rest_ref, found_ref, scalars_ref, vert_ref, grid_ref, sum_ref, edge_ref,
 ):
     modes = coarse_modes(coeff_ref[...])
     target, first, applied = target_ref[...], first_ref[...], applied_ref[...]
@@ -735,23 +738,31 @@
     )
     cross = total(sums[1] - alpha * sums[2], vert * image)
     smooth_image(smooths, sum_ref, edge_ref)
-    sum_ref[...] += change_ref[...]
-    faces_in(sum_ref, near_ref, far_ref)
     beta = progress / gamma
     alpha_next = progress / (second + beta * (2.0 * cross + beta * energy))
     share, change_share = alpha + alpha_next * beta + alpha_next, alpha_next * alpha
-    choose, every = choose_ref[...], slice(0, 512)
+    scalars_ref[...] = jnp.broadcast_to(change_share, scalars_ref.shape)
     for nz in range(8):
         for ny in range(8):
             rows = rows_of(nz, ny)
             other = get(scaled_change_ref, rows) + smooths[0].value(nz, ny)
             grid_ref[rows, :] = share * get(z_ref, rows) - change_share * other
-    held[0] = to_stored(choose, grid_ref[...])
-    sum_ref[...] = resid_ref[...] - share[None] * image_ref[...] + change_share[None] * sum_ref[...]
-    copies = [pltpu.make_async_copy(held.at[0], solution_ref, sems.at[0])]
+    found_ref[...] = to_stored(choose_ref[...], grid_ref[...])
+    rest_ref[...] = (
+        resid_ref[...] - share[None] * image_ref[...] + change_share[None] * (change_ref[...] + sum_ref[...])
+    )
+
+
+def closing(
+    found_ref, rest_ref, far_ref, near_ref, scalars_ref, choose_ref, solution_ref, residual_ref, sum_ref, held, sems
+):
+    copies = [pltpu.make_async_copy(found_ref, solution_ref, sems.at[0])]
     copies[0].start()
-    held[1] = to_stored(choose, get(sum_ref, every))
-    copies.append(pltpu.make_async_copy(held.at[1], residual_ref, sems.at[1]))
+    sum_ref[...] = rest_ref[...]
+    for rows, ref in zip(face_rows(sum_ref), (near_ref, far_ref)):
+        put(sum_ref, rows, get(sum_ref, rows) + scalars_ref[0:1, 0:1] * face_in(ref))
+    held[...] = to_stored(choose_ref[...], get(sum_ref, slice(0, 512)))
+    copies.append(pltpu.make_async_copy(held, residual_ref, sems.at[1]))
     copies[1].start()
     for copy in copies:
         copy.wait()
@@ -826,9 +837,11 @@
         [(2, 256, 128), nodes, edge],
         in_place={0: 0, 1: 1, 2: 2, 3: 3},
     )(image, scaled_change, change, scaled, far, near, added, layers, coeff, vert)
-    found, left = call(closing, [stored, stored], [grid, flat, nodes, edge, (2,) + stored], 2, hbm_out=(0, 1))(
-        coeff, step, vert, applied, target, scale, layers,
-        resid, z, image, scaled_change, change, next_far, next_near, choose,
+    rest, found, scalars = call(
+        second_step, [nodes, stored, (8, 128)], [grid, flat, nodes, edge], in_place={0: 0}
+    )(resid, coeff, step, vert, applied, target, scale, layers, z, image, scaled_change, change, choose)
+    found, left = call(closing, [stored, stored], [nodes, stored], 2, hbm_out=(0, 1))(
+        found, rest, next_far, next_near, scalars, choose
     )
     return found, left
 

time: 39.6 us -> 39.2 us (0.990)
  waiting for transfers between devices: 3.93 us -> 3.01 us
    ppermute x6, waiting for transfers between devices: 2.33 us -> 0.02 us  [swapped(): lax.ppermute(x, AXES, [(i, (i + (1 if (i % 2 == 0) != far else -1)) % siz...]
    all_to_all x2, waiting for transfers between devices: 1.6 us -> 3 us  [everyone(): lax.all_to_all(payload.reshape((devices,) + shape), AXES, 0, 0, tiled=True)]
    pallas_call x1 -> x2, Pallas kernels: 2.97 us -> 3.29 us  [the longest x1 2.04 us: per_device(): call(second_step, [nodes, stored, (8, 128)], [grid, flat, nodes, edge], i...]
  transfers between devices with their start and end apart: 8 -> 8, of which waited for: 2 -> 2; matrix products, arithmetic and copies ran while one was open for 0% -> 0% of each run, Pallas kernels for 15% -> 20%
where the time goes in v5:
time: 39.2 us; the launch traced here: 38.6 us
  starting transfers between devices  21.5 us (55%)
  Pallas kernels  13.3 us (34%)
  waiting for transfers between devices  3.01 us (8%)
  between operations  0.75 us (2%)
    ppermute x6, starting transfers between devices, swapped(): lax.ppermute(x, AXES, [(i, (i + (1 if (i % 2 == 0) != far else -1)) % siz...  16.1 us
    all_to_all x2, starting transfers between devices, everyone(): lax.all_to_all(payload.reshape((devices,) + shape), AXES, 0, 0, tiled=True)  5.37 us
    all_to_all x2, waiting for transfers between devices, everyone(): lax.all_to_all(payload.reshape((devices,) + shape), AXES, 0, 0, tiled=True)  3 us
    pallas_call x1, Pallas kernels, per_device(): call(opening, [nodes, face_row, face_row, plane, payload_rows], [(2, PLAN...  2.94 us
    pallas_call x1, Pallas kernels, per_device(): call(second_step, [nodes, stored, (8, 128)], [grid, flat, nodes, edge], i...  2.04 us
    pallas_call x1, Pallas kernels, per_device(): call(first_coarse, [grid] * 4 + [nodes], [edge])(gather, layers)  1.8 us
    pallas_call x1, Pallas kernels, per_device(): call(second_rough, [nodes] * 2 + [(48, PLANE), plane, (128, PLANE), (128,...  1.46 us
    pallas_call x1, Pallas kernels, per_device(): call(complete, [nodes] * 4 + [choice, grid], [(2, 256, 128), nodes, edge]...  1.4 us
  transfers between devices with their start and end apart: 8, of which 2 were waited for; matrix products, arithmetic and copies ran while one was open for 0% of the time, Pallas kernels for 20%

profile of v5, /device:TPU:0, one launch (start us, length us, event | category | flops | bytes accessed | tf_op | source)
XLA Modules:
  0.0 38.6 jit_solution(9365186834002042352)
XLA Ops:
  0.6 2.9 %shard_map.59 = (f32[2,512,128]{2,1,0:T(8,128)S(1)}, f32[2,64,128]{2,1,0:T(8,128)S(1)}, f32[2,64,128]{2,1,0:T(8,128)S(1)}, f32[8,256]{1,0:T(8,128)S(1)}, f32[192,128]{1,0:T(8,128)}) custom-call(f32[256,512]{1,0:T(8,128)} %forcing_ref.1, f32[1,256]{1,0:T(1,128)} %bitcast.7, s32[1,256]{1,0:T(1,128)} %order_ref.1), custom_call_target="tpu_custom_call" | custom-call | tf_op jit(solution)/shard_map/pallas_call | solution.py:807
  3.6 5.6 %collective-permute-start = (f32[2,64,128]{2,1,0:T(8,128)S(1)}, f32[2,64,128]{2,1,0:T(8,128)S(1)}, u32[]{:S(2)}, u32[]{:S(2)}) collective-permute-start(f32[2,64,128]{2,1,0:T(8,128)S(1)} %get-tuple-element.39), channel_id=1, source_target_pairs={{0,31},{1,2},{2,1},{3,4},{4,3},{5,6},{6,5},{7,8},{8,7},{9,10},{10,... | collective-permute-start | bytes 196616 | tf_op jit(solution)/shard_map/ppermute | solution.py:791
  9.1 0.0 collective-permute-start.1
  9.2 0.0 copy-start
  9.2 2.6 %all-to-all-start = ((f32[32,3,2,128]{3,2,1,0:T(2,128)}), f32[32,3,2,128]{3,2,1,0:T(2,128)S(1)}, u32[]{:S(2)}, u32[]{:S(2)}) async-start(f32[32,3,2,128]{3,2,1,0:T(2,128)} %bitcast.1), calls=%async_computation | async-start | bytes 196608 | tf_op jit(solution)/shard_map/all_to_all | solution.py:796
  11.8 0.0 collective-permute-done.far_in_ref
  11.8 0.0 collective-permute-done.1.near_in_ref
  11.8 0.0 copy-done
  11.8 1.1 %shard_map.60 = (f32[2,512,128]{2,1,0:T(8,128)S(1)}, f32[2,512,128]{2,1,0:T(8,128)S(1)}, f32[2,512,128]{2,1,0:T(8,128)S(1)}, f32[8,256]{1,0:T(8,128)S(1)}, f32[8...) custom-call(f32[2,512,128]{2,1,0:T(8,128)S(1)} %get-tuple-element.38, ...), custom_call_target="tpu_custom_call", output_to_operand_aliasing={{0}: (0, {})} | custom-call | flops 99999997952 | bytes 268435456 | tf_op jit(solution)/shard_map/pallas_call | solution.py:821
  12.9 5.3 %collective-permute-start.2 = (f32[2,64,128]{2,1,0:T(8,128)S(1)}, f32[2,64,128]{2,1,0:T(8,128)S(1)}, u32[]{:S(2)}, u32[]{:S(2)}) collective-permute-start(f32[2,64,128]{2,1,0:T(8,128)S(1)} %get-tuple-element.52), channel_id=1, source_target_pairs={{0,31},{1,2},{2,1},{3,4},{4,3},{5,6},{6,5},{7,8},{8,7},{9,10},{10,... | collective-permute-start | bytes 196616 | tf_op jit(solution)/shard_map/ppermute | solution.py:791
  18.1 0.0 collective-permute-start.3
  18.1 1.6 %all-to-all-done = f32[32,3,2,128]{3,2,1,0:T(2,128)S(1)} async-done(((f32[32,3,2,128]{3,2,1,0:T(2,128)}), f32[32,3,2,128]{3,2,1,0:T(2,128)S(1)}, u32[]{:S(2)}, u32[]{:S(2)}) %all-to-all-start) | async-done | bytes 98336 | tf_op jit(solution)/shard_map/all_to_all | solution.py:796
  19.7 1.8 %shard_map.62 = (f32[32,256]{1,0:T(8,128)S(1)}, f32[32,256]{1,0:T(8,128)S(1)}, f32[32,256]{1,0:T(8,128)S(1)}, f32[32,256]{1,0:T(8,128)S(1)}, f32[2,512,128]{2,1,0:T(8,128)S(1)}) custom-call(f32[192,128]{1,0:T(8,128)S(1)} %bitcast.6, f32[8,256]{1,0:T(8,128)S(1)} %get-tuple-element.44.layers_ref), custom_call_target="tpu_custom_call" | custom-call | tf_op jit(solution)/shard_map/pallas_call | solution.py:825
  21.5 1.5 %shard_map.63 = (f32[2,512,128]{2,1,0:T(8,128)S(1)}, f32[2,512,128]{2,1,0:T(8,128)S(1)}, f32[48,256]{1,0:T(8,128)S(1)}, f32[8,256]{1,0:T(8,128)S(1)}, f32[128,256]{1,0:T(8,128)S(1)}, /*index=5*/f32[128,256]{1,0:T(8,128)S(1)}) custom-call(f32[2,512,128]{2,1,0:T(8,128)S(1)} %get-tuple-element.46.image_ref.first_ref, ...), custom_call_target="tpu_custom_call", output_to_operand_aliasing={{0}: (1, {})} | custom-call | tf_op jit(solution)/shard_map/pallas_call | solution.py:826
  23.0 0.0 collective-permute-done.2.far_in_ref
  23.0 0.0 collective-permute-done.3.near_in_ref
  23.0 1.3 %shard_map.64 = (f32[128,256]{1,0:T(8,128)S(1)}, f32[2,56,128]{2,1,0:T(8,128)S(1)}, f32[2,56,128]{2,1,0:T(8,128)S(1)}, f32[224,128]{1,0:T(8,128)}) custom-call(f32[2,512,128]{2,1,0:T(8,128)S(1)} %get-tuple-element.46.image_ref.first_ref, f32[2,512,128]{2,1,0:T(8,128)S(1)} %get-tuple-element.49.scaled_change_ref.first_scaled_ref, ...), custom_call_target="tpu_custom_call" | custom-call | tf_op jit(solution)/shard_map/pallas_call | solution.py:829
  24.4 2.8 %all-to-all-start.1 = ((f32[32,7,1,128]{3,2,1,0:T(1,128)}), f32[32,7,1,128]{3,2,1,0:T(1,128)S(1)}, u32[]{:S(2)}, u32[]{:S(2)}) async-start(f32[32,7,1,128]{3,2,1,0:T(1,128)} %bitcast.3), calls=%async_computation.1 | async-start | bytes 229376 | tf_op jit(solution)/shard_map/all_to_all | solution.py:796
  27.1 5.3 %collective-permute-start.4 = (f32[2,56,128]{2,1,0:T(8,128)S(1)}, f32[2,56,128]{2,1,0:T(8,128)S(1)}, u32[]{:S(2)}, u32[]{:S(2)}) collective-permute-start(f32[2,56,128]{2,1,0:T(8,128)S(1)} %get-tuple-element.71), channel_id=1, source_target_pairs={{0,31},{1,2},{2,1},{3,4},{4,3},{5,6},{6,5},{7,8},{8,7},{9,10},{10,... | collective-permute-start | bytes 172040 | tf_op jit(solution)/shard_map/ppermute | solution.py:791
  32.4 0.0 collective-permute-start.5
  32.4 1.4 %shard_map.65 = (f32[2,512,128]{2,1,0:T(8,128)S(1)}, f32[2,512,128]{2,1,0:T(8,128)S(1)}, f32[2,512,128]{2,1,0:T(8,128)S(1)}, f32[2,512,128]{2,1,0:T(8,128)S(1)},...) custom-call(f32[2,512,128]{2,1,0:T(8,128)S(1)} %get-tuple-element.46, ...), custom_call_target="tpu_custom_call", output_to_operand_aliasing={{0}: (0, {}), {1}: (1, {}), {2}: (2, {}), {3}: (3, {})} | custom-call | tf_op jit(solution)/shard_map/pallas_call | solution.py:834
  33.8 1.4 %all-to-all-done.1 = f32[32,7,1,128]{3,2,1,0:T(1,128)S(1)} async-done(((f32[32,7,1,128]{3,2,1,0:T(1,128)}), f32[32,7,1,128]{3,2,1,0:T(1,128)S(1)}, u32[]{:S(2)}, u32[]{:S(2)}) %all-to-all-start.1) | async-done | bytes 114720 | tf_op jit(solution)/shard_map/all_to_all | solution.py:796
  35.2 2.0 %shard_map.66 = (f32[2,512,128]{2,1,0:T(8,128)S(1)}, f32[256,512]{1,0:T(8,128)S(1)}, f32[8,128]{1,0:T(8,128)S(1)}) custom-call(f32[2,512,128]{2,1,0:T(8,128)S(1)} %get-tuple-element.42.resid_ref, f32[32,256]{1,0:T(8,128)S(1)} %get-tuple-element.45.coeff_ref, f32[224,128]{1,0:T(8,128)S(1)} %bitcast.5, ...), custom_call_target="tpu_custom_call", output_to_operand_aliasing={{0}: (0, {})} | custom-call | tf_op jit(solution)/shard_map/pallas_call | solution.py:840
  37.3 0.0 collective-permute-done.4.far_ref
  37.3 0.0 collective-permute-done.5.near_ref
  37.3 1.2 %shard_map.67 = (f32[256,512]{1,0:T(8,128)}, f32[256,512]{1,0:T(8,128)}) custom-call(f32[256,512]{1,0:T(8,128)S(1)} %get-tuple-element.69.found_ref, f32[2,512,128]{2,1,0:T(8,128)S(1)} %get-tuple-element.70.rest_ref, f32[2,56,128]{2,1,0:T(8,128)S(1)} %collective-permute-done.4.far_ref, f32[2,56,128]{2,1,0:T(8,128)S(1)} %collective-permute-done.5.near_ref, ...), custom_call_target="tpu_custom_call" | custom-call | tf_op jit(solution)/shard_map/pallas_call | solution.py:843
  (1 shorter events, 0.0 us)
Async XLA Ops:
  3.6 8.2 %collective-permute-start = (f32[2,64,128]{2,1,0:T(8,128)S(1)}, f32[2,64,128]{2,1,0:T(8,128)S(1)}, u32[]{:S(2)}, u32[]{:S(2)}) collective-permute-start(f32[2,64,128]{2,1,0:T(8,128)S(1)} %get-tuple-element.39), channel_id=1, source_target_pairs={{0,31},{1,2},{2,1},{3,4},{4,3},{5,6},{6,5},{7,8},{8,7},{9,10},{10,... | collective-permute-start | bytes 196616 | tf_op jit(solution)/shard_map/ppermute | solution.py:791
  9.1 2.6 %collective-permute-start.1 = (f32[2,64,128]{2,1,0:T(8,128)S(1)}, f32[2,64,128]{2,1,0:T(8,128)S(1)}, u32[]{:S(2)}, u32[]{:S(2)}) collective-permute-start(f32[2,64,128]{2,1,0:T(8,128)S(1)} %get-tuple-element.40), channel_id=1, source_target_pairs={{0,1},{1,0},{2,3},{3,2},{4,5},{5,4},{6,7},{7,6},{8,9},{9,8},{10,11... | collective-permute-start | bytes 196616 | tf_op jit(solution)/shard_map/ppermute | solution.py:791
  9.2 2.6 %copy-start = (bf16[64,384]{1,0:T(8,128)(2,1)S(1)}, bf16[64,384]{1,0:T(8,128)(2,1)}, u32[]{:S(2)}) copy-start(bf16[64,384]{1,0:T(8,128)(2,1)} %constant.2.clone.table_ref) | copy-start | bytes 147460
  9.2 10.5 %all-to-all-start = ((f32[32,3,2,128]{3,2,1,0:T(2,128)}), f32[32,3,2,128]{3,2,1,0:T(2,128)S(1)}, u32[]{:S(2)}, u32[]{:S(2)}) async-start(f32[32,3,2,128]{3,2,1,0:T(2,128)} %bitcast.1), calls=%async_computation | async-start | bytes 196608 | tf_op jit(solution)/shard_map/all_to_all | solution.py:796
  12.9 10.1 %collective-permute-start.2 = (f32[2,64,128]{2,1,0:T(8,128)S(1)}, f32[2,64,128]{2,1,0:T(8,128)S(1)}, u32[]{:S(2)}, u32[]{:S(2)}) collective-permute-start(f32[2,64,128]{2,1,0:T(8,128)S(1)} %get-tuple-element.52), channel_id=1, source_target_pairs={{0,31},{1,2},{2,1},{3,4},{4,3},{5,6},{6,5},{7,8},{8,7},{9,10},{10,... | collective-permute-start | bytes 196616 | tf_op jit(solution)/shard_map/ppermute | solution.py:791
  18.1 4.9 %collective-permute-start.3 = (f32[2,64,128]{2,1,0:T(8,128)S(1)}, f32[2,64,128]{2,1,0:T(8,128)S(1)}, u32[]{:S(2)}, u32[]{:S(2)}) collective-permute-start(f32[2,64,128]{2,1,0:T(8,128)S(1)} %get-tuple-element.53), channel_id=1, source_target_pairs={{0,1},{1,0},{2,3},{3,2},{4,5},{5,4},{6,7},{7,6},{8,9},{9,8},{10,11... | collective-permute-start | bytes 196616 | tf_op jit(solution)/shard_map/ppermute | solution.py:791
  24.4 10.9 %all-to-all-start.1 = ((f32[32,7,1,128]{3,2,1,0:T(1,128)}), f32[32,7,1,128]{3,2,1,0:T(1,128)S(1)}, u32[]{:S(2)}, u32[]{:S(2)}) async-start(f32[32,7,1,128]{3,2,1,0:T(1,128)} %bitcast.3), calls=%async_computation.1 | async-start | bytes 229376 | tf_op jit(solution)/shard_map/all_to_all | solution.py:796
  27.1 10.2 %collective-permute-start.4 = (f32[2,56,128]{2,1,0:T(8,128)S(1)}, f32[2,56,128]{2,1,0:T(8,128)S(1)}, u32[]{:S(2)}, u32[]{:S(2)}) collective-permute-start(f32[2,56,128]{2,1,0:T(8,128)S(1)} %get-tuple-element.71), channel_id=1, source_target_pairs={{0,31},{1,2},{2,1},{3,4},{4,3},{5,6},{6,5},{7,8},{8,7},{9,10},{10,... | collective-permute-start | bytes 172040 | tf_op jit(solution)/shard_map/ppermute | solution.py:791
  32.4 4.9 %collective-permute-start.5 = (f32[2,56,128]{2,1,0:T(8,128)S(1)}, f32[2,56,128]{2,1,0:T(8,128)S(1)}, u32[]{:S(2)}, u32[]{:S(2)}) collective-permute-start(f32[2,56,128]{2,1,0:T(8,128)S(1)} %get-tuple-element.72), channel_id=1, source_target_pairs={{0,1},{1,0},{2,3},{3,2},{4,5},{5,4},{6,7},{7,6},{8,9},{9,8},{10,11... | collective-permute-start | bytes 172040 | tf_op jit(solution)/shard_map/ppermute | solution.py:791

commit v6 on v2

--- a/solution.py
+++ b/solution.py
@@ -73,7 +73,7 @@
 DIAG = np.diag(STIFF)
 ENDS = np.array([2.0] + [1.0] * 6 + [2.0])
 MASS = np.diag(WEIGHTS)
-STIFF_XY = np.tile(np.kron(MASS, STIFF) + np.kron(STIFF, MASS), (1, 2))
+STIFF_XY = np.kron(MASS, STIFF) + np.kron(STIFF, MASS)
 STIFF_PARTS = []
 for part in range(3):
     STIFF_PARTS.append((STIFF_XY - sum(STIFF_PARTS)).astype(ml_dtypes.bfloat16).astype(np.float64))
@@ -326,23 +326,16 @@
     return 0 if node == 0 else (2 if node == 7 else 1)
 
 
-def product(tables, values):
+def product(table, values):
     low, middle, high = pieces(values)
-
-    def dot(k, right):
-        return jnp.dot(tables[k], right, preferred_element_type=F32)
-
-    return dot(0, high) + ((dot(0, middle) + dot(1, high)) + (dot(1, middle) + (dot(0, low) + dot(2, high))))
+    stacked = jnp.concatenate([high, middle, high, middle, low, high], axis=0)
+    return jnp.dot(table, stacked, preferred_element_type=F32)
 
 
 def operate(z_ref, xy_ref, out_ref, table_ref, coeff, weight_x):
-    row, col = (lax.broadcasted_iota(jnp.int32, (256, 256), axis) for axis in range(2))
-    tables = [
-        jnp.where(row // 64 == col // 64, jnp.tile(table_ref[k].astype(F32), (4, 2)), 0.0).astype(jnp.bfloat16) for k in range(3)
-    ]
-    for half in range(2):
-        rows = slice(half * 256, half * 256 + 256)
-        xy_ref[rows, :] = product(tables, get(z_ref, rows))
+    for nz in range(8):
+        rows = slice(64 * nz, 64 * nz + 64)
+        xy_ref[rows, :] = product(table_ref[...], get(z_ref, rows))
     for ny in range(8):
         tiles = [get(z_ref, rows_of(nz, ny)) for nz in range(8)]
         even = [tiles[k] + tiles[7 - k] for k in range(4)]
@@ -421,20 +414,21 @@
     ]
     for copy in small + parts:
         copy.start()
-    for copy in small:
+    for copy in small + parts:
         copy.wait()
     order = held_order[...]
     choose = selection(order)
-    coeff = jnp.zeros((8, PLANE), F32)
-    for piece in pieces(jnp.broadcast_to(held_kappa[...], (8, PLANE))):
-        coeff = coeff + lax.dot_general(piece, choose, (((1,), (1,)), ((), ())), preferred_element_type=F32)
+    choose = jnp.concatenate([choose] * 3, axis=1)
+    coeff = lax.dot_general(
+        jnp.concatenate(pieces(jnp.broadcast_to(held_kappa[...], (8, PLANE))), axis=1),
+        choose,
+        (((1,), (1,)), ((), ())),
+        preferred_element_type=F32,
+    )
     own = jnp.concatenate([coeff[0:3], order.astype(F32), coeff[4:8]], axis=0)
     own_ref[...] = own
-    for k, copy in enumerate(parts):
-        copy.wait()
-        load = jnp.zeros((PLANE, 256), F32)
-        for piece in pieces(held[k]):
-            load = load + jnp.dot(choose, piece, preferred_element_type=F32)
+    for k in range(2):
+        load = jnp.dot(choose, jnp.concatenate(pieces(held[k]), axis=0), preferred_element_type=F32)
         put(load_ref, slice(256 * k, 256 * k + 256), load.T)
     sum_xy(load_ref)
     faces_out(load_ref, near_ref, far_ref)
@@ -595,8 +589,7 @@
     faces = below_above(face_in(near_in_ref), face_in(far_in_ref))
     tiles = [slice(8 * ny, 8 * ny + 8) for ny in range(8)]
     added = added_by(faces, kappas, columns_of_nodes())
-    small_tables = [table_ref[k, :, 0:64] for k in range(3)]
-    xy_ref[...] = product(small_tables, jnp.concatenate(added, axis=1))
+    xy_ref[...] = product(table_ref[...], jnp.concatenate(added, axis=1))
     along, at_face = [], []
     for k in range(2):
         along.append(local_along(own, weight_x, added[k]))
@@ -736,10 +729,12 @@
 
 
 def to_stored(choose, value):
-    total = jnp.zeros((choose.shape[0], value.shape[0]), F32)
-    for piece in pieces(value)[1:]:
-        total = total + lax.dot_general(choose, piece, (((1,), (1,)), ((), ())), preferred_element_type=F32)
-    return total
+    return lax.dot_general(
+        jnp.concatenate([choose] * 2, axis=1),
+        jnp.concatenate(pieces(value)[1:], axis=1),
+        (((1,), (1,)), ((), ())),
+        preferred_element_type=F32,
+    )
 
 
 def closing(
@@ -762,11 +757,9 @@
         put(sum_ref, rows, get(sum_ref, rows) + second[0] * face_in(ref))
     copies = [pltpu.make_async_copy(held.at[0], solution_ref, sems.at[0])]
     copies[0].start()
-    for part in range(2):
-        stored = slice(128 * part, 128 * part + 128)
-        held[1, stored, :] = to_stored(choose[stored], get(sum_ref, slice(0, 512)))
-        copies.append(pltpu.make_async_copy(held.at[1, stored], residual_ref.at[stored], sems.at[1 + part]))
-        copies[-1].start()
+    held[1] = to_stored(choose, get(sum_ref, slice(0, 512)))
+    copies.append(pltpu.make_async_copy(held.at[1], residual_ref, sems.at[1]))
+    copies[1].start()
     for copy in copies:
         copy.wait()
 
@@ -804,7 +797,7 @@
     nodes, face, face_row = (2, 512, 128), (2, 56, 128), (2, 64, 128)
     plane, grid, flat = (8, PLANE), (devices, PLANE), (512, PLANE)
     edge, stored, choice = (2, 128, 128), (PLANE, 512), ((PLANE, PLANE), jnp.bfloat16)
-    table = jnp.asarray(np.stack(STIFF_PARTS), jnp.bfloat16)
+    table = jnp.asarray(np.concatenate([STIFF_PARTS[k] for k in (0, 0, 1, 1, 0, 2)], 1), jnp.bfloat16)
     long = pl.CostEstimate(flops=10**11, bytes_accessed=2**28, transcendentals=0)
     payload_rows = (devices * 6, 128)
     load, far, near, own, payload = call(
@@ -840,7 +833,7 @@
     modes, scalars = call(second_coarse, [(24, PLANE), (8, 128)], [grid])(
         coeff, step, vert, applied, target, scale, first_modes
     )
-    found, left = call(closing, [stored, stored], [flat, nodes, edge, (2,) + stored], 3, hbm_out=(0, 1))(
+    found, left = call(closing, [stored, stored], [flat, nodes, edge, (2,) + stored], 2, hbm_out=(0, 1))(
         resid, scaled, image, scaled_change, change, next_far, next_near, modes, layers, scalars, choose
     )
     return found, left

time: 39.6 us -> 39 us (0.985)
  Pallas kernels: 13.5 us -> 12.8 us
  waiting for transfers between devices: 2.97 us -> 3.4 us
    all_to_all x2, waiting for transfers between devices: 2.96 us -> 3.39 us  [everyone(): lax.all_to_all(payload.reshape((devices,) + shape), AXES, 0, 0, tiled=True)]
  transfers between devices with their start and end apart: 8 -> 8, of which waited for: 2 -> 2; matrix products, arithmetic and copies ran while one was open for 0% -> 0% of each run, Pallas kernels for 18% -> 17%
where the time goes in v6:
time: 39 us; the launch traced here: 38.4 us
  starting transfers between devices  21.5 us (55%)
  Pallas kernels  12.8 us (33%)
  waiting for transfers between devices  3.4 us (9%)
  between operations  0.74 us (2%)
    ppermute x6, starting transfers between devices, swapped(): lax.ppermute(x, AXES, [(i, (i + (1 if (i % 2 == 0) != far else -1)) % siz...  16.1 us
    all_to_all x2, starting transfers between devices, everyone(): lax.all_to_all(payload.reshape((devices,) + shape), AXES, 0, 0, tiled=True)  5.36 us
    all_to_all x2, waiting for transfers between devices, everyone(): lax.all_to_all(payload.reshape((devices,) + shape), AXES, 0, 0, tiled=True)  3.39 us
    pallas_call x1, Pallas kernels, per_device(): call(opening, [nodes, face_row, face_row, plane, payload_rows], [(2, PLAN...  2.95 us
    pallas_call x1, Pallas kernels, per_device(): call(closing, [stored, stored], [flat, nodes, edge, (2,) + stored], 2, hb...  1.92 us
    pallas_call x1, Pallas kernels, per_device(): call(first_coarse, [grid] * 4 + [nodes], [edge])(gather, layers)  1.8 us
    pallas_call x1, Pallas kernels, per_device(): call(second_rough, [nodes] * 2 + [(48, PLANE), plane, (128, PLANE), (128,...  1.46 us
    pallas_call x1, Pallas kernels, per_device(): call(second_faces, [(128, PLANE), face, face, (devices * 7, 128)], [edge,...  1.35 us
  transfers between devices with their start and end apart: 8, of which 2 were waited for; matrix products, arithmetic and copies ran while one was open for 0% of the time, Pallas kernels for 17%

profile of v6, /device:TPU:0, one launch (start us, length us, event | category | flops | bytes accessed | tf_op | source)
XLA Modules:
  0.0 38.4 jit_solution(13190408879010398528)
XLA Ops:
  0.6 2.9 %shard_map.59 = (f32[2,512,128]{2,1,0:T(8,128)S(1)}, f32[2,64,128]{2,1,0:T(8,128)S(1)}, f32[2,64,128]{2,1,0:T(8,128)S(1)}, f32[8,256]{1,0:T(8,128)S(1)}, f32[192,128]{1,0:T(8,128)}) custom-call(f32[256,512]{1,0:T(8,128)} %forcing_ref.1, f32[1,256]{1,0:T(1,128)} %bitcast.7, s32[1,256]{1,0:T(1,128)} %order_ref.1), custom_call_target="tpu_custom_call" | custom-call | tf_op jit(solution)/shard_map/pallas_call | solution.py:803
  3.6 5.6 %collective-permute-start = (f32[2,64,128]{2,1,0:T(8,128)S(1)}, f32[2,64,128]{2,1,0:T(8,128)S(1)}, u32[]{:S(2)}, u32[]{:S(2)}) collective-permute-start(f32[2,64,128]{2,1,0:T(8,128)S(1)} %get-tuple-element.38), channel_id=1, source_target_pairs={{0,31},{1,2},{2,1},{3,4},{4,3},{5,6},{6,5},{7,8},{8,7},{9,10},{10,... | collective-permute-start | bytes 196616 | tf_op jit(solution)/shard_map/ppermute | solution.py:787
  9.1 0.0 collective-permute-start.1
  9.2 0.0 copy-start
  9.2 2.6 %all-to-all-start = ((f32[32,3,2,128]{3,2,1,0:T(2,128)}), f32[32,3,2,128]{3,2,1,0:T(2,128)S(1)}, u32[]{:S(2)}, u32[]{:S(2)}) async-start(f32[32,3,2,128]{3,2,1,0:T(2,128)} %bitcast.1), calls=%async_computation | async-start | bytes 196608 | tf_op jit(solution)/shard_map/all_to_all | solution.py:792
  11.8 0.0 collective-permute-done.far_in_ref
  11.8 0.0 collective-permute-done.1.near_in_ref
  11.8 0.0 copy-done
  11.8 1.1 %shard_map.60 = (f32[2,512,128]{2,1,0:T(8,128)S(1)}, f32[2,512,128]{2,1,0:T(8,128)S(1)}, f32[2,512,128]{2,1,0:T(8,128)S(1)}, f32[8,256]{1,0:T(8,128)S(1)}, f32[8...) custom-call(f32[2,512,128]{2,1,0:T(8,128)S(1)} %get-tuple-element.37, ...), custom_call_target="tpu_custom_call", output_to_operand_aliasing={{0}: (0, {})} | custom-call | flops 99999997952 | bytes 268435456 | tf_op jit(solution)/shard_map/pallas_call | solution.py:817
  12.9 5.3 %collective-permute-start.2 = (f32[2,64,128]{2,1,0:T(8,128)S(1)}, f32[2,64,128]{2,1,0:T(8,128)S(1)}, u32[]{:S(2)}, u32[]{:S(2)}) collective-permute-start(f32[2,64,128]{2,1,0:T(8,128)S(1)} %get-tuple-element.49), channel_id=1, source_target_pairs={{0,31},{1,2},{2,1},{3,4},{4,3},{5,6},{6,5},{7,8},{8,7},{9,10},{10,... | collective-permute-start | bytes 196616 | tf_op jit(solution)/shard_map/ppermute | solution.py:787
  18.1 0.0 collective-permute-start.3
  18.1 1.6 %all-to-all-done = f32[32,3,2,128]{3,2,1,0:T(2,128)S(1)} async-done(((f32[32,3,2,128]{3,2,1,0:T(2,128)}), f32[32,3,2,128]{3,2,1,0:T(2,128)S(1)}, u32[]{:S(2)}, u32[]{:S(2)}) %all-to-all-start) | async-done | bytes 98336 | tf_op jit(solution)/shard_map/all_to_all | solution.py:792
  19.7 1.8 %shard_map.62 = (f32[32,256]{1,0:T(8,128)S(1)}, f32[32,256]{1,0:T(8,128)S(1)}, f32[32,256]{1,0:T(8,128)S(1)}, f32[32,256]{1,0:T(8,128)S(1)}, f32[2,512,128]{2,1,0:T(8,128)S(1)}) custom-call(f32[192,128]{1,0:T(8,128)S(1)} %bitcast.6, f32[8,256]{1,0:T(8,128)S(1)} %get-tuple-element.45.layers_ref), custom_call_target="tpu_custom_call" | custom-call | tf_op jit(solution)/shard_map/pallas_call | solution.py:821
  21.5 1.5 %shard_map.63 = (f32[2,512,128]{2,1,0:T(8,128)S(1)}, f32[2,512,128]{2,1,0:T(8,128)S(1)}, f32[48,256]{1,0:T(8,128)S(1)}, f32[8,256]{1,0:T(8,128)S(1)}, f32[128,256]{1,0:T(8,128)S(1)}, /*index=5*/f32[128,256]{1,0:T(8,128)S(1)}) custom-call(f32[2,512,128]{2,1,0:T(8,128)S(1)} %get-tuple-element.43.image_ref.first_ref, ...), custom_call_target="tpu_custom_call", output_to_operand_aliasing={{0}: (1, {})} | custom-call | tf_op jit(solution)/shard_map/pallas_call | solution.py:822
  23.0 0.0 collective-permute-done.2.far_in_ref
  23.0 0.0 collective-permute-done.3.near_in_ref
  23.0 1.3 %shard_map.64 = (f32[128,256]{1,0:T(8,128)S(1)}, f32[2,56,128]{2,1,0:T(8,128)S(1)}, f32[2,56,128]{2,1,0:T(8,128)S(1)}, f32[224,128]{1,0:T(8,128)}) custom-call(f32[2,512,128]{2,1,0:T(8,128)S(1)} %get-tuple-element.43.image_ref.first_ref, f32[2,512,128]{2,1,0:T(8,128)S(1)} %get-tuple-element.47.scaled_change_ref.first_scaled_ref, ...), custom_call_target="tpu_custom_call" | custom-call | tf_op jit(solution)/shard_map/pallas_call | solution.py:825
  24.4 2.8 %all-to-all-start.1 = ((f32[32,7,1,128]{3,2,1,0:T(1,128)}), f32[32,7,1,128]{3,2,1,0:T(1,128)S(1)}, u32[]{:S(2)}, u32[]{:S(2)}) async-start(f32[32,7,1,128]{3,2,1,0:T(1,128)} %bitcast.3), calls=%async_computation.1 | async-start | bytes 229376 | tf_op jit(solution)/shard_map/all_to_all | solution.py:792
  27.1 5.3 %collective-permute-start.4 = (f32[2,56,128]{2,1,0:T(8,128)S(1)}, f32[2,56,128]{2,1,0:T(8,128)S(1)}, u32[]{:S(2)}, u32[]{:S(2)}) collective-permute-start(f32[2,56,128]{2,1,0:T(8,128)S(1)} %get-tuple-element.62), channel_id=1, source_target_pairs={{0,31},{1,2},{2,1},{3,4},{4,3},{5,6},{6,5},{7,8},{8,7},{9,10},{10,... | collective-permute-start | bytes 172040 | tf_op jit(solution)/shard_map/ppermute | solution.py:787
  32.4 0.0 collective-permute-start.5
  32.4 1.0 %shard_map.65 = (f32[2,512,128]{2,1,0:T(8,128)S(1)}, f32[2,512,128]{2,1,0:T(8,128)S(1)}, f32[2,512,128]{2,1,0:T(8,128)S(1)}, bf16[256,256]{1,0:T(8,128)(2,1)S(1)...) custom-call(f32[2,512,128]{2,1,0:T(8,128)S(1)} %get-tuple-element.43.i, ...), custom_call_target="tpu_custom_call", output_to_operand_aliasing={{0}: (0, {}), {1}: (1, {}), {2}: (2, {})} | custom-call | tf_op jit(solution)/shard_map/pallas_call | solution.py:830
  33.5 1.8 %all-to-all-done.1 = f32[32,7,1,128]{3,2,1,0:T(1,128)S(1)} async-done(((f32[32,7,1,128]{3,2,1,0:T(1,128)}), f32[32,7,1,128]{3,2,1,0:T(1,128)S(1)}, u32[]{:S(2)}, u32[]{:S(2)}) %all-to-all-start.1) | async-done | bytes 114720 | tf_op jit(solution)/shard_map/all_to_all | solution.py:792
  35.2 1.2 %shard_map.66 = (f32[24,256]{1,0:T(8,128)S(1)}, f32[8,128]{1,0:T(8,128)S(1)}) custom-call(f32[32,256]{1,0:T(8,128)S(1)} %get-tuple-element.57.coeff_ref, f32[224,128]{1,0:T(8,128)S(1)} %bitcast.5, f32[32,256]{1,0:T(8,128)S(1)} %get-tuple-element.58.vert_ref.first_ref, f32[32,256]{1,0:T(8,128)S(1)} %get-tuple-element.65.applied_ref, ...), custom_call_target="tpu_custom_call" | custom-call | tf_op jit(solution)/shard_map/pallas_call | solution.py:833
  36.5 0.0 collective-permute-done.4.far_ref
  36.5 0.0 collective-permute-done.5.near_ref
  36.5 1.9 %shard_map.67 = (f32[256,512]{1,0:T(8,128)}, f32[256,512]{1,0:T(8,128)}) custom-call(f32[2,512,128]{2,1,0:T(8,128)S(1)} %get-tuple-element.41.resid_ref, f32[2,512,128]{2,1,0:T(8,128)S(1)} %get-tuple-element.42.scaled_ref, f32[2,512,128]{2,1,0:T(8,128)S(1)} %get-tuple-element.59.image_ref, f32[2,512,128]{2,1,0:T(8,128)S(1)} %get-tuple-element.60.scaled_change_ref, ...), custom_call_target="tpu_custom_call" | custom-call | tf_op jit(solution)/shard_map/pallas_call | solution.py:836
  (1 shorter events, 0.0 us)
Async XLA Ops:
  3.6 8.2 %collective-permute-start = (f32[2,64,128]{2,1,0:T(8,128)S(1)}, f32[2,64,128]{2,1,0:T(8,128)S(1)}, u32[]{:S(2)}, u32[]{:S(2)}) collective-permute-start(f32[2,64,128]{2,1,0:T(8,128)S(1)} %get-tuple-element.38), channel_id=1, source_target_pairs={{0,31},{1,2},{2,1},{3,4},{4,3},{5,6},{6,5},{7,8},{8,7},{9,10},{10,... | collective-permute-start | bytes 196616 | tf_op jit(solution)/shard_map/ppermute | solution.py:787
  9.1 2.6 %collective-permute-start.1 = (f32[2,64,128]{2,1,0:T(8,128)S(1)}, f32[2,64,128]{2,1,0:T(8,128)S(1)}, u32[]{:S(2)}, u32[]{:S(2)}) collective-permute-start(f32[2,64,128]{2,1,0:T(8,128)S(1)} %get-tuple-element.39), channel_id=1, source_target_pairs={{0,1},{1,0},{2,3},{3,2},{4,5},{5,4},{6,7},{7,6},{8,9},{9,8},{10,11... | collective-permute-start | bytes 196616 | tf_op jit(solution)/shard_map/ppermute | solution.py:787
  9.2 2.6 %copy-start = (bf16[64,384]{1,0:T(8,128)(2,1)S(1)}, bf16[64,384]{1,0:T(8,128)(2,1)}, u32[]{:S(2)}) copy-start(bf16[64,384]{1,0:T(8,128)(2,1)} %constant.2.clone.table_ref) | copy-start | bytes 147460
  9.2 10.6 %all-to-all-start = ((f32[32,3,2,128]{3,2,1,0:T(2,128)}), f32[32,3,2,128]{3,2,1,0:T(2,128)S(1)}, u32[]{:S(2)}, u32[]{:S(2)}) async-start(f32[32,3,2,128]{3,2,1,0:T(2,128)} %bitcast.1), calls=%async_computation | async-start | bytes 196608 | tf_op jit(solution)/shard_map/all_to_all | solution.py:792
  12.9 10.1 %collective-permute-start.2 = (f32[2,64,128]{2,1,0:T(8,128)S(1)}, f32[2,64,128]{2,1,0:T(8,128)S(1)}, u32[]{:S(2)}, u32[]{:S(2)}) collective-permute-start(f32[2,64,128]{2,1,0:T(8,128)S(1)} %get-tuple-element.49), channel_id=1, source_target_pairs={{0,31},{1,2},{2,1},{3,4},{4,3},{5,6},{6,5},{7,8},{8,7},{9,10},{10,... | collective-permute-start | bytes 196616 | tf_op jit(solution)/shard_map/ppermute | solution.py:787
  18.1 4.9 %collective-permute-start.3 = (f32[2,64,128]{2,1,0:T(8,128)S(1)}, f32[2,64,128]{2,1,0:T(8,128)S(1)}, u32[]{:S(2)}, u32[]{:S(2)}) collective-permute-start(f32[2,64,128]{2,1,0:T(8,128)S(1)} %get-tuple-element.50), channel_id=1, source_target_pairs={{0,1},{1,0},{2,3},{3,2},{4,5},{5,4},{6,7},{7,6},{8,9},{9,8},{10,11... | collective-permute-start | bytes 196616 | tf_op jit(solution)/shard_map/ppermute | solution.py:787
  24.4 10.9 %all-to-all-start.1 = ((f32[32,7,1,128]{3,2,1,0:T(1,128)}), f32[32,7,1,128]{3,2,1,0:T(1,128)S(1)}, u32[]{:S(2)}, u32[]{:S(2)}) async-start(f32[32,7,1,128]{3,2,1,0:T(1,128)} %bitcast.3), calls=%async_computation.1 | async-start | bytes 229376 | tf_op jit(solution)/shard_map/all_to_all | solution.py:792
  27.1 9.3 %collective-permute-start.4 = (f32[2,56,128]{2,1,0:T(8,128)S(1)}, f32[2,56,128]{2,1,0:T(8,128)S(1)}, u32[]{:S(2)}, u32[]{:S(2)}) collective-permute-start(f32[2,56,128]{2,1,0:T(8,128)S(1)} %get-tuple-element.62), channel_id=1, source_target_pairs={{0,31},{1,2},{2,1},{3,4},{4,3},{5,6},{6,5},{7,8},{8,7},{9,10},{10,... | collective-permute-start | bytes 172040 | tf_op jit(solution)/shard_map/ppermute | solution.py:787
  32.4 4.0 %collective-permute-start.5 = (f32[2,56,128]{2,1,0:T(8,128)S(1)}, f32[2,56,128]{2,1,0:T(8,128)S(1)}, u32[]{:S(2)}, u32[]{:S(2)}) collective-permute-start(f32[2,56,128]{2,1,0:T(8,128)S(1)} %get-tuple-element.63), channel_id=1, source_target_pairs={{0,1},{1,0},{2,3},{3,2},{4,5},{5,4},{6,7},{7,6},{8,9},{9,8},{10,11... | collective-permute-start | bytes 172040 | tf_op jit(solution)/shard_map/ppermute | solution.py:787

commit v7 on v6

--- a/solution.py
+++ b/solution.py
@@ -410,7 +410,8 @@
         pltpu.make_async_copy(kappa_ref, held_kappa, sems.at[1]),
     ]
     parts = [
-        pltpu.make_async_copy(forcing_ref.at[:, pl.ds(256 * k, 256)], held.at[k], sems.at[2 + k]) for k in range(2)
+        pltpu.make_async_copy(forcing_ref.at[pl.ds(64 * k, 64)], held.at[pl.ds(64 * k, 64)], sems.at[2 + k])
+        for k in range(4)
     ]
     for copy in small + parts:
         copy.start()
@@ -428,7 +429,7 @@
     own = jnp.concatenate([coeff[0:3], order.astype(F32), coeff[4:8]], axis=0)
     own_ref[...] = own
     for k in range(2):
-        load = jnp.dot(choose, jnp.concatenate(pieces(held[k]), axis=0), preferred_element_type=F32)
+        load = jnp.dot(choose, jnp.concatenate(pieces(held[:, 256 * k : 256 * k + 256]), axis=0), preferred_element_type=F32)
         put(load_ref, slice(256 * k, 256 * k + 256), load.T)
     sum_xy(load_ref)
     faces_out(load_ref, near_ref, far_ref)
@@ -438,7 +439,7 @@
 
     @pl.when(starts_early())
     def _():
-        write_payload(load_ref, own_ref, payload_ref, held_payload, sems.at[4])
+        write_payload(load_ref, own_ref, payload_ref, held_payload, sems.at[6])
 
 
 def starts_early():
@@ -574,6 +575,18 @@
     sums_ref[...] = jnp.concatenate([total * inv_ends for total in sums], axis=0)
     for k, rows in enumerate((slice(0, 64), slice(448, 512))):
         outer_ref[64 * k : 64 * k + 64, :] = get(whole_ref, rows)
+
+
+def first_rest(
+    coarse_ref, image_ref, layers_ref, table_ref, resid_ref, scaled_ref,
+    vert_ref, target_ref, scale_ref, coeff_ref, scaled_change_ref, change_ref, sums_ref, planes_ref, column_ref, outer_ref,
+    smooth_ref, edge_ref, xy_ref, whole_ref,
+):
+    first_coarse(coarse_ref, layers_ref, vert_ref, target_ref, scale_ref, coeff_ref, smooth_ref, edge_ref)
+    second_rough(
+        image_ref, smooth_ref, layers_ref, table_ref, resid_ref, scaled_ref,
+        scaled_change_ref, change_ref, sums_ref, planes_ref, column_ref, outer_ref, xy_ref, whole_ref,
+    )
 
 
 def second_faces(
@@ -803,8 +816,8 @@
     load, far, near, own, payload = call(
         opening,
         [nodes, face_row, face_row, plane, payload_rows],
-        [(2, PLANE, 256), (1, PLANE), ((1, PLANE), jnp.int32), payload_rows],
-        5,
+        [stored, (1, PLANE), ((1, PLANE), jnp.int32), payload_rows],
+        7,
         hbm_in=(0, 1, 2),
         hbm_out=(4,),
         inputs=3,
@@ -818,10 +831,11 @@
         first_faces, [nodes, nodes, nodes, plane, plane, face_row, face_row], [flat], cost=long, in_place={0: 0}
     )(load, far, near, own, table)
     far, near = swapped(far, True), swapped(near, False)
-    vert, target, scale, coeff, smooth = call(first_coarse, [grid] * 4 + [nodes], [edge])(gather, layers)
-    scaled_change, change, sums, planes, column_planes, outer = call(
-        second_rough, [nodes] * 2 + [(48, PLANE), plane, (128, PLANE), (128, PLANE)], [flat, nodes], in_place={1: 0}
-    )(image, smooth, layers, table, resid, scaled)
+    vert, target, scale, coeff, scaled_change, change, sums, planes, column_planes, outer = call(
+        first_rest,
+        [grid] * 4 + [nodes] * 2 + [(48, PLANE), plane, (128, PLANE), (128, PLANE)],
+        [nodes, edge, flat, nodes],
+    )(gather, image, layers, table, resid, scaled)
     added, next_far, next_near, payload = call(
         second_faces, [(128, PLANE), face, face, (devices * 7, 128)], [edge, (64, 2 * PLANE)]
     )(image, scaled_change, change, outer, far, near, layers, table, scaled, lower, sums, planes, column_planes)

time: 39 us -> 39.1 us (level)
    pallas_call x3 -> x2, Pallas kernels: 6.21 us -> 6.02 us  [the longest x1 3.03 us: per_device(): call(opening, [nodes, face_row, face_row, plane, payload_rows], [stored,...]
  transfers between devices with their start and end apart: 8 -> 8, of which waited for: 2 -> 2; matrix products, arithmetic and copies ran while one was open for 0% -> 0% of each run, Pallas kernels for 17% -> 16%
where the time goes in v7:
time: 39.1 us; the launch traced here: 38.5 us
  starting transfers between devices  21.7 us (55%)
  Pallas kernels  12.6 us (32%)
  waiting for transfers between devices  3.39 us (9%)
  between operations  0.74 us (2%)
    ppermute x6, starting transfers between devices, swapped(): lax.ppermute(x, AXES, [(i, (i + (1 if (i % 2 == 0) != far else -1)) % siz...  16.1 us
    all_to_all x2, starting transfers between devices, everyone(): lax.all_to_all(payload.reshape((devices,) + shape), AXES, 0, 0, tiled=True)  5.63 us
    all_to_all x2, waiting for transfers between devices, everyone(): lax.all_to_all(payload.reshape((devices,) + shape), AXES, 0, 0, tiled=True)  3.38 us
    pallas_call x1, Pallas kernels, per_device(): call(opening, [nodes, face_row, face_row, plane, payload_rows], [stored,...  3.03 us
    pallas_call x1, Pallas kernels, per_device(): call(first_rest, [grid] * 4 + [nodes] * 2 + [(48, PLANE), plane, (128, PL...  3 us
    pallas_call x1, Pallas kernels, per_device(): call(closing, [stored, stored], [flat, nodes, edge, (2,) + stored], 2, hb...  1.92 us
    pallas_call x1, Pallas kernels, per_device(): call(second_faces, [(128, PLANE), face, face, (devices * 7, 128)], [edge,...  1.37 us
    pallas_call x1, Pallas kernels, per_device(): call(second_coarse, [(24, PLANE), (8, 128)], [grid])  1.2 us
  transfers between devices with their start and end apart: 8, of which 2 were waited for; matrix products, arithmetic and copies ran while one was open for 0% of the time, Pallas kernels for 16%

profile of v7, /device:TPU:0, one launch (start us, length us, event | category | flops | bytes accessed | tf_op | source)
XLA Modules:
  0.0 38.5 jit_solution(1069353908525155736)
XLA Ops:
  0.6 3.0 %shard_map.59 = (f32[2,512,128]{2,1,0:T(8,128)S(1)}, f32[2,64,128]{2,1,0:T(8,128)S(1)}, f32[2,64,128]{2,1,0:T(8,128)S(1)}, f32[8,256]{1,0:T(8,128)S(1)}, f32[192,128]{1,0:T(8,128)}) custom-call(f32[256,512]{1,0:T(8,128)} %forcing_ref.1, f32[1,256]{1,0:T(1,128)} %bitcast.7, s32[1,256]{1,0:T(1,128)} %order_ref.1), custom_call_target="tpu_custom_call" | custom-call | tf_op jit(solution)/shard_map/pallas_call | solution.py:816
  3.7 5.6 %collective-permute-start = (f32[2,64,128]{2,1,0:T(8,128)S(1)}, f32[2,64,128]{2,1,0:T(8,128)S(1)}, u32[]{:S(2)}, u32[]{:S(2)}) collective-permute-start(f32[2,64,128]{2,1,0:T(8,128)S(1)} %get-tuple-element.37), channel_id=1, source_target_pairs={{0,31},{1,2},{2,1},{3,4},{4,3},{5,6},{6,5},{7,8},{8,7},{9,10},{10,... | collective-permute-start | bytes 196616 | tf_op jit(solution)/shard_map/ppermute | solution.py:800
  9.2 0.0 collective-permute-start.1
  9.2 0.0 copy-start
  9.3 2.6 %all-to-all-start = ((f32[32,3,2,128]{3,2,1,0:T(2,128)}), f32[32,3,2,128]{3,2,1,0:T(2,128)S(1)}, u32[]{:S(2)}, u32[]{:S(2)}) async-start(f32[32,3,2,128]{3,2,1,0:T(2,128)} %bitcast.1), calls=%async_computation | async-start | bytes 196608 | tf_op jit(solution)/shard_map/all_to_all | solution.py:805
  11.9 0.0 collective-permute-done.far_in_ref
  11.9 0.0 collective-permute-done.1.near_in_ref
  11.9 0.0 copy-done
  11.9 1.1 %shard_map.60 = (f32[2,512,128]{2,1,0:T(8,128)S(1)}, f32[2,512,128]{2,1,0:T(8,128)S(1)}, f32[2,512,128]{2,1,0:T(8,128)S(1)}, f32[8,256]{1,0:T(8,128)S(1)}, f32[8...) custom-call(f32[2,512,128]{2,1,0:T(8,128)S(1)} %get-tuple-element.36, ...), custom_call_target="tpu_custom_call", output_to_operand_aliasing={{0}: (0, {})} | custom-call | flops 99999997952 | bytes 268435456 | tf_op jit(solution)/shard_map/pallas_call | solution.py:830
  13.0 5.3 %collective-permute-start.2 = (f32[2,64,128]{2,1,0:T(8,128)S(1)}, f32[2,64,128]{2,1,0:T(8,128)S(1)}, u32[]{:S(2)}, u32[]{:S(2)}) collective-permute-start(f32[2,64,128]{2,1,0:T(8,128)S(1)} %get-tuple-element.47), channel_id=1, source_target_pairs={{0,31},{1,2},{2,1},{3,4},{4,3},{5,6},{6,5},{7,8},{8,7},{9,10},{10,... | collective-permute-start | bytes 196616 | tf_op jit(solution)/shard_map/ppermute | solution.py:800
  18.2 0.0 collective-permute-start.3
  18.2 1.6 %all-to-all-done = f32[32,3,2,128]{3,2,1,0:T(2,128)S(1)} async-done(((f32[32,3,2,128]{3,2,1,0:T(2,128)}), f32[32,3,2,128]{3,2,1,0:T(2,128)S(1)}, u32[]{:S(2)}, u32[]{:S(2)}) %all-to-all-start) | async-done | bytes 98336 | tf_op jit(solution)/shard_map/all_to_all | solution.py:805
  19.8 3.0 %shard_map.62 = (f32[32,256]{1,0:T(8,128)S(1)}, f32[32,256]{1,0:T(8,128)S(1)}, f32[32,256]{1,0:T(8,128)S(1)}, f32[32,256]{1,0:T(8,128)S(1)}, f32[2,512,128]{2,1,...) custom-call(f32[192,128]{1,0:T(8,128)S(1)} %bitcast.6, ...), custom_call_target="tpu_custom_call" | custom-call | tf_op jit(solution)/shard_map/pallas_call | solution.py:834
  22.8 0.0 collective-permute-done.2.far_in_ref
  22.8 0.0 collective-permute-done.3.near_in_ref
  22.8 1.4 %shard_map.63 = (f32[128,256]{1,0:T(8,128)S(1)}, f32[2,56,128]{2,1,0:T(8,128)}, f32[2,56,128]{2,1,0:T(8,128)S(1)}, f32[224,128]{1,0:T(8,128)}) custom-call(f32[2,512,128]{2,1,0:T(8,128)S(1)} %get-tuple-element.42.image_ref.first_ref, f32[2,512,128]{2,1,0:T(8,128)S(1)} %get-tuple-element.45.scaled_change_ref.first_scaled_ref, ...), custom_call_target="tpu_custom_call" | custom-call | tf_op jit(solution)/shard_map/pallas_call | solution.py:839
  24.2 3.0 %all-to-all-start.1 = ((f32[32,7,1,128]{3,2,1,0:T(1,128)}), f32[32,7,1,128]{3,2,1,0:T(1,128)S(1)}, u32[]{:S(2)}, u32[]{:S(2)}) async-start(f32[32,7,1,128]{3,2,1,0:T(1,128)} %bitcast.3), calls=%async_computation.1 | async-start | bytes 229376 | tf_op jit(solution)/shard_map/all_to_all | solution.py:805
  27.2 5.3 %collective-permute-start.4 = (f32[2,56,128]{2,1,0:T(8,128)}, f32[2,56,128]{2,1,0:T(8,128)S(1)}, u32[]{:S(2)}, u32[]{:S(2)}) collective-permute-start(f32[2,56,128]{2,1,0:T(8,128)} %get-tuple-element.60), channel_id=1, source_target_pairs={{0,31},{1,2},{2,1},{3,4},{4,3},{5,6},{6,5},{7,8},{8,7},{9,10},{10,... | collective-permute-start | bytes 172040 | tf_op jit(solution)/shard_map/ppermute | solution.py:800
  32.5 0.0 collective-permute-start.5
  32.5 1.0 %shard_map.64 = (f32[2,512,128]{2,1,0:T(8,128)S(1)}, f32[2,512,128]{2,1,0:T(8,128)S(1)}, f32[2,512,128]{2,1,0:T(8,128)S(1)}, bf16[256,256]{1,0:T(8,128)(2,1)S(1)...) custom-call(f32[2,512,128]{2,1,0:T(8,128)S(1)} %get-tuple-element.42.i, ...), custom_call_target="tpu_custom_call", output_to_operand_aliasing={{0}: (0, {}), {1}: (1, {}), {2}: (2, {})} | custom-call | tf_op jit(solution)/shard_map/pallas_call | solution.py:844
  33.6 1.8 %all-to-all-done.1 = f32[32,7,1,128]{3,2,1,0:T(1,128)S(1)} async-done(((f32[32,7,1,128]{3,2,1,0:T(1,128)}), f32[32,7,1,128]{3,2,1,0:T(1,128)S(1)}, u32[]{:S(2)}, u32[]{:S(2)}) %all-to-all-start.1) | async-done | bytes 114720 | tf_op jit(solution)/shard_map/all_to_all | solution.py:805
  35.4 1.2 %shard_map.65 = (f32[24,256]{1,0:T(8,128)S(1)}, f32[8,128]{1,0:T(8,128)S(1)}) custom-call(f32[32,256]{1,0:T(8,128)S(1)} %get-tuple-element.55.coeff_ref, f32[224,128]{1,0:T(8,128)S(1)} %bitcast.5, f32[32,256]{1,0:T(8,128)S(1)} %get-tuple-element.56.vert_ref.first_ref, f32[32,256]{1,0:T(8,128)S(1)} %get-tuple-element.63.applied_ref, ...), custom_call_target="tpu_custom_call" | custom-call | tf_op jit(solution)/shard_map/pallas_call | solution.py:847
  36.6 0.0 collective-permute-done.4.far_ref
  36.6 0.0 collective-permute-done.5.near_ref
  36.6 1.9 %shard_map.66 = (f32[256,512]{1,0:T(8,128)}, f32[256,512]{1,0:T(8,128)}) custom-call(f32[2,512,128]{2,1,0:T(8,128)S(1)} %get-tuple-element.40.resid_ref, f32[2,512,128]{2,1,0:T(8,128)S(1)} %get-tuple-element.41.scaled_ref, f32[2,512,128]{2,1,0:T(8,128)S(1)} %get-tuple-element.57.image_ref, f32[2,512,128]{2,1,0:T(8,128)S(1)} %get-tuple-element.58.scaled_change_ref, ...), custom_call_target="tpu_custom_call" | custom-call | tf_op jit(solution)/shard_map/pallas_call | solution.py:850
  (1 shorter events, 0.0 us)
Async XLA Ops:
  3.7 8.2 %collective-permute-start = (f32[2,64,128]{2,1,0:T(8,128)S(1)}, f32[2,64,128]{2,1,0:T(8,128)S(1)}, u32[]{:S(2)}, u32[]{:S(2)}) collective-permute-start(f32[2,64,128]{2,1,0:T(8,128)S(1)} %get-tuple-element.37), channel_id=1, source_target_pairs={{0,31},{1,2},{2,1},{3,4},{4,3},{5,6},{6,5},{7,8},{8,7},{9,10},{10,... | collective-permute-start | bytes 196616 | tf_op jit(solution)/shard_map/ppermute | solution.py:800
  9.2 2.6 %collective-permute-start.1 = (f32[2,64,128]{2,1,0:T(8,128)S(1)}, f32[2,64,128]{2,1,0:T(8,128)S(1)}, u32[]{:S(2)}, u32[]{:S(2)}) collective-permute-start(f32[2,64,128]{2,1,0:T(8,128)S(1)} %get-tuple-element.38), channel_id=1, source_target_pairs={{0,1},{1,0},{2,3},{3,2},{4,5},{5,4},{6,7},{7,6},{8,9},{9,8},{10,11... | collective-permute-start | bytes 196616 | tf_op jit(solution)/shard_map/ppermute | solution.py:800
  9.2 2.6 %copy-start = (bf16[64,384]{1,0:T(8,128)(2,1)S(1)}, bf16[64,384]{1,0:T(8,128)(2,1)}, u32[]{:S(2)}) copy-start(bf16[64,384]{1,0:T(8,128)(2,1)} %constant.2.clone.table_ref) | copy-start | bytes 147460
  9.3 10.5 %all-to-all-start = ((f32[32,3,2,128]{3,2,1,0:T(2,128)}), f32[32,3,2,128]{3,2,1,0:T(2,128)S(1)}, u32[]{:S(2)}, u32[]{:S(2)}) async-start(f32[32,3,2,128]{3,2,1,0:T(2,128)} %bitcast.1), calls=%async_computation | async-start | bytes 196608 | tf_op jit(solution)/shard_map/all_to_all | solution.py:805
  13.0 9.9 %collective-permute-start.2 = (f32[2,64,128]{2,1,0:T(8,128)S(1)}, f32[2,64,128]{2,1,0:T(8,128)S(1)}, u32[]{:S(2)}, u32[]{:S(2)}) collective-permute-start(f32[2,64,128]{2,1,0:T(8,128)S(1)} %get-tuple-element.47), channel_id=1, source_target_pairs={{0,31},{1,2},{2,1},{3,4},{4,3},{5,6},{6,5},{7,8},{8,7},{9,10},{10,... | collective-permute-start | bytes 196616 | tf_op jit(solution)/shard_map/ppermute | solution.py:800
  18.2 4.6 %collective-permute-start.3 = (f32[2,64,128]{2,1,0:T(8,128)S(1)}, f32[2,64,128]{2,1,0:T(8,128)S(1)}, u32[]{:S(2)}, u32[]{:S(2)}) collective-permute-start(f32[2,64,128]{2,1,0:T(8,128)S(1)} %get-tuple-element.48), channel_id=1, source_target_pairs={{0,1},{1,0},{2,3},{3,2},{4,5},{5,4},{6,7},{7,6},{8,9},{9,8},{10,11... | collective-permute-start | bytes 196616 | tf_op jit(solution)/shard_map/ppermute | solution.py:800
  24.2 11.2 %all-to-all-start.1 = ((f32[32,7,1,128]{3,2,1,0:T(1,128)}), f32[32,7,1,128]{3,2,1,0:T(1,128)S(1)}, u32[]{:S(2)}, u32[]{:S(2)}) async-start(f32[32,7,1,128]{3,2,1,0:T(1,128)} %bitcast.3), calls=%async_computation.1 | async-start | bytes 229376 | tf_op jit(solution)/shard_map/all_to_all | solution.py:805
  27.2 9.3 %collective-permute-start.4 = (f32[2,56,128]{2,1,0:T(8,128)}, f32[2,56,128]{2,1,0:T(8,128)S(1)}, u32[]{:S(2)}, u32[]{:S(2)}) collective-permute-start(f32[2,56,128]{2,1,0:T(8,128)} %get-tuple-element.60), channel_id=1, source_target_pairs={{0,31},{1,2},{2,1},{3,4},{4,3},{5,6},{6,5},{7,8},{8,7},{9,10},{10,... | collective-permute-start | bytes 172040 | tf_op jit(solution)/shard_map/ppermute | solution.py:800
  32.5 4.0 %collective-permute-start.5 = (f32[2,56,128]{2,1,0:T(8,128)S(1)}, f32[2,56,128]{2,1,0:T(8,128)S(1)}, u32[]{:S(2)}, u32[]{:S(2)}) collective-permute-start(f32[2,56,128]{2,1,0:T(8,128)S(1)} %get-tuple-element.61), channel_id=1, source_target_pairs={{0,1},{1,0},{2,3},{3,2},{4,5},{5,4},{6,7},{7,6},{8,9},{9,8},{10,11... | collective-permute-start | bytes 172040 | tf_op jit(solution)/shard_map/ppermute | solution.py:800
